TPU v7x, 32 devices: a whole 2x2x4 slice. The times are simulated.
32 devices in a mesh: groups: 1, local: 32 (over z, y, x, core).
Axes of the slice: x: 2, y: 2, z: 4, core: 2. Of those that a mesh axis runs over, the one named last changes fastest.
Arguments:
- tokens: bfloat16 [2048, 2048], P(('groups', 'local')), may hold values from -6 to 6
- expert_ids: int32 [2048, 2], P(('groups', 'local')), may hold values from 0 to 3, all different within a row; in each aligned block of 64 rows (0 to 63, 64 to 127, ...) at most 48 rows name the same one
- gate_weights: float32 [2048, 2], P(('groups', 'local')), may hold values from 0.2 to 1
- norm_gain: float32 [2048], replicated, may hold values from 0.25 to 1.75
- norm_bias: float32 [2048], replicated, may hold values from -3 to 3
- w_in: bfloat16 [32, 2048, 1024], P('local'), may hold values from -0.125 to 0.125
- b_in: float32 [32, 1024], P('local'), may hold values from -4 to 4
- w_out: bfloat16 [32, 1024, 2048], P('local'), may hold values from -0.0625 to 0.0625
- b_out: float32 [4, 2048], replicated, may hold values from -3 to 3
Outputs:
- mixed_out: bfloat16 [2048, 2048], P(('groups', 'local'))
Inputs may be any that keep to these rules, and one draw needn't show every extreme that they name: `expert_ids`: among the 64 tokens of one device, no expert is named by more than 48 pairs, a bound that some block reaches; a token's 2 experts differ.
All inputs are finite; a program needn't handle non-finite values.
Results may differ from a plain program's by a relative error of at most 0.008.
Values may be sent and summed in bfloat16 or wider, within the bound.
No kernel may reach another device: no remote copies, remote signals or barrier semaphores. Data moves between devices by JAX's collectives and lax.ppermute only.
A program may use at most 128 MiB of HBM per device.

v0:
```python
import jax
import jax.numpy as jnp
from jax import lax
from jax.sharding import PartitionSpec as P


def layer_norm(values, gain, bias):
    floats = values.astype(jnp.float32)
    row_mean = jnp.mean(floats, axis=-1, keepdims=True)
    centered = floats - row_mean
    row_var = jnp.mean(centered * centered, axis=-1, keepdims=True)
    return centered * lax.rsqrt(row_var + 1e-05) * gain + bias


def expert_block(row_block, w_in, b_in, w_out):
    hidden = jnp.einsum("ncd,dh->nch", row_block, w_in[0], preferred_element_type=jnp.float32)
    hidden = jnp.maximum(hidden + b_in[0][None, None, :], 0.0).astype(jnp.bfloat16)
    partial_value = jnp.einsum("nch,hd->ncd", hidden, w_out[0], preferred_element_type=jnp.float32)
    return partial_value.astype(jnp.bfloat16)


def local(tokens, expert_ids, gate_weights, norm_gain, norm_bias, w_in, b_in, w_out, b_out):
    tok_dev, model_width = tokens.shape
    top_count = expert_ids.shape[1]
    devices = lax.axis_size("local")
    experts = b_out.shape[0]
    shared = devices // experts
    slot_cap = min(
        tok_dev, shared * max(1, (3 * tok_dev * top_count // (2 * experts) + shared - 1) // shared)
    )
    sent_rows = layer_norm(tokens, norm_gain, norm_bias).astype(jnp.bfloat16)
    flat_ids = expert_ids.reshape(-1)
    onehot = (flat_ids[:, None] == jnp.arange(experts, dtype=jnp.int32)[None, :]).astype(jnp.int32)
    slot_rank = jnp.sum(jnp.cumsum(onehot, axis=0) * onehot, axis=1) - 1
    slot_rows = flat_ids * slot_cap + slot_rank
    blocks = jnp.zeros((experts * slot_cap, model_width), jnp.bfloat16)
    blocks = blocks.at[slot_rows].set(jnp.repeat(sent_rows, top_count, axis=0))
    outgoing = blocks.reshape(experts, 1, slot_cap, model_width)
    outgoing = jnp.broadcast_to(outgoing, (experts, shared, slot_cap, model_width)).reshape(
        devices, slot_cap, model_width
    )
    received = lax.all_to_all(outgoing, "local", split_axis=0, concat_axis=0, tiled=True)
    partial_value = expert_block(received, w_in, b_in, w_out)
    returned = lax.all_to_all(partial_value, "local", split_axis=0, concat_axis=0, tiled=True)
    summed = jnp.sum(
        returned.reshape(experts, shared, slot_cap, model_width).astype(jnp.float32), axis=1
    )
    summed = (summed + b_out[:, None, :]).reshape(experts * slot_cap, model_width)
    picked = summed[slot_rows].reshape(tok_dev, top_count, model_width)
    mixed_out = tokens.astype(jnp.float32) + jnp.sum(gate_weights[:, :, None] * picked, axis=1)
    return mixed_out.astype(jnp.bfloat16)


def solution(mesh):
    in_specs = (
        P(("groups", "local"), None),
        P(("groups", "local"), None),
        P(("groups", "local"), None),
        P(),
        P(),
        P("local", None, None),
        P("local", None),
        P("local", None, None),
        P(),
    )
    out_specs = P(("groups", "local"), None)
    return jax.shard_map(local, mesh=mesh, in_specs=in_specs, out_specs=out_specs, check_vma=False)
```

profile of v0, /device:TPU:0, one launch (start us, length us, event | category | flops | bytes accessed | tf_op | source)
XLA Modules:
  0.0 322.1 jit_solution(17872554592413547629)
XLA Ops:
  0.0 0.8 copy.15
  0.8 0.7 broadcast_multiply_fusion
  1.4 0.1 eq.15
  1.6 0.1 fusion.14
  1.7 0.2 reduce_window_sum.11
  1.9 0.2 select_reduce_fusion
  2.0 0.1 copy.14
  2.1 0.1 mul.49
  2.3 1.1 convert_reduce_fusion.1
  3.4 1.2 fusion.7
  4.6 1.1 fusion.10
  5.7 0.3 broadcast_in_dim.9
  6.1 0.2 reshape.86
  6.3 1.6 scatter_custom_fusion
  7.9 0.8 broadcast_in_dim.11
  8.7 0.0 copy-start.3
  8.7 145.7 %all_to_all.10 = bf16[32,48,2048]{2,1,0:T(8,128)(2,1)S(1)} all-to-all(bf16[32,48,2048]{2,1,0:T(8,128)(2,1)S(1)} %bitcast.23), channel_id=1, replica_groups=mesh['groups'=1,'local'=32] {'local'}, dimensions={0} | all-to-all | bytes 12582912 | tf_op jit(solution)/shard_map/all_to_all | solution.py:42
  154.4 6.9 %fusion.1 = f32[32,48,1024]{2,1,0:T(8,128)S(1)} fusion(bf16[32,48,2048]{2,1,0:T(8,128)(2,1)S(1)} %all_to_all.10, bf16[1,2048,1024]{2,1,0:T(8,128)(2,1)S(1)} %copy-done.3), kind=kOutput, calls=%fused_computation.6 | convolution fusion | flops 6442450944 | bytes 16777216 | tf_op jit(solution)/shard_map/ncd,dh->nch/dot_general | solution.py:16
  161.3 0.0 copy-done.4
  161.3 0.0 copy-done.5
  161.4 8.5 %convolution_convert_fusion = bf16[32,48,2048]{2,1,0:T(8,128)(2,1)} fusion(bf16[1,1024,2048]{2,1,0:T(8,128)(2,1)S(1)} %copy-done.4, f32[32,48,1024]{2,1,0:T(8,128)S(1)} %fusion.1, f32[1024]{0:T(1024)S(1)} %bitcast.25), kind=kOutput, calls=%fused_computation.4 | convolution fusion | flops 6450315264 | bytes 16781312 | tf_op jit(solution)/shard_map/nch,hd->ncd/dot_general | solution.py:18
  169.9 4.0 %all-to-all-start.1 = ((bf16[32,48,2048]{2,1,0:T(8,128)(2,1)}), bf16[32,48,2048]{2,1,0:T(8,128)(2,1)}, u32[]{:S(2)}, u32[]{:S(2)}) async-start(bf16[32,48,2048]{2,1,0:T(8,128)(2,1)} %convolution_convert_fusion), calls=%async_computation.1 | async-start | bytes 12582912 | tf_op jit(solution)/shard_map/all_to_all | solution.py:44
  173.9 0.0 copy-start.1
  174.0 0.1 copy.13
  174.1 139.8 %all-to-all-done.1 = bf16[32,48,2048]{2,1,0:T(8,128)(2,1)} async-done(((bf16[32,48,2048]{2,1,0:T(8,128)(2,1)}), bf16[32,48,2048]{2,1,0:T(8,128)(2,1)}, u32[]{:S(2)}, u32[]{:S(2)}) %all-to-all-start.1) | async-done | bytes 6291488 | tf_op jit(solution)/shard_map/all_to_all | solution.py:44
  313.8 4.2 %convert_reduce_fusion = f32[4,48,2048]{2,1,0:T(8,128)S(1)} fusion(bf16[32,48,2048]{2,1,0:T(8,128)(2,1)} %all-to-all-done.1), kind=kLoop, calls=%fused_computation.2 | loop fusion | flops 5898240 | bytes 7864320 | tf_op jit(solution)/shard_map/reduce_sum | solution.py:45
  318.0 0.2 broadcast_add_fusion
  318.2 0.0 copy-start
  318.2 1.0 gather_fusion
  319.2 0.6 reshape.72
  319.8 1.5 multiply_reduce_fusion
  321.3 0.8 fusion.11
  (11 shorter events, 0.0 us)
Async XLA Ops:
  8.7 145.7 %copy-start.3 = (bf16[1,2048,1024]{2,1,0:T(8,128)(2,1)S(1)}, bf16[1,2048,1024]{2,1,0:T(8,128)(2,1)}, u32[]{:S(2)}) copy-start(bf16[1,2048,1024]{2,1,0:T(8,128)(2,1)} %param.14) | copy-start | bytes 12582916
  154.4 6.9 %copy-start.4 = (bf16[1,1024,2048]{2,1,0:T(8,128)(2,1)S(1)}, bf16[1,1024,2048]{2,1,0:T(8,128)(2,1)}, u32[]{:S(2)}) copy-start(bf16[1,1024,2048]{2,1,0:T(8,128)(2,1)} %param.16) | copy-start | bytes 12582916
  154.4 6.9 %copy-start.5 = (f32[1,1024]{1,0:T(1,128)S(1)}, f32[1,1024]{1,0:T(1,128)}, u32[]{:S(2)}) copy-start(f32[1,1024]{1,0:T(1,128)} %param.15) | copy-start | bytes 12292
  169.9 4.1 %copy-start.2 = (f32[64,2]{0,1:T(2,128)S(1)}, f32[64,2]{0,1:T(2,128)}, u32[]{:S(2)}) copy-start(f32[64,2]{0,1:T(2,128)} %param.11) | copy-start | bytes 1540
  169.9 144.0 %all-to-all-start.1 = ((bf16[32,48,2048]{2,1,0:T(8,128)(2,1)}), bf16[32,48,2048]{2,1,0:T(8,128)(2,1)}, u32[]{:S(2)}, u32[]{:S(2)}) async-start(bf16[32,48,2048]{2,1,0:T(8,128)(2,1)} %convolution_convert_fusion), calls=%async_computation.1 | async-start | bytes 12582912 | tf_op jit(solution)/shard_map/all_to_all | solution.py:44
  173.9 144.1 %copy-start.1 = (f32[4,2048]{1,0:T(4,128)S(1)}, f32[4,2048]{1,0:T(4,128)}, u32[]{:S(2)}) copy-start(f32[4,2048]{1,0:T(4,128)} %param.17) | copy-start | bytes 98308
  318.2 3.1 copy-start
where the time goes:
time: 322 us
  blocking collectives  146 us (45%)
  waiting for transfers between devices  140 us (43%)
  matrix products  15.5 us (5%)
  other arithmetic  11.1 us (3%)
  local copies, waits for them, and re-layouts  5.76 us (2%)
  starting transfers between devices  4.05 us (1%)
    all_to_all x1, blocking collectives, local(): lax.all_to_all(outgoing, 'local', split_axis=0, concat_axis=0, tiled=True)  146 us
    all_to_all x1, waiting for transfers between devices, local(): lax.all_to_all(partial_value, 'local', split_axis=0, concat_axis=0, tiled...  140 us
    dot_general x1, matrix products, expert_block(): jnp.einsum('nch,hd->ncd', hidden, w_out[0], preferred_element_type=jnp.fl...  8.53 us
    dot_general x1, matrix products, expert_block(): jnp.einsum('ncd,dh->nch', row_block, w_in[0], preferred_element_type=jnp....  6.93 us
  transfers between devices with their start and end apart: 1, of which 1 were waited for; matrix products, arithmetic and copies ran while one was open for 0% of the time, Pallas kernels for 0%

commit v1 on v0

v1 whole, which is shorter than its diff:
```python
import functools

import jax
import jax.numpy as jnp
from jax import lax
from jax.experimental import pallas as pl
from jax.experimental.pallas import tpu as pltpu
from jax.sharding import PartitionSpec as P


def dispatch_kernel(cap, experts, plane_ref, ids_ref, tokens_ref, gain_ref, bias_ref, *out_refs):
    floats = tokens_ref[...].astype(jnp.float32)
    row_mean = jnp.mean(floats, axis=-1, keepdims=True)
    centered = floats - row_mean
    row_var = jnp.mean(centered * centered, axis=-1, keepdims=True)
    normed = centered * lax.rsqrt(row_var + 1e-05) * gain_ref[...] + bias_ref[...]
    normed = normed.astype(jnp.bfloat16)
    tok = floats.shape[0]
    top = ids_ref.shape[0]
    named = lax.rem(plane_ref[0] + lax.broadcasted_iota(jnp.int32, (8, tok), 0), experts)
    member = named == ids_ref[0:1, :]
    for k in range(1, top):
        member = member | (named == ids_ref[k : k + 1, :])
    member = jnp.where(member, 1.0, 0.0)
    before = lax.broadcasted_iota(jnp.int32, (tok, tok), 0) < lax.broadcasted_iota(jnp.int32, (tok, tok), 1)
    rank = jnp.dot(
        member.astype(jnp.bfloat16),
        jnp.where(before, 1.0, 0.0).astype(jnp.bfloat16),
        preferred_element_type=jnp.float32,
    )
    slot = lax.broadcasted_iota(jnp.int32, (cap, tok), 0).astype(jnp.float32)
    for d in range(experts):
        pick = jnp.where(slot == rank[d : d + 1, :], member[d : d + 1, :], 0.0).astype(jnp.bfloat16)
        out_refs[d][...] = jnp.dot(pick, normed, preferred_element_type=jnp.float32).astype(jnp.bfloat16)


def dispatch(plane, ids, tokens, gain, bias, cap, experts):
    width = tokens.shape[1]
    vmem = pl.BlockSpec(memory_space=pltpu.VMEM)
    return pl.pallas_call(
        functools.partial(dispatch_kernel, cap, experts),
        out_shape=[jax.ShapeDtypeStruct((cap, width), jnp.bfloat16)] * experts,
        in_specs=[pl.BlockSpec(memory_space=pltpu.SMEM)] + [vmem] * 4,
        out_specs=[vmem] * experts,
        name="dispatch",
    )(plane, ids.T, tokens, gain[None, :], bias[None, :])


def combine_kernel(cap, experts, plane_ref, ids_ref, gates_ref, tokens_ref, b_out_ref, *refs):
    row_refs, out_ref = refs[:-1], refs[-1]
    tok, top = ids_ref.shape
    lanes = 128
    named = lax.rem(plane_ref[0] + lax.broadcasted_iota(jnp.int32, (tok, lanes), 1), experts)
    member = jnp.zeros((tok, lanes), jnp.float32)
    gate = jnp.zeros((tok, lanes), jnp.float32)
    for k in range(top):
        hit = named == ids_ref[:, k : k + 1]
        member = jnp.where(hit, 1.0, member)
        gate = jnp.where(hit, gates_ref[:, k : k + 1], gate)
    before = lax.broadcasted_iota(jnp.int32, (tok, tok), 1) < lax.broadcasted_iota(jnp.int32, (tok, tok), 0)
    rank = jnp.dot(
        jnp.where(before, 1.0, 0.0).astype(jnp.bfloat16),
        member.astype(jnp.bfloat16),
        preferred_element_type=jnp.float32,
    )
    slot = lax.broadcasted_iota(jnp.int32, (tok, cap), 1).astype(jnp.float32)
    total = None
    for d in range(experts):
        pick = jnp.where(slot == rank[:, d : d + 1], member[:, d : d + 1], 0.0).astype(jnp.bfloat16)
        rows = jnp.dot(pick, row_refs[d][...], preferred_element_type=jnp.float32)
        bias = b_out_ref[pl.ds(lax.rem(plane_ref[0] + d, experts), 1), :]
        term = gate[:, d : d + 1] * (rows + bias)
        total = term if total is None else total + term
    out_ref[...] = (tokens_ref[...].astype(jnp.float32) + total).astype(jnp.bfloat16)


def combine(plane, ids, gates, tokens, b_out, rows, cap):
    experts = b_out.shape[0]
    vmem = pl.BlockSpec(memory_space=pltpu.VMEM)
    return pl.pallas_call(
        functools.partial(combine_kernel, cap, experts),
        out_shape=jax.ShapeDtypeStruct(tokens.shape, jnp.bfloat16),
        in_specs=[pl.BlockSpec(memory_space=pltpu.SMEM)] + [vmem] * (4 + experts),
        out_specs=vmem,
        name="combine",
    )(plane, ids, gates, tokens, b_out, *rows)


def expert_rows(rows, w_in, b_in, w_out):
    total = None
    for k in range(2):
        hidden = jnp.dot(rows, w_in[k], preferred_element_type=jnp.float32)
        hidden = jnp.maximum(hidden + b_in[k], 0.0).astype(jnp.bfloat16)
        part = jnp.dot(hidden, w_out[k], preferred_element_type=jnp.float32)
        total = part if total is None else total + part
    return total


def local(tokens, expert_ids, gate_weights, norm_gain, norm_bias, w_in, b_in, w_out, b_out):
    tok_dev = tokens.shape[0]
    top_count = expert_ids.shape[1]
    devices = lax.axis_size("local")
    experts = b_out.shape[0]
    shared = devices // experts
    assert shared == 8
    slot_cap = min(
        tok_dev, shared * max(1, (3 * tok_dev * top_count // (2 * experts) + shared - 1) // shared)
    )
    plane = (lax.axis_index("local") // shared).reshape(1).astype(jnp.int32)

    def across(value, bit):
        return lax.ppermute(value, "local", [(i, i ^ bit) for i in range(devices)])

    def along(value, planes):
        return lax.ppermute(value, "local", [(i, (i + planes * shared) % devices) for i in range(devices)])

    w_in, w_out = [w_in[0], across(w_in[0], 1)], [w_out[0], across(w_out[0], 1)]
    b_in = [b_in, across(b_in, 1)]

    blocks = dispatch(plane, expert_ids, tokens, norm_gain, norm_bias, slot_cap, experts)
    results = []
    for d in range(experts):
        near, far = (2, 4) if d % 2 == 0 else (4, 2)
        block = blocks[d] if d == 0 else along(blocks[d], d)
        first = across(block, near)
        second = across(block, far)
        third = across(first, far)
        rows = jnp.concatenate([block, first, second, third])
        part = expert_rows(rows, w_in, b_in, w_out).reshape(4, slot_cap, -1)
        part_first = part[1] + across(part[3].astype(jnp.bfloat16), far).astype(jnp.float32)
        summed = part[0] + across(part_first.astype(jnp.bfloat16), near).astype(jnp.float32)
        summed = summed + across(part[2].astype(jnp.bfloat16), far).astype(jnp.float32)
        summed = summed.astype(jnp.bfloat16)
        results.append(summed if d == 0 else along(summed, -d))
    return combine(plane, expert_ids, gate_weights, tokens, b_out, results, slot_cap)


def solution(mesh):
    in_specs = (
        P(("groups", "local"), None),
        P(("groups", "local"), None),
        P(("groups", "local"), None),
        P(),
        P(),
        P("local", None, None),
        P("local", None),
        P("local", None, None),
        P(),
    )
    out_specs = P(("groups", "local"), None)
    return jax.shard_map(local, mesh=mesh, in_specs=in_specs, out_specs=out_specs, check_vma=False)
```

time: 322 us -> 166 us (0.52)
  blocking collectives: 146 us -> 0 us
  waiting for transfers between devices: 140 us -> 53.7 us
  matrix products: 15.5 us -> 51.4 us
  starting transfers between devices: 4.05 us -> 37.2 us
  local copies, waits for them, and re-layouts: 5.76 us -> 10.8 us
  Pallas kernels: 0 us -> 5 us
  other arithmetic: 11.1 us -> 7.13 us
    all_to_all x1 -> x0, blocking collectives: 146 us -> none  [local(): lax.all_to_all(outgoing, 'local', split_axis=0, concat_axis=0, tiled=True)]
    all_to_all x1 -> x0, waiting for transfers between devices: 140 us -> none  [local(): lax.all_to_all(partial_value, 'local', split_axis=0, concat_axis=0, tiled...]
    ppermute x0 -> x33, waiting for transfers between devices: none -> 53.7 us  [the longest x27 28.8 us: across(): return lax.ppermute(value, 'local', [(i, i ^ bit) for i in range(devices)])]
    ppermute x0 -> x33, starting transfers between devices: none -> 37.2 us  [the longest x27 28.9 us: across(): return lax.ppermute(value, 'local', [(i, i ^ bit) for i in range(devices)])]
    dot_general x2 -> x8, matrix products: 15.5 us -> 51.4 us  [expert_rows(): part = jnp.dot(hidden, w_out[k], preferred_element_type=jnp.float32)]
    reduce_sum x5 -> x0, other arithmetic: 8.13 us -> none  [the longest x1 4.18 us: local(): jnp.sum(returned.reshape(experts, shared, slot_cap, model_width).astype(j...]
    unnamed x14 -> x32, local copies, waits for them, and re-layouts: 0.89 us -> 7.55 us
    convert_element_type x3 -> x8, other arithmetic: 1.99 us -> 7.13 us  [the longest x4 3.96 us: local(): summed = summed.astype(jnp.bfloat16)]
  transfers between devices with their start and end apart: 1 -> 33, of which waited for: 1 -> 16; matrix products, arithmetic and copies ran while one was open for 0% -> 37% of each run, Pallas kernels for 0% -> 0%
where the time goes in v1:
time: 166 us
  waiting for transfers between devices  53.7 us (32%)
  matrix products  51.4 us (31%)
  starting transfers between devices  37.2 us (22%)
  local copies, waits for them, and re-layouts  10.8 us (7%)
  other arithmetic  7.13 us (4%)
  Pallas kernels  5 us (3%)
    dot_general x8, matrix products, expert_rows(): part = jnp.dot(hidden, w_out[k], preferred_element_type=jnp.float32)  51.4 us
    ppermute x27, starting transfers between devices, across(): return lax.ppermute(value, 'local', [(i, i ^ bit) for i in range(devices)])  28.9 us
    ppermute x27, waiting for transfers between devices, across(): return lax.ppermute(value, 'local', [(i, i ^ bit) for i in range(devices)])  28.8 us
    ppermute x6, waiting for transfers between devices, along(): lax.ppermute(value, 'local', [(i, (i + planes * shared) % devices) for i...  24.9 us
    ppermute x6, starting transfers between devices, along(): lax.ppermute(value, 'local', [(i, (i + planes * shared) % devices) for i...  8.26 us
    unnamed x32, local copies, waits for them, and re-layouts  7.55 us
    convert_element_type x4, other arithmetic, local(): summed = summed.astype(jnp.bfloat16)  3.96 us
  transfers between devices with their start and end apart: 33, of which 16 were waited for; matrix products, arithmetic and copies ran while one was open for 37% of the time, Pallas kernels for 0%

profile of v1, /device:TPU:0, one launch (start us, length us, event | category | flops | bytes accessed | tf_op | source)
XLA Modules:
  0.0 165.5 jit_solution(11952944683245369642)
XLA Ops:
  0.0 2.3 %dispatch.1 = (bf16[48,2048]{1,0:T(8,128)(2,1)}, bf16[48,2048]{1,0:T(8,128)(2,1)}, bf16[48,2048]{1,0:T(8,128)(2,1)}, bf16[48,2048]{1,0:T(8,128)(2,1)}) custom-call(s32[1]{0:T(128)} %bitcast.plane_ref, s32[2,64]{1,0:T(2,128)} %bitcast.50, bf16[64,2048]{1,0:T(8,128)(2,1)} %tokens_ref.3, f32[1,2048]{1,0:T(1,128)} %bitcast.48, f32[1,2048]{1,0:T(1,128)} %bitcast.49), custom_call_target="tpu_custom_call" | custom-call | tf_op jit(solution)/shard_map/dispatch/pallas_call | solution.py:40
  2.3 2.9 %collective-permute-start = (bf16[48,2048]{1,0:T(8,128)(2,1)}, bf16[48,2048]{1,0:T(8,128)(2,1)}, u32[]{:S(2)}, u32[]{:S(2)}) collective-permute-start(bf16[48,2048]{1,0:T(8,128)(2,1)} %get-tuple-element.9), channel_id=1, source_target_pairs={{0,2},{1,3},{2,0},{3,1},{4,6},{5,7},{6,4},{7,5},{8,10},{9,11},{10,... | collective-permute-start | bytes 589832 | tf_op jit(solution)/shard_map/ppermute | solution.py:112
  5.2 1.5 collective-permute-start.1
  6.7 3.6 %collective-permute-start.25 = (bf16[48,2048]{1,0:T(8,128)(2,1)}, bf16[48,2048]{1,0:T(8,128)(2,1)S(1)}, u32[]{:S(2)}, u32[]{:S(2)}) collective-permute-start(bf16[48,2048]{1,0:T(8,128)(2,1)} %get-tuple-element.12), channel_id=1, source_target_pairs={{0,24},{1,25},{2,26},{3,27},{4,28},{5,29},{6,30},{7,31},{8,0},{9,1... | collective-permute-start | bytes 589832 | tf_op jit(solution)/shard_map/ppermute | solution.py:115
  15.6 10.6 %collective-permute-done.17 = bf16[48,2048]{1,0:T(8,128)(2,1)S(1)} collective-permute-done((bf16[48,2048]{1,0:T(8,128)(2,1)}, bf16[48,2048]{1,0:T(8,128)(2,1)S(1)}, u32[]{:S(2)}, u32[]{:S(2)}) %collective-permute-start.17) | collective-permute-done | bytes 196640 | tf_op jit(solution)/shard_map/ppermute | solution.py:115
  26.3 8.8 %collective-permute-done.9 = bf16[48,2048]{1,0:T(8,128)(2,1)S(1)} collective-permute-done((bf16[48,2048]{1,0:T(8,128)(2,1)}, bf16[48,2048]{1,0:T(8,128)(2,1)S(1)}, u32[]{:S(2)}, u32[]{:S(2)}) %collective-permute-start.9) | collective-permute-done | bytes 196640 | tf_op jit(solution)/shard_map/ppermute | solution.py:115
  36.7 1.6 collective-permute-start.2
  39.2 7.7 %collective-permute-done.2 = bf16[48,2048]{1,0:T(8,128)(2,1)S(1)} collective-permute-done((bf16[48,2048]{1,0:T(8,128)(2,1)}, bf16[48,2048]{1,0:T(8,128)(2,1)S(1)}, u32[]{:S(2)}, u32[]{:S(2)}) %collective-permute-start.2) | collective-permute-done | bytes 196640 | tf_op jit(solution)/shard_map/ppermute | solution.py:112
  47.5 6.7 %fusion.19 = f32[192,2048]{1,0:T(8,128)} fusion(bf16[192,2048]{1,0:T(8,128)(2,1)S(1)} %constant_dynamic-update-slice_fusion, f32[1024]{0:T(1024)} %bitcast.53, bf16[1,1024,2048]{2,1,0:T(8,128)(2,1)} %param.16, bf16[1,2048,1024]{2,1,0:T(8,128)(2,1)} %param.14), kind=kOutput, calls=%fused_computation.31 | convolution fusion | flops 1611202560 | bytes 10752000 | tf_op jit(solution)/shard_map/dot_general | solution.py:94
  54.2 1.5 collective-permute-start.18
  57.3 3.4 %collective-permute-done.18 = bf16[48,2048]{1,0:T(8,128)(2,1)S(1)} collective-permute-done((bf16[48,2048]{1,0:T(8,128)(2,1)}, bf16[48,2048]{1,0:T(8,128)(2,1)S(1)}, u32[]{:S(2)}, u32[]{:S(2)}) %collective-permute-start.18) | collective-permute-done | bytes 196640 | tf_op jit(solution)/shard_map/ppermute | solution.py:112
  62.8 3.6 %collective-permute-done.10 = bf16[48,2048]{1,0:T(8,128)(2,1)S(1)} collective-permute-done((bf16[48,2048]{1,0:T(8,128)(2,1)S(1)}, bf16[48,2048]{1,0:T(8,128)(2,1)S(1)}, u32[]{:S(2)}, u32[]{:S(2)}) %collective-permute-start.10) | collective-permute-done | bytes 196640 | tf_op jit(solution)/shard_map/ppermute | solution.py:112
  66.4 1.5 collective-permute-start.28
  70.0 2.0 %collective-permute-done.28 = bf16[48,2048]{1,0:T(8,128)(2,1)S(1)} collective-permute-done((bf16[48,2048]{1,0:T(8,128)(2,1)S(1)}, bf16[48,2048]{1,0:T(8,128)(2,1)S(1)}, u32[]{:S(2)}, u32[]{:S(2)}) %collective-permute-start.28) | collective-permute-done | bytes 196640 | tf_op jit(solution)/shard_map/ppermute | solution.py:112
  72.0 2.0 %collective-permute-start.12 = (bf16[48,2048]{1,0:T(8,128)(2,1)S(1)}, bf16[48,2048]{1,0:T(8,128)(2,1)S(1)}, u32[]{:S(2)}, u32[]{:S(2)}) collective-permute-start(bf16[48,2048]{1,0:T(8,128)(2,1)S(1)} %collective-permute-done.10), channel_id=1, source_target_pairs={{0,2},{1,3},{2,0},{3,1},{4,6},{5,7},{6,4},{7,5},{8,10},{9,11},{10,... | collective-permute-start | bytes 589832 | tf_op jit(solution)/shard_map/ppermute | solution.py:112
  74.8 3.0 %collective-permute-done.12 = bf16[48,2048]{1,0:T(8,128)(2,1)S(1)} collective-permute-done((bf16[48,2048]{1,0:T(8,128)(2,1)S(1)}, bf16[48,2048]{1,0:T(8,128)(2,1)S(1)}, u32[]{:S(2)}, u32[]{:S(2)}) %collective-permute-start.12) | collective-permute-done | bytes 196640 | tf_op jit(solution)/shard_map/ppermute | solution.py:112
  77.7 5.5 %fusion.16 = f32[192,2048]{1,0:T(8,128)S(1)} fusion(bf16[192,2048]{1,0:T(8,128)(2,1)} %copy-done.1, f32[1024]{0:T(1024)S(1)} %bitcast.54, bf16[1,1024,2048]{2,1,0:T(8,128)(2,1)} %param.16, bf16[1,2048,1024]{2,1,0:T(8,128)(2,1)} %param.14), kind=kOutput, calls=%fused_computation.28 | convolution fusion | flops 1611202560 | bytes 10752000 | tf_op jit(solution)/shard_map/dot_general | solution.py:94
  83.3 6.4 %fusion.17 = f32[192,2048]{1,0:T(8,128)} fusion(bf16[192,2048]{1,0:T(8,128)(2,1)S(1)} %constant_dynamic-update-slice_fusion.8, f32[1024]{0:T(1024)S(1)} %bitcast.55, bf16[1,1024,2048]{2,1,0:T(8,128)(2,1)} %param.16, bf16[1,2048,1024]{2,1,0:T(8,128)(2,1)} %param.14), kind=kOutput, calls=%fused_computation.29 | convolution fusion | flops 1611202560 | bytes 10752000 | tf_op jit(solution)/shard_map/dot_general | solution.py:94
  89.7 6.5 %fusion.18 = f32[192,2048]{1,0:T(8,128)} fusion(bf16[192,2048]{1,0:T(8,128)(2,1)S(1)} %constant_dynamic-update-slice_fusion.4, f32[1024]{0:T(1024)S(1)} %bitcast.56, bf16[1,1024,2048]{2,1,0:T(8,128)(2,1)} %param.16, bf16[1,2048,1024]{2,1,0:T(8,128)(2,1)} %param.14), kind=kOutput, calls=%fused_computation.30 | convolution fusion | flops 1611202560 | bytes 10752000 | tf_op jit(solution)/shard_map/dot_general | solution.py:94
  96.2 6.7 %fusion.75 = (bf16[192,2048]{1,0:T(8,128)(2,1)S(1)}, f32[192,2048]{1,0:T(8,128)}) fusion(f32[192,2048]{1,0:T(8,128)S(1)} %fusion.16, bf16[1024,2048]{1,0:T(8,128)(2,1)} %collective-permute-done.5, bf16[192,2048]{1,0:T(8,128)(2,1)} %copy-done.1, bf16[2048,1024]{1,0:T(8,128)(2,1)} %collective-permute-done.3, f32[1024]{0:T(1024)S(1)} %bitcast.44), kind=kOutput, calls=%fused_computation.107 | convolution fusion | flops 1611988992 | bytes 13111296 | tf_op jit(solution)/shard_map/dot_general | solution.py:94
  103.6 2.0 %collective-permute-start.29 = (bf16[48,2048]{1,0:T(8,128)(2,1)}, bf16[48,2048]{1,0:T(8,128)(2,1)}, u32[]{:S(2)}, u32[]{:S(2)}) collective-permute-start(bf16[48,2048]{1,0:T(8,128)(2,1)} %get-tuple-element.13), channel_id=1, source_target_pairs={{0,2},{1,3},{2,0},{3,1},{4,6},{5,7},{6,4},{7,5},{8,10},{9,11},{10,... | collective-permute-start | bytes 589832 | tf_op jit(solution)/shard_map/ppermute | solution.py:112
  105.7 5.9 %fusion.74 = (bf16[192,2048]{1,0:T(8,128)(2,1)S(1)}, f32[192,2048]{1,0:T(8,128)S(1)}) fusion(f32[192,2048]{1,0:T(8,128)} %fusion.17, bf16[1024,2048]{1,0:T(8,128)(2,1)} %collective-permute-done.5, bf16[192,2048]{1,0:T(8,128)(2,1)} %copy-done, bf16[2048,1024]{1,0:T(8,128)(2,1)} %collective-permute-done.3, f32[1024]{0:T(1024)S(1)} %bitcast.45), kind=kOutput, calls=%fused_computation.106 | convolution fusion | flops 1611988992 | bytes 13111296 | tf_op jit(solution)/shard_map/dot_general | solution.py:94
  114.3 6.9 %fusion.73 = (bf16[192,2048]{1,0:T(8,128)(2,1)S(1)}, f32[192,2048]{1,0:T(8,128)}) fusion(f32[192,2048]{1,0:T(8,128)} %fusion.18, bf16[1024,2048]{1,0:T(8,128)(2,1)} %collective-permute-done.5, bf16[192,2048]{1,0:T(8,128)(2,1)S(1)} %constant_dynamic-update-slice_fusion.4, bf16[2048,1024]{1,0:T(8,128)(2,1)} %collective-permute-done.3, f32[1024]{0:T(1024)S(1)} %bitcast.46), kind=kOutput, calls=%fused_computation.105 | convolution fusion | flops 1611988992 | bytes 13111296 | tf_op jit(solution)/shard_map/dot_general | solution.py:94
  122.0 2.0 %collective-permute-start.13 = (bf16[48,2048]{1,0:T(8,128)(2,1)}, bf16[48,2048]{1,0:T(8,128)(2,1)}, u32[]{:S(2)}, u32[]{:S(2)}) collective-permute-start(bf16[48,2048]{1,0:T(8,128)(2,1)} %get-tuple-element.17), channel_id=1, source_target_pairs={{0,2},{1,3},{2,0},{3,1},{4,6},{5,7},{6,4},{7,5},{8,10},{9,11},{10,... | collective-permute-start | bytes 589832 | tf_op jit(solution)/shard_map/ppermute | solution.py:112
  123.9 6.8 %fusion.72 = (bf16[192,2048]{1,0:T(8,128)(2,1)}, f32[192,2048]{1,0:T(8,128)S(1)}) fusion(f32[192,2048]{1,0:T(8,128)} %fusion.19, bf16[1024,2048]{1,0:T(8,128)(2,1)} %collective-permute-done.5, bf16[192,2048]{1,0:T(8,128)(2,1)} %copy-done.2, bf16[2048,1024]{1,0:T(8,128)(2,1)} %collective-permute-done.3, f32[1024]{0:T(1024)S(1)} %bitcast.47), kind=kOutput, calls=%fused_computation.104 | convolution fusion | flops 1611988992 | bytes 13111296 | tf_op jit(solution)/shard_map/dot_general | solution.py:94
  137.2 2.3 %collective-permute-done.6 = bf16[48,2048]{1,0:T(8,128)(2,1)S(1)} collective-permute-done((bf16[48,2048]{1,0:T(8,128)(2,1)S(1)}, bf16[48,2048]{1,0:T(8,128)(2,1)S(1)}, u32[]{:S(2)}, u32[]{:S(2)}) %collective-permute-start.6) | collective-permute-done | bytes 196640 | tf_op jit(solution)/shard_map/ppermute | solution.py:112
  140.7 1.5 collective-permute-start.22
  142.2 3.6 %collective-permute-done.30 = bf16[48,2048]{1,0:T(8,128)(2,1)S(1)} collective-permute-done((bf16[48,2048]{1,0:T(8,128)(2,1)S(1)}, bf16[48,2048]{1,0:T(8,128)(2,1)S(1)}, u32[]{:S(2)}, u32[]{:S(2)}) %collective-permute-start.30) | collective-permute-done | bytes 196640 | tf_op jit(solution)/shard_map/ppermute | solution.py:112
  148.1 1.5 collective-permute-start.7
  152.6 3.1 %collective-permute-start.16 = (bf16[48,2048]{1,0:T(8,128)(2,1)S(1)}, bf16[48,2048]{1,0:T(8,128)(2,1)S(1)}, u32[]{:S(2)}, u32[]{:S(2)}) collective-permute-start(bf16[48,2048]{1,0:T(8,128)(2,1)S(1)} %fusion.28), channel_id=1, source_target_pairs={{0,24},{1,25},{2,26},{3,27},{4,28},{5,29},{6,30},{7,31},{8,0},{9,1... | collective-permute-start | bytes 589832 | tf_op jit(solution)/shard_map/ppermute | solution.py:115
  157.2 4.2 %collective-permute-done.24.refs_2_ = bf16[48,2048]{1,0:T(8,128)(2,1)S(1)} collective-permute-done((bf16[48,2048]{1,0:T(8,128)(2,1)S(1)}, bf16[48,2048]{1,0:T(8,128)(2,1)S(1)}, u32[]{:S(2)}, u32[]{:S(2)}) %collective-permute-start.24) | collective-permute-done | bytes 196640 | tf_op jit(solution)/shard_map/ppermute | solution.py:115
  162.8 2.7 %combine.1 = bf16[64,2048]{1,0:T(8,128)(2,1)} custom-call(s32[1]{0:T(128)} %bitcast.plane_ref, s32[64,2]{1,0:T(8,128)} %copy.10.ids_ref, f32[64,2]{1,0:T(8,128)} %copy.11.gates_ref, bf16[64,2048]{1,0:T(8,128)(2,1)} %tokens_ref.3, f32[4,2048]{1,0:T(4,128)} %b_out_ref.1, bf16[48,2048]{1,0:T(8,128)(2,1)} %fusion.31.refs_0_, bf16[48,2048]{1,0:T(8,128)(2,1)} %copy-done.5, ...), custom_call_target="tpu_custom_call" | custom-call | tf_op jit(solution)/shard_map/combine/pallas_call | solution.py:80
  (92 shorter events, 34.8 us)
Async XLA Ops:
  2.3 32.9 %collective-permute-start = (bf16[48,2048]{1,0:T(8,128)(2,1)}, bf16[48,2048]{1,0:T(8,128)(2,1)}, u32[]{:S(2)}, u32[]{:S(2)}) collective-permute-start(bf16[48,2048]{1,0:T(8,128)(2,1)} %get-tuple-element.9), channel_id=1, source_target_pairs={{0,2},{1,3},{2,0},{3,1},{4,6},{5,7},{6,4},{7,5},{8,10},{9,11},{10,... | collective-permute-start | bytes 589832 | tf_op jit(solution)/shard_map/ppermute | solution.py:112
  5.2 31.4 %collective-permute-start.1 = (bf16[48,2048]{1,0:T(8,128)(2,1)}, bf16[48,2048]{1,0:T(8,128)(2,1)}, u32[]{:S(2)}, u32[]{:S(2)}) collective-permute-start(bf16[48,2048]{1,0:T(8,128)(2,1)} %get-tuple-element.9), channel_id=1, source_target_pairs={{0,4},{1,5},{2,6},{3,7},{4,0},{5,1},{6,2},{7,3},{8,12},{9,13},{10,... | collective-permute-start | bytes 589832 | tf_op jit(solution)/shard_map/ppermute | solution.py:112
  6.7 7.8 %collective-permute-start.25 = (bf16[48,2048]{1,0:T(8,128)(2,1)}, bf16[48,2048]{1,0:T(8,128)(2,1)S(1)}, u32[]{:S(2)}, u32[]{:S(2)}) collective-permute-start(bf16[48,2048]{1,0:T(8,128)(2,1)} %get-tuple-element.12), channel_id=1, source_target_pairs={{0,24},{1,25},{2,26},{3,27},{4,28},{5,29},{6,30},{7,31},{8,0},{9,1... | collective-permute-start | bytes 589832 | tf_op jit(solution)/shard_map/ppermute | solution.py:115
  10.3 85.9 %collective-permute-start.3 = (bf16[2048,1024]{1,0:T(8,128)(2,1)}, bf16[2048,1024]{1,0:T(8,128)(2,1)}, u32[]{:S(2)}, u32[]{:S(2)}) collective-permute-start(bf16[2048,1024]{1,0:T(8,128)(2,1)} %bitcast.51), channel_id=1, source_target_pairs={{0,1},{1,0},{2,3},{3,2},{4,5},{5,4},{6,7},{7,6},{8,9},{9,8},{10,11... | collective-permute-start | bytes 12582920 | tf_op jit(solution)/shard_map/ppermute | solution.py:112
  10.3 85.9 %collective-permute-start.5 = (bf16[1024,2048]{1,0:T(8,128)(2,1)}, bf16[1024,2048]{1,0:T(8,128)(2,1)}, u32[]{:S(2)}, u32[]{:S(2)}) collective-permute-start(bf16[1024,2048]{1,0:T(8,128)(2,1)} %bitcast.52), channel_id=1, source_target_pairs={{0,1},{1,0},{2,3},{3,2},{4,5},{5,4},{6,7},{7,6},{8,9},{9,8},{10,11... | collective-permute-start | bytes 12582920 | tf_op jit(solution)/shard_map/ppermute | solution.py:112
  14.6 11.7 %collective-permute-start.17 = (bf16[48,2048]{1,0:T(8,128)(2,1)}, bf16[48,2048]{1,0:T(8,128)(2,1)S(1)}, u32[]{:S(2)}, u32[]{:S(2)}) collective-permute-start(bf16[48,2048]{1,0:T(8,128)(2,1)} %get-tuple-element.11), channel_id=1, source_target_pairs={{0,16},{1,17},{2,18},{3,19},{4,20},{5,21},{6,22},{7,23},{8,24},{9,... | collective-permute-start | bytes 589832 | tf_op jit(solution)/shard_map/ppermute | solution.py:115
  26.3 8.8 %collective-permute-start.9 = (bf16[48,2048]{1,0:T(8,128)(2,1)}, bf16[48,2048]{1,0:T(8,128)(2,1)S(1)}, u32[]{:S(2)}, u32[]{:S(2)}) collective-permute-start(bf16[48,2048]{1,0:T(8,128)(2,1)} %get-tuple-element.10), channel_id=1, source_target_pairs={{0,8},{1,9},{2,10},{3,11},{4,12},{5,13},{6,14},{7,15},{8,16},{9,17... | collective-permute-start | bytes 589832 | tf_op jit(solution)/shard_map/ppermute | solution.py:115
  35.1 61.1 %collective-permute-start.4 = (f32[1,1024]{1,0:T(1,128)}, f32[1,1024]{1,0:T(1,128)S(1)}, u32[]{:S(2)}, u32[]{:S(2)}) collective-permute-start(f32[1,1024]{1,0:T(1,128)} %param.15), channel_id=1, source_target_pairs={{0,1},{1,0},{2,3},{3,2},{4,5},{5,4},{6,7},{7,6},{8,9},{9,8},{10,11... | collective-permute-start | bytes 12296 | tf_op jit(solution)/shard_map/ppermute | solution.py:112
  35.1 19.1 %collective-permute-start.26 = (bf16[48,2048]{1,0:T(8,128)(2,1)}, bf16[48,2048]{1,0:T(8,128)(2,1)S(1)}, u32[]{:S(2)}, u32[]{:S(2)}) collective-permute-start(bf16[48,2048]{1,0:T(8,128)(2,1)} %copy-done.7), channel_id=1, source_target_pairs={{0,4},{1,5},{2,6},{3,7},{4,0},{5,1},{6,2},{7,3},{8,12},{9,13},{10,... | collective-permute-start | bytes 589832 | tf_op jit(solution)/shard_map/ppermute | solution.py:112
  36.7 10.3 %collective-permute-start.2 = (bf16[48,2048]{1,0:T(8,128)(2,1)}, bf16[48,2048]{1,0:T(8,128)(2,1)S(1)}, u32[]{:S(2)}, u32[]{:S(2)}) collective-permute-start(bf16[48,2048]{1,0:T(8,128)(2,1)} %collective-permute-done), channel_id=1, source_target_pairs={{0,4},{1,5},{2,6},{3,7},{4,0},{5,1},{6,2},{7,3},{8,12},{9,13},{10,... | collective-permute-start | bytes 589832 | tf_op jit(solution)/shard_map/ppermute | solution.py:112
  47.0 8.8 %collective-permute-start.27 = (bf16[48,2048]{1,0:T(8,128)(2,1)}, bf16[48,2048]{1,0:T(8,128)(2,1)}, u32[]{:S(2)}, u32[]{:S(2)}) collective-permute-start(bf16[48,2048]{1,0:T(8,128)(2,1)} %copy-done.7), channel_id=1, source_target_pairs={{0,2},{1,3},{2,0},{3,1},{4,6},{5,7},{6,4},{7,5},{8,10},{9,11},{10,... | collective-permute-start | bytes 589832 | tf_op jit(solution)/shard_map/ppermute | solution.py:112
  54.2 6.5 %collective-permute-start.18 = (bf16[48,2048]{1,0:T(8,128)(2,1)}, bf16[48,2048]{1,0:T(8,128)(2,1)S(1)}, u32[]{:S(2)}, u32[]{:S(2)}) collective-permute-start(bf16[48,2048]{1,0:T(8,128)(2,1)} %copy-done.6), channel_id=1, source_target_pairs={{0,2},{1,3},{2,0},{3,1},{4,6},{5,7},{6,4},{7,5},{8,10},{9,11},{10,... | collective-permute-start | bytes 589832 | tf_op jit(solution)/shard_map/ppermute | solution.py:112
  55.8 6.4 %collective-permute-start.19 = (bf16[48,2048]{1,0:T(8,128)(2,1)}, bf16[48,2048]{1,0:T(8,128)(2,1)S(1)}, u32[]{:S(2)}, u32[]{:S(2)}) collective-permute-start(bf16[48,2048]{1,0:T(8,128)(2,1)} %copy-done.6), channel_id=1, source_target_pairs={{0,4},{1,5},{2,6},{3,7},{4,0},{5,1},{6,2},{7,3},{8,12},{9,13},{10,... | collective-permute-start | bytes 589832 | tf_op jit(solution)/shard_map/ppermute | solution.py:112
  60.7 5.7 %collective-permute-start.10 = (bf16[48,2048]{1,0:T(8,128)(2,1)S(1)}, bf16[48,2048]{1,0:T(8,128)(2,1)S(1)}, u32[]{:S(2)}, u32[]{:S(2)}) collective-permute-start(bf16[48,2048]{1,0:T(8,128)(2,1)S(1)} %collective-permute-done.9), channel_id=1, source_target_pairs={{0,4},{1,5},{2,6},{3,7},{4,0},{5,1},{6,2},{7,3},{8,12},{9,13},{10,... | collective-permute-start | bytes 589832 | tf_op jit(solution)/shard_map/ppermute | solution.py:112
  62.1 6.9 %collective-permute-start.11 = (bf16[48,2048]{1,0:T(8,128)(2,1)S(1)}, bf16[48,2048]{1,0:T(8,128)(2,1)S(1)}, u32[]{:S(2)}, u32[]{:S(2)}) collective-permute-start(bf16[48,2048]{1,0:T(8,128)(2,1)S(1)} %collective-permute-done.9), channel_id=1, source_target_pairs={{0,2},{1,3},{2,0},{3,1},{4,6},{5,7},{6,4},{7,5},{8,10},{9,11},{10,... | collective-permute-start | bytes 589832 | tf_op jit(solution)/shard_map/ppermute | solution.py:112
  66.4 5.7 %collective-permute-start.28 = (bf16[48,2048]{1,0:T(8,128)(2,1)S(1)}, bf16[48,2048]{1,0:T(8,128)(2,1)S(1)}, u32[]{:S(2)}, u32[]{:S(2)}) collective-permute-start(bf16[48,2048]{1,0:T(8,128)(2,1)S(1)} %collective-permute-done.26), channel_id=1, source_target_pairs={{0,2},{1,3},{2,0},{3,1},{4,6},{5,7},{6,4},{7,5},{8,10},{9,11},{10,... | collective-permute-start | bytes 589832 | tf_op jit(solution)/shard_map/ppermute | solution.py:112
  69.1 5.7 %collective-permute-start.20 = (bf16[48,2048]{1,0:T(8,128)(2,1)S(1)}, bf16[48,2048]{1,0:T(8,128)(2,1)S(1)}, u32[]{:S(2)}, u32[]{:S(2)}) collective-permute-start(bf16[48,2048]{1,0:T(8,128)(2,1)S(1)} %collective-permute-done.18), channel_id=1, source_target_pairs={{0,4},{1,5},{2,6},{3,7},{4,0},{5,1},{6,2},{7,3},{8,12},{9,13},{10,... | collective-permute-start | bytes 589832 | tf_op jit(solution)/shard_map/ppermute | solution.py:112
  72.0 5.7 %collective-permute-start.12 = (bf16[48,2048]{1,0:T(8,128)(2,1)S(1)}, bf16[48,2048]{1,0:T(8,128)(2,1)S(1)}, u32[]{:S(2)}, u32[]{:S(2)}) collective-permute-start(bf16[48,2048]{1,0:T(8,128)(2,1)S(1)} %collective-permute-done.10), channel_id=1, source_target_pairs={{0,2},{1,3},{2,0},{3,1},{4,6},{5,7},{6,4},{7,5},{8,10},{9,11},{10,... | collective-permute-start | bytes 589832 | tf_op jit(solution)/shard_map/ppermute | solution.py:112
  103.6 28.2 %collective-permute-start.29 = (bf16[48,2048]{1,0:T(8,128)(2,1)}, bf16[48,2048]{1,0:T(8,128)(2,1)}, u32[]{:S(2)}, u32[]{:S(2)}) collective-permute-start(bf16[48,2048]{1,0:T(8,128)(2,1)} %get-tuple-element.13), channel_id=1, source_target_pairs={{0,2},{1,3},{2,0},{3,1},{4,6},{5,7},{6,4},{7,5},{8,10},{9,11},{10,... | collective-permute-start | bytes 589832 | tf_op jit(solution)/shard_map/ppermute | solution.py:112
  105.6 35.1 %collective-permute-start.31 = (bf16[48,2048]{1,0:T(8,128)(2,1)}, bf16[48,2048]{1,0:T(8,128)(2,1)}, u32[]{:S(2)}, u32[]{:S(2)}) collective-permute-start(bf16[48,2048]{1,0:T(8,128)(2,1)} %get-tuple-element.14), channel_id=1, source_target_pairs={{0,2},{1,3},{2,0},{3,1},{4,6},{5,7},{6,4},{7,5},{8,10},{9,11},{10,... | collective-permute-start | bytes 589832 | tf_op jit(solution)/shard_map/ppermute | solution.py:112
  112.3 20.7 %collective-permute-start.21 = (bf16[48,2048]{1,0:T(8,128)(2,1)}, bf16[48,2048]{1,0:T(8,128)(2,1)}, u32[]{:S(2)}, u32[]{:S(2)}) collective-permute-start(bf16[48,2048]{1,0:T(8,128)(2,1)} %get-tuple-element.15), channel_id=1, source_target_pairs={{0,4},{1,5},{2,6},{3,7},{4,0},{5,1},{6,2},{7,3},{8,12},{9,13},{10,... | collective-permute-start | bytes 589832 | tf_op jit(solution)/shard_map/ppermute | solution.py:112
  113.0 35.1 %collective-permute-start.23 = (bf16[48,2048]{1,0:T(8,128)(2,1)S(1)}, bf16[48,2048]{1,0:T(8,128)(2,1)}, u32[]{:S(2)}, u32[]{:S(2)}) collective-permute-start(bf16[48,2048]{1,0:T(8,128)(2,1)S(1)} %get-tuple-element.16), channel_id=1, source_target_pairs={{0,4},{1,5},{2,6},{3,7},{4,0},{5,1},{6,2},{7,3},{8,12},{9,13},{10,... | collective-permute-start | bytes 589832 | tf_op jit(solution)/shard_map/ppermute | solution.py:112
  122.0 12.8 %collective-permute-start.13 = (bf16[48,2048]{1,0:T(8,128)(2,1)}, bf16[48,2048]{1,0:T(8,128)(2,1)}, u32[]{:S(2)}, u32[]{:S(2)}) collective-permute-start(bf16[48,2048]{1,0:T(8,128)(2,1)} %get-tuple-element.17), channel_id=1, source_target_pairs={{0,2},{1,3},{2,0},{3,1},{4,6},{5,7},{6,4},{7,5},{8,10},{9,11},{10,... | collective-permute-start | bytes 589832 | tf_op jit(solution)/shard_map/ppermute | solution.py:112
  131.8 18.8 %collective-permute-start.15 = (bf16[48,2048]{1,0:T(8,128)(2,1)S(1)}, bf16[48,2048]{1,0:T(8,128)(2,1)S(1)}, u32[]{:S(2)}, u32[]{:S(2)}) collective-permute-start(bf16[48,2048]{1,0:T(8,128)(2,1)S(1)} %get-tuple-element.18), channel_id=1, source_target_pairs={{0,2},{1,3},{2,0},{3,1},{4,6},{5,7},{6,4},{7,5},{8,10},{9,11},{10,... | collective-permute-start | bytes 589832 | tf_op jit(solution)/shard_map/ppermute | solution.py:112
  133.0 6.5 %collective-permute-start.6 = (bf16[48,2048]{1,0:T(8,128)(2,1)S(1)}, bf16[48,2048]{1,0:T(8,128)(2,1)S(1)}, u32[]{:S(2)}, u32[]{:S(2)}) collective-permute-start(bf16[48,2048]{1,0:T(8,128)(2,1)S(1)} %get-tuple-element.19), channel_id=1, source_target_pairs={{0,4},{1,5},{2,6},{3,7},{4,0},{5,1},{6,2},{7,3},{8,12},{9,13},{10,... | collective-permute-start | bytes 589832 | tf_op jit(solution)/shard_map/ppermute | solution.py:112
  134.7 21.0 %collective-permute-start.8 = (bf16[48,2048]{1,0:T(8,128)(2,1)S(1)}, bf16[48,2048]{1,0:T(8,128)(2,1)S(1)}, u32[]{:S(2)}, u32[]{:S(2)}) collective-permute-start(bf16[48,2048]{1,0:T(8,128)(2,1)S(1)} %get-tuple-element.20), channel_id=1, source_target_pairs={{0,4},{1,5},{2,6},{3,7},{4,0},{5,1},{6,2},{7,3},{8,12},{9,13},{10,... | collective-permute-start | bytes 589832 | tf_op jit(solution)/shard_map/ppermute | solution.py:112
  139.5 6.3 %collective-permute-start.30 = (bf16[48,2048]{1,0:T(8,128)(2,1)S(1)}, bf16[48,2048]{1,0:T(8,128)(2,1)S(1)}, u32[]{:S(2)}, u32[]{:S(2)}) collective-permute-start(bf16[48,2048]{1,0:T(8,128)(2,1)S(1)} %fusion.20), channel_id=1, source_target_pairs={{0,4},{1,5},{2,6},{3,7},{4,0},{5,1},{6,2},{7,3},{8,12},{9,13},{10,... | collective-permute-start | bytes 589832 | tf_op jit(solution)/shard_map/ppermute | solution.py:112
  140.7 8.9 %collective-permute-start.22 = (bf16[48,2048]{1,0:T(8,128)(2,1)S(1)}, bf16[48,2048]{1,0:T(8,128)(2,1)S(1)}, u32[]{:S(2)}, u32[]{:S(2)}) collective-permute-start(bf16[48,2048]{1,0:T(8,128)(2,1)S(1)} %fusion.23), channel_id=1, source_target_pairs={{0,2},{1,3},{2,0},{3,1},{4,6},{5,7},{6,4},{7,5},{8,10},{9,11},{10,... | collective-permute-start | bytes 589832 | tf_op jit(solution)/shard_map/ppermute | solution.py:112
  148.1 7.6 %collective-permute-start.7 = (bf16[48,2048]{1,0:T(8,128)(2,1)S(1)}, bf16[48,2048]{1,0:T(8,128)(2,1)S(1)}, u32[]{:S(2)}, u32[]{:S(2)}) collective-permute-start(bf16[48,2048]{1,0:T(8,128)(2,1)S(1)} %fusion.29), channel_id=1, source_target_pairs={{0,2},{1,3},{2,0},{3,1},{4,6},{5,7},{6,4},{7,5},{8,10},{9,11},{10,... | collective-permute-start | bytes 589832 | tf_op jit(solution)/shard_map/ppermute | solution.py:112
  149.6 7.6 %collective-permute-start.32 = (bf16[48,2048]{1,0:T(8,128)(2,1)S(1)}, bf16[48,2048]{1,0:T(8,128)(2,1)S(1)}, u32[]{:S(2)}, u32[]{:S(2)}) collective-permute-start(bf16[48,2048]{1,0:T(8,128)(2,1)S(1)} %fusion.22), channel_id=1, source_target_pairs={{0,8},{1,9},{2,10},{3,11},{4,12},{5,13},{6,14},{7,15},{8,16},{9,17... | collective-permute-start | bytes 589832 | tf_op jit(solution)/shard_map/ppermute | solution.py:115
  150.7 10.8 %collective-permute-start.24 = (bf16[48,2048]{1,0:T(8,128)(2,1)S(1)}, bf16[48,2048]{1,0:T(8,128)(2,1)S(1)}, u32[]{:S(2)}, u32[]{:S(2)}) collective-permute-start(bf16[48,2048]{1,0:T(8,128)(2,1)S(1)} %fusion.25), channel_id=1, source_target_pairs={{0,16},{1,17},{2,18},{3,19},{4,20},{5,21},{6,22},{7,23},{8,24},{9,... | collective-permute-start | bytes 589832 | tf_op jit(solution)/shard_map/ppermute | solution.py:115
  152.6 9.3 %collective-permute-start.16 = (bf16[48,2048]{1,0:T(8,128)(2,1)S(1)}, bf16[48,2048]{1,0:T(8,128)(2,1)S(1)}, u32[]{:S(2)}, u32[]{:S(2)}) collective-permute-start(bf16[48,2048]{1,0:T(8,128)(2,1)S(1)} %fusion.28), channel_id=1, source_target_pairs={{0,24},{1,25},{2,26},{3,27},{4,28},{5,29},{6,30},{7,31},{8,0},{9,1... | collective-permute-start | bytes 589832 | tf_op jit(solution)/shard_map/ppermute | solution.py:115
  (10 other events, 81.4 us)

commit v2 on v1

--- a/solution.py
+++ b/solution.py
@@ -6,6 +6,10 @@
 from jax.experimental import pallas as pl
 from jax.experimental.pallas import tpu as pltpu
 from jax.sharding import PartitionSpec as P
+
+
+def in_vmem(value):
+    return pltpu.with_memory_space_constraint(value, pltpu.VMEM)
 
 
 def dispatch_kernel(cap, experts, plane_ref, ids_ref, tokens_ref, gain_ref, bias_ref, *out_refs):
@@ -39,9 +43,10 @@
     vmem = pl.BlockSpec(memory_space=pltpu.VMEM)
     return pl.pallas_call(
         functools.partial(dispatch_kernel, cap, experts),
-        out_shape=[jax.ShapeDtypeStruct((cap, width), jnp.bfloat16)] * experts,
+        out_shape=[pltpu.VMEM((cap, width), jnp.bfloat16)] * experts,
         in_specs=[pl.BlockSpec(memory_space=pltpu.SMEM)] + [vmem] * 4,
         out_specs=[vmem] * experts,
+        compiler_params=pltpu.CompilerParams(vmem_limit_bytes=8 << 20),
         name="dispatch",
     )(plane, ids.T, tokens, gain[None, :], bias[None, :])
 
@@ -82,18 +87,49 @@
         out_shape=jax.ShapeDtypeStruct(tokens.shape, jnp.bfloat16),
         in_specs=[pl.BlockSpec(memory_space=pltpu.SMEM)] + [vmem] * (4 + experts),
         out_specs=vmem,
+        compiler_params=pltpu.CompilerParams(vmem_limit_bytes=8 << 20),
         name="combine",
-    )(plane, ids, gates, tokens, b_out, *rows)
+    )(plane, ids, gates, in_vmem(tokens), b_out, *[in_vmem(value) for value in rows])
 
 
-def expert_rows(rows, w_in, b_in, w_out):
-    total = None
-    for k in range(2):
-        hidden = jnp.dot(rows, w_in[k], preferred_element_type=jnp.float32)
-        hidden = jnp.maximum(hidden + b_in[k], 0.0).astype(jnp.bfloat16)
-        part = jnp.dot(hidden, w_out[k], preferred_element_type=jnp.float32)
-        total = part if total is None else total + part
-    return total
+def expert_kernel(tile, *refs):
+    blocks = (len(refs) - 8) // 2
+    row_refs, (in_0, in_1, bias_0, bias_1, out_0, out_1) = refs[:blocks], refs[blocks : blocks + 6]
+    part_refs, (rows, hidden) = refs[blocks + 6 : -2], refs[-2:]
+    cap = row_refs[0].shape[0]
+    units = in_0.shape[1]
+    for b in range(blocks):
+        rows[b * cap : (b + 1) * cap, :] = row_refs[b][...]
+    for k, (w_in, bias) in enumerate(((in_0, bias_0), (in_1, bias_1))):
+        for start in range(0, units, tile):
+            cols = slice(start, start + tile)
+            sums = jnp.dot(rows[...], w_in[:, cols], preferred_element_type=jnp.float32) + bias[:, cols]
+            hidden[:, k * units + start : k * units + start + tile] = jnp.maximum(sums, 0.0).astype(jnp.bfloat16)
+    for start in range(0, out_0.shape[1], tile):
+        cols = slice(start, start + tile)
+        sums = jnp.dot(hidden[:, :units], out_0[:, cols], preferred_element_type=jnp.float32)
+        sums += jnp.dot(hidden[:, units:], out_1[:, cols], preferred_element_type=jnp.float32)
+        for b in range(blocks):
+            part_refs[b][:, cols] = sums[b * cap : (b + 1) * cap, :].astype(part_refs[b].dtype)
+
+
+def expert_rows(rows, weights, types):
+    cap, width = rows[0].shape
+    units = weights[0].shape[1]
+    count = len(rows) * cap
+    vmem = pl.BlockSpec(memory_space=pltpu.VMEM)
+    return pl.pallas_call(
+        functools.partial(expert_kernel, 512),
+        out_shape=[pltpu.VMEM((cap, width), kind) for kind in types],
+        in_specs=[vmem] * (len(rows) + 6),
+        out_specs=[vmem] * len(rows),
+        scratch_shapes=[pltpu.VMEM((count, width), jnp.bfloat16), pltpu.VMEM((count, 2 * units), jnp.bfloat16)],
+        compiler_params=pltpu.CompilerParams(vmem_limit_bytes=12 << 20),
+        cost_estimate=pl.CostEstimate(
+            flops=8 * count * width * units, bytes_accessed=8 * width * units, transcendentals=0
+        ),
+        name="expert",
+    )(*[in_vmem(value) for value in (*rows, *weights)])
 
 
 def local(tokens, expert_ids, gate_weights, norm_gain, norm_bias, w_in, b_in, w_out, b_out):
@@ -106,6 +142,7 @@
     slot_cap = min(
         tok_dev, shared * max(1, (3 * tok_dev * top_count // (2 * experts) + shared - 1) // shared)
     )
+    slot_cap += -slot_cap % 16
     plane = (lax.axis_index("local") // shared).reshape(1).astype(jnp.int32)
 
     def across(value, bit):
@@ -114,8 +151,9 @@
     def along(value, planes):
         return lax.ppermute(value, "local", [(i, (i + planes * shared) % devices) for i in range(devices)])
 
-    w_in, w_out = [w_in[0], across(w_in[0], 1)], [w_out[0], across(w_out[0], 1)]
-    b_in = [b_in, across(b_in, 1)]
+    w_in, w_out = w_in[0], w_out[0]
+    weights = (w_in, across(w_in, 1), b_in, across(b_in, 1), w_out, across(w_out, 1))
+    kinds = (jnp.float32, jnp.float32, jnp.bfloat16, jnp.bfloat16)
 
     blocks = dispatch(plane, expert_ids, tokens, norm_gain, norm_bias, slot_cap, experts)
     results = []
@@ -125,12 +163,10 @@
         first = across(block, near)
         second = across(block, far)
         third = across(first, far)
-        rows = jnp.concatenate([block, first, second, third])
-        part = expert_rows(rows, w_in, b_in, w_out).reshape(4, slot_cap, -1)
-        part_first = part[1] + across(part[3].astype(jnp.bfloat16), far).astype(jnp.float32)
+        part = expert_rows([block, first, second, third], weights, kinds)
+        part_first = part[1] + across(part[3], far).astype(jnp.float32)
         summed = part[0] + across(part_first.astype(jnp.bfloat16), near).astype(jnp.float32)
-        summed = summed + across(part[2].astype(jnp.bfloat16), far).astype(jnp.float32)
-        summed = summed.astype(jnp.bfloat16)
+        summed = (summed + across(part[2], far).astype(jnp.float32)).astype(jnp.bfloat16)
         results.append(summed if d == 0 else along(summed, -d))
     return combine(plane, expert_ids, gate_weights, tokens, b_out, results, slot_cap)
 

time: 166 us -> 117 us (0.70)
  matrix products: 51.4 us -> 0 us
  Pallas kernels: 5 us -> 30.4 us
  waiting for transfers between devices: 53.7 us -> 38.4 us
  other arithmetic: 7.13 us -> 0.39 us
    dot_general x8 -> x0, matrix products: 51.4 us -> none  [expert_rows(): part = jnp.dot(hidden, w_out[k], preferred_element_type=jnp.float32)]
    pallas_call x0 -> x4, Pallas kernels: none -> 28.4 us  [expert_rows(): pl.pallas_call(functools.partial(expert_kernel, 512), out_shape=[pltpu.VM...]
    ppermute x27, waiting for transfers between devices: 28.8 us -> 20.8 us  [across(): return lax.ppermute(value, 'local', [(i, i ^ bit) for i in range(devices)])]
    ppermute x6, waiting for transfers between devices: 24.9 us -> 17.6 us  [along(): lax.ppermute(value, 'local', [(i, (i + planes * shared) % devices) for i...]
    convert_element_type x4, other arithmetic: 3.96 us -> 0.25 us  [local(): (summed + across(part[2], far).astype(jnp.float32)).astype(jnp.bfloat16)]
    slice x4 -> x0, local copies, waits for them, and re-layouts: 3.25 us -> none  [local(): part[3].astype(jnp.bfloat16)]
    convert_element_type x4, other arithmetic: 3.17 us -> 0.15 us  [local(): part_first.astype(jnp.bfloat16)]
    unnamed x32 -> x26, local copies, waits for them, and re-layouts: 7.55 us -> 9.64 us
  transfers between devices with their start and end apart: 33 -> 33, of which waited for: 16 -> 12; matrix products, arithmetic and copies ran while one was open for 37% -> 2% of each run, Pallas kernels for 0% -> 25%
where the time goes in v2:
time: 117 us; the launch traced here: 116 us
  waiting for transfers between devices  38.4 us (33%)
  starting transfers between devices  37.3 us (32%)
  Pallas kernels  30.4 us (26%)
  local copies, waits for them, and re-layouts  9.64 us (8%)
    ppermute x27, starting transfers between devices, across(): return lax.ppermute(value, 'local', [(i, i ^ bit) for i in range(devices)])  29.5 us
    pallas_call x4, Pallas kernels, expert_rows(): pl.pallas_call(functools.partial(expert_kernel, 512), out_shape=[pltpu.VM...  28.4 us
    ppermute x27, waiting for transfers between devices, across(): return lax.ppermute(value, 'local', [(i, i ^ bit) for i in range(devices)])  20.8 us
    ppermute x6, waiting for transfers between devices, along(): lax.ppermute(value, 'local', [(i, (i + planes * shared) % devices) for i...  17.6 us
    unnamed x26, local copies, waits for them, and re-layouts  9.64 us
    ppermute x6, starting transfers between devices, along(): lax.ppermute(value, 'local', [(i, (i + planes * shared) % devices) for i...  7.82 us
  transfers between devices with their start and end apart: 33, of which 12 were waited for; matrix products, arithmetic and copies ran while one was open for 2% of the time, Pallas kernels for 25%

profile of v2, /device:TPU:0, one launch (start us, length us, event | category | flops | bytes accessed | tf_op | source)
XLA Modules:
  0.0 116.3 jit_solution(9454765748526161631)
XLA Ops:
  4.1 5.1 %collective-permute-start.25 = (bf16[48,2048]{1,0:T(8,128)(2,1)S(1)}, bf16[48,2048]{1,0:T(8,128)(2,1)S(1)}, u32[]{:S(2)}, u32[]{:S(2)}) collective-permute-start(bf16[48,2048]{1,0:T(8,128)(2,1)S(1)} %get-tuple-element.40), channel_id=1, source_target_pairs={{0,24},{1,25},{2,26},{3,27},{4,28},{5,29},{6,30},{7,31},{8,0},{9,1... | collective-permute-start | bytes 589832 | tf_op jit(solution)/shard_map/ppermute | solution.py:152
  9.3 4.2 %collective-permute-done.4.refs_7_ = f32[1,1024]{1,0:T(1,128)S(1)} collective-permute-done((f32[1,1024]{1,0:T(1,128)}, f32[1,1024]{1,0:T(1,128)S(1)}, u32[]{:S(2)}, u32[]{:S(2)}) %collective-permute-start.4) | collective-permute-done | bytes 4128 | tf_op jit(solution)/shard_map/ppermute | solution.py:149
  14.6 1.7 %collective-permute-start.26 = (bf16[48,2048]{1,0:T(8,128)(2,1)S(1)}, bf16[48,2048]{1,0:T(8,128)(2,1)S(1)}, u32[]{:S(2)}, u32[]{:S(2)}) collective-permute-start(bf16[48,2048]{1,0:T(8,128)(2,1)S(1)} %collective-permute-done.25.refs_0_), channel_id=1, source_target_pairs={{0,4},{1,5},{2,6},{3,7},{4,0},{5,1},{6,2},{7,3},{8,12},{9,13},{10,... | collective-permute-start | bytes 589832 | tf_op jit(solution)/shard_map/ppermute | solution.py:149
  16.4 9.8 %collective-permute-done.17.refs_0_ = bf16[48,2048]{1,0:T(8,128)(2,1)S(1)} collective-permute-done((bf16[48,2048]{1,0:T(8,128)(2,1)S(1)}, bf16[48,2048]{1,0:T(8,128)(2,1)S(1)}, u32[]{:S(2)}, u32[]{:S(2)}) %collective-permute-start.17) | collective-permute-done | bytes 196640 | tf_op jit(solution)/shard_map/ppermute | solution.py:152
  26.1 1.5 %collective-permute-start.27 = (bf16[48,2048]{1,0:T(8,128)(2,1)S(1)}, bf16[48,2048]{1,0:T(8,128)(2,1)S(1)}, u32[]{:S(2)}, u32[]{:S(2)}) collective-permute-start(bf16[48,2048]{1,0:T(8,128)(2,1)S(1)} %collective-permute-done.25.refs_0_), channel_id=1, source_target_pairs={{0,2},{1,3},{2,0},{3,1},{4,6},{5,7},{6,4},{7,5},{8,10},{9,11},{10,... | collective-permute-start | bytes 589832 | tf_op jit(solution)/shard_map/ppermute | solution.py:149
  28.1 1.5 %collective-permute-start.28 = (bf16[48,2048]{1,0:T(8,128)(2,1)S(1)}, bf16[48,2048]{1,0:T(8,128)(2,1)S(1)}, u32[]{:S(2)}, u32[]{:S(2)}) collective-permute-start(bf16[48,2048]{1,0:T(8,128)(2,1)S(1)} %collective-permute-done.26.refs_1_), channel_id=1, source_target_pairs={{0,2},{1,3},{2,0},{3,1},{4,6},{5,7},{6,4},{7,5},{8,10},{9,11},{10,... | collective-permute-start | bytes 589832 | tf_op jit(solution)/shard_map/ppermute | solution.py:149
  31.2 2.7 %collective-permute-done.27.refs_2_ = bf16[48,2048]{1,0:T(8,128)(2,1)S(1)} collective-permute-done((bf16[48,2048]{1,0:T(8,128)(2,1)S(1)}, bf16[48,2048]{1,0:T(8,128)(2,1)S(1)}, u32[]{:S(2)}, u32[]{:S(2)}) %collective-permute-start.27) | collective-permute-done | bytes 196640 | tf_op jit(solution)/shard_map/ppermute | solution.py:149
  35.4 2.7 %collective-permute-done.18.refs_1_ = bf16[48,2048]{1,0:T(8,128)(2,1)S(1)} collective-permute-done((bf16[48,2048]{1,0:T(8,128)(2,1)S(1)}, bf16[48,2048]{1,0:T(8,128)(2,1)S(1)}, u32[]{:S(2)}, u32[]{:S(2)}) %collective-permute-start.18) | collective-permute-done | bytes 196640 | tf_op jit(solution)/shard_map/ppermute | solution.py:149
  38.1 1.5 %collective-permute-start.1 = (bf16[48,2048]{1,0:T(8,128)(2,1)S(1)}, bf16[48,2048]{1,0:T(8,128)(2,1)S(1)}, u32[]{:S(2)}, u32[]{:S(2)}) collective-permute-start(bf16[48,2048]{1,0:T(8,128)(2,1)S(1)} %get-tuple-element.25.refs_0_), channel_id=1, source_target_pairs={{0,4},{1,5},{2,6},{3,7},{4,0},{5,1},{6,2},{7,3},{8,12},{9,13},{10,... | collective-permute-start | bytes 589832 | tf_op jit(solution)/shard_map/ppermute | solution.py:149
  39.6 2.7 %collective-permute-done.28.refs_3_ = bf16[48,2048]{1,0:T(8,128)(2,1)S(1)} collective-permute-done((bf16[48,2048]{1,0:T(8,128)(2,1)S(1)}, bf16[48,2048]{1,0:T(8,128)(2,1)S(1)}, u32[]{:S(2)}, u32[]{:S(2)}) %collective-permute-start.28) | collective-permute-done | bytes 196640 | tf_op jit(solution)/shard_map/ppermute | solution.py:149
  42.3 1.5 %collective-permute-start.19 = (bf16[48,2048]{1,0:T(8,128)(2,1)S(1)}, bf16[48,2048]{1,0:T(8,128)(2,1)S(1)}, u32[]{:S(2)}, u32[]{:S(2)}) collective-permute-start(bf16[48,2048]{1,0:T(8,128)(2,1)S(1)} %collective-permute-done.17.refs_0_), channel_id=1, source_target_pairs={{0,4},{1,5},{2,6},{3,7},{4,0},{5,1},{6,2},{7,3},{8,12},{9,13},{10,... | collective-permute-start | bytes 589832 | tf_op jit(solution)/shard_map/ppermute | solution.py:149
  44.3 1.5 %collective-permute-start.20 = (bf16[48,2048]{1,0:T(8,128)(2,1)S(1)}, bf16[48,2048]{1,0:T(8,128)(2,1)S(1)}, u32[]{:S(2)}, u32[]{:S(2)}) collective-permute-start(bf16[48,2048]{1,0:T(8,128)(2,1)S(1)} %collective-permute-done.18.refs_1_), channel_id=1, source_target_pairs={{0,4},{1,5},{2,6},{3,7},{4,0},{5,1},{6,2},{7,3},{8,12},{9,13},{10,... | collective-permute-start | bytes 589832 | tf_op jit(solution)/shard_map/ppermute | solution.py:149
  45.9 2.2 %copy-done = bf16[1,2048,1024]{2,1,0:T(8,128)(2,1)S(1)} copy-done((bf16[1,2048,1024]{2,1,0:T(8,128)(2,1)S(1)}, bf16[1,2048,1024]{2,1,0:T(8,128)(2,1)}, u32[]{:S(2)}) %copy-start) | copy-done | bytes 4194328
  48.1 2.2 %copy-done.2 = bf16[1,1024,2048]{2,1,0:T(8,128)(2,1)S(1)} copy-done((bf16[1,1024,2048]{2,1,0:T(8,128)(2,1)S(1)}, bf16[1,1024,2048]{2,1,0:T(8,128)(2,1)}, u32[]{:S(2)}) %copy-start.2) | copy-done | bytes 4194328
  50.9 6.9 %expert.7 = (f32[48,2048]{1,0:T(8,128)S(1)}, f32[48,2048]{1,0:T(8,128)S(1)}, bf16[48,2048]{1,0:T(8,128)(2,1)S(1)}, bf16[48,2048]{1,0:T(8,128)(2,1)S(1)}) custom-call(bf16[48,2048]{1,0:T(8,128)(2,1)S(1)} %collective-permute-done.25.refs_0_, bf16[48,2048]{1,0:T(8,128)(2,1)S(1)} %collective-permute-done.26.refs_1_, ...), custom_call_target="tpu_custom_call" | custom-call | flops 3221225472 | bytes 16777216 | tf_op jit(solution)/shard_map/expert/pallas_call | solution.py:121
  57.9 1.6 %collective-permute-start.11 = (bf16[48,2048]{1,0:T(8,128)(2,1)S(1)}, bf16[48,2048]{1,0:T(8,128)(2,1)S(1)}, u32[]{:S(2)}, u32[]{:S(2)}) collective-permute-start(bf16[48,2048]{1,0:T(8,128)(2,1)S(1)} %collective-permute-done.9.refs_0_), channel_id=1, source_target_pairs={{0,2},{1,3},{2,0},{3,1},{4,6},{5,7},{6,4},{7,5},{8,10},{9,11},{10,... | collective-permute-start | bytes 589832 | tf_op jit(solution)/shard_map/ppermute | solution.py:149
  60.5 1.5 %collective-permute-start.29 = (bf16[48,2048]{1,0:T(8,128)(2,1)S(1)}, bf16[48,2048]{1,0:T(8,128)(2,1)S(1)}, u32[]{:S(2)}, u32[]{:S(2)}) collective-permute-start(bf16[48,2048]{1,0:T(8,128)(2,1)S(1)} %get-tuple-element.43), channel_id=1, source_target_pairs={{0,2},{1,3},{2,0},{3,1},{4,6},{5,7},{6,4},{7,5},{8,10},{9,11},{10,... | collective-permute-start | bytes 589832 | tf_op jit(solution)/shard_map/ppermute | solution.py:149
  62.0 6.9 %expert.6 = (f32[48,2048]{1,0:T(8,128)S(1)}, f32[48,2048]{1,0:T(8,128)S(1)}, bf16[48,2048]{1,0:T(8,128)(2,1)S(1)}, bf16[48,2048]{1,0:T(8,128)(2,1)S(1)}) custom-call(bf16[48,2048]{1,0:T(8,128)(2,1)S(1)} %collective-permute-done.17.refs_0_, bf16[48,2048]{1,0:T(8,128)(2,1)S(1)} %collective-permute-done.18.refs_1_, ...), custom_call_target="tpu_custom_call" | custom-call | flops 3221225472 | bytes 16777216 | tf_op jit(solution)/shard_map/expert/pallas_call | solution.py:121
  69.5 1.6 %collective-permute-start.21 = (bf16[48,2048]{1,0:T(8,128)(2,1)S(1)}, bf16[48,2048]{1,0:T(8,128)(2,1)S(1)}, u32[]{:S(2)}, u32[]{:S(2)}) collective-permute-start(bf16[48,2048]{1,0:T(8,128)(2,1)S(1)} %get-tuple-element.38), channel_id=1, source_target_pairs={{0,4},{1,5},{2,6},{3,7},{4,0},{5,1},{6,2},{7,3},{8,12},{9,13},{10,... | collective-permute-start | bytes 589832 | tf_op jit(solution)/shard_map/ppermute | solution.py:149
  71.1 7.6 %expert.5 = (f32[48,2048]{1,0:T(8,128)S(1)}, f32[48,2048]{1,0:T(8,128)S(1)}, bf16[48,2048]{1,0:T(8,128)(2,1)S(1)}, bf16[48,2048]{1,0:T(8,128)(2,1)S(1)}) custom-call(bf16[48,2048]{1,0:T(8,128)(2,1)S(1)} %collective-permute-done.9.refs_0_, bf16[48,2048]{1,0:T(8,128)(2,1)S(1)} %collective-permute-done.10.refs_1_, ...), custom_call_target="tpu_custom_call" | custom-call | flops 3221225472 | bytes 16777216 | tf_op jit(solution)/shard_map/expert/pallas_call | solution.py:121
  78.9 1.9 %collective-permute-start.13 = (bf16[48,2048]{1,0:T(8,128)(2,1)S(1)}, bf16[48,2048]{1,0:T(8,128)(2,1)S(1)}, u32[]{:S(2)}, u32[]{:S(2)}) collective-permute-start(bf16[48,2048]{1,0:T(8,128)(2,1)S(1)} %get-tuple-element.33), channel_id=1, source_target_pairs={{0,2},{1,3},{2,0},{3,1},{4,6},{5,7},{6,4},{7,5},{8,10},{9,11},{10,... | collective-permute-start | bytes 589832 | tf_op jit(solution)/shard_map/ppermute | solution.py:149
  80.8 6.9 %expert.4 = (f32[48,2048]{1,0:T(8,128)S(1)}, f32[48,2048]{1,0:T(8,128)S(1)}, bf16[48,2048]{1,0:T(8,128)(2,1)S(1)}, bf16[48,2048]{1,0:T(8,128)(2,1)S(1)}) custom-call(bf16[48,2048]{1,0:T(8,128)(2,1)S(1)} %get-tuple-element.25.refs_0_, bf16[48,2048]{1,0:T(8,128)(2,1)S(1)} %collective-permute-done.refs_1_, bf16[48,2048]{1,0:T(8,128)(2,1)S(1)} %collective-permute-done.1.refs_2_, ...), custom_call_target="tpu_custom_call" | custom-call | flops 3221225472 | bytes 16777216 | tf_op jit(solution)/shard_map/expert/pallas_call | solution.py:121
  88.0 2.0 %collective-permute-start.6 = (bf16[48,2048]{1,0:T(8,128)(2,1)S(1)}, bf16[48,2048]{1,0:T(8,128)(2,1)S(1)}, u32[]{:S(2)}, u32[]{:S(2)}) collective-permute-start(bf16[48,2048]{1,0:T(8,128)(2,1)S(1)} %get-tuple-element.28), channel_id=1, source_target_pairs={{0,4},{1,5},{2,6},{3,7},{4,0},{5,1},{6,2},{7,3},{8,12},{9,13},{10,... | collective-permute-start | bytes 589832 | tf_op jit(solution)/shard_map/ppermute | solution.py:149
  90.2 4.1 %collective-permute-done.6 = bf16[48,2048]{1,0:T(8,128)(2,1)S(1)} collective-permute-done((bf16[48,2048]{1,0:T(8,128)(2,1)S(1)}, bf16[48,2048]{1,0:T(8,128)(2,1)S(1)}, u32[]{:S(2)}, u32[]{:S(2)}) %collective-permute-start.6) | collective-permute-done | bytes 196640 | tf_op jit(solution)/shard_map/ppermute | solution.py:149
  94.3 1.7 %collective-permute-start.30 = (bf16[48,2048]{1,0:T(8,128)(2,1)S(1)}, bf16[48,2048]{1,0:T(8,128)(2,1)S(1)}, u32[]{:S(2)}, u32[]{:S(2)}) collective-permute-start(bf16[48,2048]{1,0:T(8,128)(2,1)S(1)} %add_convert_fusion.1), channel_id=1, source_target_pairs={{0,4},{1,5},{2,6},{3,7},{4,0},{5,1},{6,2},{7,3},{8,12},{9,13},{10,... | collective-permute-start | bytes 589832 | tf_op jit(solution)/shard_map/ppermute | solution.py:149
  96.0 1.6 %collective-permute-start.22 = (bf16[48,2048]{1,0:T(8,128)(2,1)S(1)}, bf16[48,2048]{1,0:T(8,128)(2,1)S(1)}, u32[]{:S(2)}, u32[]{:S(2)}) collective-permute-start(bf16[48,2048]{1,0:T(8,128)(2,1)S(1)} %add_convert_fusion.3), channel_id=1, source_target_pairs={{0,2},{1,3},{2,0},{3,1},{4,6},{5,7},{6,4},{7,5},{8,10},{9,11},{10,... | collective-permute-start | bytes 589832 | tf_op jit(solution)/shard_map/ppermute | solution.py:149
  97.6 3.0 %collective-permute-done.30 = bf16[48,2048]{1,0:T(8,128)(2,1)S(1)} collective-permute-done((bf16[48,2048]{1,0:T(8,128)(2,1)S(1)}, bf16[48,2048]{1,0:T(8,128)(2,1)S(1)}, u32[]{:S(2)}, u32[]{:S(2)}) %collective-permute-start.30) | collective-permute-done | bytes 196640 | tf_op jit(solution)/shard_map/ppermute | solution.py:149
  100.6 1.7 %collective-permute-start.14 = (bf16[48,2048]{1,0:T(8,128)(2,1)S(1)}, bf16[48,2048]{1,0:T(8,128)(2,1)S(1)}, u32[]{:S(2)}, u32[]{:S(2)}) collective-permute-start(bf16[48,2048]{1,0:T(8,128)(2,1)S(1)} %add_convert_fusion.5), channel_id=1, source_target_pairs={{0,4},{1,5},{2,6},{3,7},{4,0},{5,1},{6,2},{7,3},{8,12},{9,13},{10,... | collective-permute-start | bytes 589832 | tf_op jit(solution)/shard_map/ppermute | solution.py:149
  102.3 1.6 %collective-permute-start.7 = (bf16[48,2048]{1,0:T(8,128)(2,1)S(1)}, bf16[48,2048]{1,0:T(8,128)(2,1)S(1)}, u32[]{:S(2)}, u32[]{:S(2)}) collective-permute-start(bf16[48,2048]{1,0:T(8,128)(2,1)S(1)} %add_convert_fusion.7), channel_id=1, source_target_pairs={{0,2},{1,3},{2,0},{3,1},{4,6},{5,7},{6,4},{7,5},{8,10},{9,11},{10,... | collective-permute-start | bytes 589832 | tf_op jit(solution)/shard_map/ppermute | solution.py:149
  106.3 1.7 %collective-permute-start.16 = (bf16[48,2048]{1,0:T(8,128)(2,1)S(1)}, bf16[48,2048]{1,0:T(8,128)(2,1)S(1)}, u32[]{:S(2)}, u32[]{:S(2)}) collective-permute-start(bf16[48,2048]{1,0:T(8,128)(2,1)S(1)} %add_convert_fusion.4), channel_id=1, source_target_pairs={{0,24},{1,25},{2,26},{3,27},{4,28},{5,29},{6,30},{7,31},{8,0},{9,1... | collective-permute-start | bytes 589832 | tf_op jit(solution)/shard_map/ppermute | solution.py:152
  108.2 3.4 %collective-permute-done.32.refs_3_ = bf16[48,2048]{1,0:T(8,128)(2,1)S(1)} collective-permute-done((bf16[48,2048]{1,0:T(8,128)(2,1)S(1)}, bf16[48,2048]{1,0:T(8,128)(2,1)S(1)}, u32[]{:S(2)}, u32[]{:S(2)}) %collective-permute-start.32) | collective-permute-done | bytes 196640 | tf_op jit(solution)/shard_map/ppermute | solution.py:152
  111.6 3.3 %collective-permute-done.24.refs_2_ = bf16[48,2048]{1,0:T(8,128)(2,1)S(1)} collective-permute-done((bf16[48,2048]{1,0:T(8,128)(2,1)S(1)}, bf16[48,2048]{1,0:T(8,128)(2,1)S(1)}, u32[]{:S(2)}, u32[]{:S(2)}) %collective-permute-start.24) | collective-permute-done | bytes 196640 | tf_op jit(solution)/shard_map/ppermute | solution.py:152
  (74 shorter events, 16.5 us)
Async XLA Ops:
  0.0 43.8 %collective-permute-start.3 = (bf16[2048,1024]{1,0:T(8,128)(2,1)}, bf16[2048,1024]{1,0:T(8,128)(2,1)}, u32[]{:S(2)}, u32[]{:S(2)}) collective-permute-start(bf16[2048,1024]{1,0:T(8,128)(2,1)} %bitcast.6), channel_id=1, source_target_pairs={{0,1},{1,0},{2,3},{3,2},{4,5},{5,4},{6,7},{7,6},{8,9},{9,8},{10,11... | collective-permute-start | bytes 12582920 | tf_op jit(solution)/shard_map/ppermute | solution.py:149
  0.5 43.9 %collective-permute-start.5 = (bf16[1024,2048]{1,0:T(8,128)(2,1)}, bf16[1024,2048]{1,0:T(8,128)(2,1)}, u32[]{:S(2)}, u32[]{:S(2)}) collective-permute-start(bf16[1024,2048]{1,0:T(8,128)(2,1)} %bitcast.11), channel_id=1, source_target_pairs={{0,1},{1,0},{2,3},{3,2},{4,5},{5,4},{6,7},{7,6},{8,9},{9,8},{10,11... | collective-permute-start | bytes 12582920 | tf_op jit(solution)/shard_map/ppermute | solution.py:149
  4.1 10.5 %collective-permute-start.25 = (bf16[48,2048]{1,0:T(8,128)(2,1)S(1)}, bf16[48,2048]{1,0:T(8,128)(2,1)S(1)}, u32[]{:S(2)}, u32[]{:S(2)}) collective-permute-start(bf16[48,2048]{1,0:T(8,128)(2,1)S(1)} %get-tuple-element.40), channel_id=1, source_target_pairs={{0,24},{1,25},{2,26},{3,27},{4,28},{5,29},{6,30},{7,31},{8,0},{9,1... | collective-permute-start | bytes 589832 | tf_op jit(solution)/shard_map/ppermute | solution.py:152
  9.3 16.9 %collective-permute-start.17 = (bf16[48,2048]{1,0:T(8,128)(2,1)S(1)}, bf16[48,2048]{1,0:T(8,128)(2,1)S(1)}, u32[]{:S(2)}, u32[]{:S(2)}) collective-permute-start(bf16[48,2048]{1,0:T(8,128)(2,1)S(1)} %get-tuple-element.35), channel_id=1, source_target_pairs={{0,16},{1,17},{2,18},{3,19},{4,20},{5,21},{6,22},{7,23},{8,24},{9,... | collective-permute-start | bytes 589832 | tf_op jit(solution)/shard_map/ppermute | solution.py:152
  13.5 14.2 %collective-permute-start.9 = (bf16[48,2048]{1,0:T(8,128)(2,1)S(1)}, bf16[48,2048]{1,0:T(8,128)(2,1)S(1)}, u32[]{:S(2)}, u32[]{:S(2)}) collective-permute-start(bf16[48,2048]{1,0:T(8,128)(2,1)S(1)} %get-tuple-element.30), channel_id=1, source_target_pairs={{0,8},{1,9},{2,10},{3,11},{4,12},{5,13},{6,14},{7,15},{8,16},{9,17... | collective-permute-start | bytes 589832 | tf_op jit(solution)/shard_map/ppermute | solution.py:152
  14.6 13.5 %collective-permute-start.26 = (bf16[48,2048]{1,0:T(8,128)(2,1)S(1)}, bf16[48,2048]{1,0:T(8,128)(2,1)S(1)}, u32[]{:S(2)}, u32[]{:S(2)}) collective-permute-start(bf16[48,2048]{1,0:T(8,128)(2,1)S(1)} %collective-permute-done.25.refs_0_), channel_id=1, source_target_pairs={{0,4},{1,5},{2,6},{3,7},{4,0},{5,1},{6,2},{7,3},{8,12},{9,13},{10,... | collective-permute-start | bytes 589832 | tf_op jit(solution)/shard_map/ppermute | solution.py:149
  26.1 7.8 %collective-permute-start.27 = (bf16[48,2048]{1,0:T(8,128)(2,1)S(1)}, bf16[48,2048]{1,0:T(8,128)(2,1)S(1)}, u32[]{:S(2)}, u32[]{:S(2)}) collective-permute-start(bf16[48,2048]{1,0:T(8,128)(2,1)S(1)} %collective-permute-done.25.refs_0_), channel_id=1, source_target_pairs={{0,2},{1,3},{2,0},{3,1},{4,6},{5,7},{6,4},{7,5},{8,10},{9,11},{10,... | collective-permute-start | bytes 589832 | tf_op jit(solution)/shard_map/ppermute | solution.py:149
  27.6 10.5 %collective-permute-start.18 = (bf16[48,2048]{1,0:T(8,128)(2,1)S(1)}, bf16[48,2048]{1,0:T(8,128)(2,1)S(1)}, u32[]{:S(2)}, u32[]{:S(2)}) collective-permute-start(bf16[48,2048]{1,0:T(8,128)(2,1)S(1)} %collective-permute-done.17.refs_0_), channel_id=1, source_target_pairs={{0,2},{1,3},{2,0},{3,1},{4,6},{5,7},{6,4},{7,5},{8,10},{9,11},{10,... | collective-permute-start | bytes 589832 | tf_op jit(solution)/shard_map/ppermute | solution.py:149
  28.1 14.2 %collective-permute-start.28 = (bf16[48,2048]{1,0:T(8,128)(2,1)S(1)}, bf16[48,2048]{1,0:T(8,128)(2,1)S(1)}, u32[]{:S(2)}, u32[]{:S(2)}) collective-permute-start(bf16[48,2048]{1,0:T(8,128)(2,1)S(1)} %collective-permute-done.26.refs_1_), channel_id=1, source_target_pairs={{0,2},{1,3},{2,0},{3,1},{4,6},{5,7},{6,4},{7,5},{8,10},{9,11},{10,... | collective-permute-start | bytes 589832 | tf_op jit(solution)/shard_map/ppermute | solution.py:149
  33.9 24.0 %collective-permute-start = (bf16[48,2048]{1,0:T(8,128)(2,1)S(1)}, bf16[48,2048]{1,0:T(8,128)(2,1)S(1)}, u32[]{:S(2)}, u32[]{:S(2)}) collective-permute-start(bf16[48,2048]{1,0:T(8,128)(2,1)S(1)} %get-tuple-element.25.refs_0_), channel_id=1, source_target_pairs={{0,2},{1,3},{2,0},{3,1},{4,6},{5,7},{6,4},{7,5},{8,10},{9,11},{10,... | collective-permute-start | bytes 589832 | tf_op jit(solution)/shard_map/ppermute | solution.py:149
  38.1 40.6 %collective-permute-start.1 = (bf16[48,2048]{1,0:T(8,128)(2,1)S(1)}, bf16[48,2048]{1,0:T(8,128)(2,1)S(1)}, u32[]{:S(2)}, u32[]{:S(2)}) collective-permute-start(bf16[48,2048]{1,0:T(8,128)(2,1)S(1)} %get-tuple-element.25.refs_0_), channel_id=1, source_target_pairs={{0,4},{1,5},{2,6},{3,7},{4,0},{5,1},{6,2},{7,3},{8,12},{9,13},{10,... | collective-permute-start | bytes 589832 | tf_op jit(solution)/shard_map/ppermute | solution.py:149
  42.3 17.1 %collective-permute-start.19 = (bf16[48,2048]{1,0:T(8,128)(2,1)S(1)}, bf16[48,2048]{1,0:T(8,128)(2,1)S(1)}, u32[]{:S(2)}, u32[]{:S(2)}) collective-permute-start(bf16[48,2048]{1,0:T(8,128)(2,1)S(1)} %collective-permute-done.17.refs_0_), channel_id=1, source_target_pairs={{0,4},{1,5},{2,6},{3,7},{4,0},{5,1},{6,2},{7,3},{8,12},{9,13},{10,... | collective-permute-start | bytes 589832 | tf_op jit(solution)/shard_map/ppermute | solution.py:149
  43.8 16.1 %collective-permute-start.10 = (bf16[48,2048]{1,0:T(8,128)(2,1)S(1)}, bf16[48,2048]{1,0:T(8,128)(2,1)S(1)}, u32[]{:S(2)}, u32[]{:S(2)}) collective-permute-start(bf16[48,2048]{1,0:T(8,128)(2,1)S(1)} %collective-permute-done.9.refs_0_), channel_id=1, source_target_pairs={{0,4},{1,5},{2,6},{3,7},{4,0},{5,1},{6,2},{7,3},{8,12},{9,13},{10,... | collective-permute-start | bytes 589832 | tf_op jit(solution)/shard_map/ppermute | solution.py:149
  44.3 16.1 %collective-permute-start.20 = (bf16[48,2048]{1,0:T(8,128)(2,1)S(1)}, bf16[48,2048]{1,0:T(8,128)(2,1)S(1)}, u32[]{:S(2)}, u32[]{:S(2)}) collective-permute-start(bf16[48,2048]{1,0:T(8,128)(2,1)S(1)} %collective-permute-done.18.refs_1_), channel_id=1, source_target_pairs={{0,4},{1,5},{2,6},{3,7},{4,0},{5,1},{6,2},{7,3},{8,12},{9,13},{10,... | collective-permute-start | bytes 589832 | tf_op jit(solution)/shard_map/ppermute | solution.py:149
  57.9 11.0 %collective-permute-start.11 = (bf16[48,2048]{1,0:T(8,128)(2,1)S(1)}, bf16[48,2048]{1,0:T(8,128)(2,1)S(1)}, u32[]{:S(2)}, u32[]{:S(2)}) collective-permute-start(bf16[48,2048]{1,0:T(8,128)(2,1)S(1)} %collective-permute-done.9.refs_0_), channel_id=1, source_target_pairs={{0,2},{1,3},{2,0},{3,1},{4,6},{5,7},{6,4},{7,5},{8,10},{9,11},{10,... | collective-permute-start | bytes 589832 | tf_op jit(solution)/shard_map/ppermute | solution.py:149
  59.4 19.4 %collective-permute-start.2 = (bf16[48,2048]{1,0:T(8,128)(2,1)S(1)}, bf16[48,2048]{1,0:T(8,128)(2,1)S(1)}, u32[]{:S(2)}, u32[]{:S(2)}) collective-permute-start(bf16[48,2048]{1,0:T(8,128)(2,1)S(1)} %collective-permute-done.refs_1_), channel_id=1, source_target_pairs={{0,4},{1,5},{2,6},{3,7},{4,0},{5,1},{6,2},{7,3},{8,12},{9,13},{10,... | collective-permute-start | bytes 589832 | tf_op jit(solution)/shard_map/ppermute | solution.py:149
  59.9 9.6 %collective-permute-start.12 = (bf16[48,2048]{1,0:T(8,128)(2,1)S(1)}, bf16[48,2048]{1,0:T(8,128)(2,1)S(1)}, u32[]{:S(2)}, u32[]{:S(2)}) collective-permute-start(bf16[48,2048]{1,0:T(8,128)(2,1)S(1)} %collective-permute-done.10.refs_1_), channel_id=1, source_target_pairs={{0,2},{1,3},{2,0},{3,1},{4,6},{5,7},{6,4},{7,5},{8,10},{9,11},{10,... | collective-permute-start | bytes 589832 | tf_op jit(solution)/shard_map/ppermute | solution.py:149
  60.5 27.2 %collective-permute-start.29 = (bf16[48,2048]{1,0:T(8,128)(2,1)S(1)}, bf16[48,2048]{1,0:T(8,128)(2,1)S(1)}, u32[]{:S(2)}, u32[]{:S(2)}) collective-permute-start(bf16[48,2048]{1,0:T(8,128)(2,1)S(1)} %get-tuple-element.43), channel_id=1, source_target_pairs={{0,2},{1,3},{2,0},{3,1},{4,6},{5,7},{6,4},{7,5},{8,10},{9,11},{10,... | collective-permute-start | bytes 589832 | tf_op jit(solution)/shard_map/ppermute | solution.py:149
  68.9 27.1 %collective-permute-start.31 = (bf16[48,2048]{1,0:T(8,128)(2,1)S(1)}, bf16[48,2048]{1,0:T(8,128)(2,1)S(1)}, u32[]{:S(2)}, u32[]{:S(2)}) collective-permute-start(bf16[48,2048]{1,0:T(8,128)(2,1)S(1)} %get-tuple-element.44), channel_id=1, source_target_pairs={{0,2},{1,3},{2,0},{3,1},{4,6},{5,7},{6,4},{7,5},{8,10},{9,11},{10,... | collective-permute-start | bytes 589832 | tf_op jit(solution)/shard_map/ppermute | solution.py:149
  69.5 18.5 %collective-permute-start.21 = (bf16[48,2048]{1,0:T(8,128)(2,1)S(1)}, bf16[48,2048]{1,0:T(8,128)(2,1)S(1)}, u32[]{:S(2)}, u32[]{:S(2)}) collective-permute-start(bf16[48,2048]{1,0:T(8,128)(2,1)S(1)} %get-tuple-element.38), channel_id=1, source_target_pairs={{0,4},{1,5},{2,6},{3,7},{4,0},{5,1},{6,2},{7,3},{8,12},{9,13},{10,... | collective-permute-start | bytes 589832 | tf_op jit(solution)/shard_map/ppermute | solution.py:149
  78.7 23.6 %collective-permute-start.23 = (bf16[48,2048]{1,0:T(8,128)(2,1)S(1)}, bf16[48,2048]{1,0:T(8,128)(2,1)S(1)}, u32[]{:S(2)}, u32[]{:S(2)}) collective-permute-start(bf16[48,2048]{1,0:T(8,128)(2,1)S(1)} %get-tuple-element.39), channel_id=1, source_target_pairs={{0,4},{1,5},{2,6},{3,7},{4,0},{5,1},{6,2},{7,3},{8,12},{9,13},{10,... | collective-permute-start | bytes 589832 | tf_op jit(solution)/shard_map/ppermute | solution.py:149
  78.9 11.2 %collective-permute-start.13 = (bf16[48,2048]{1,0:T(8,128)(2,1)S(1)}, bf16[48,2048]{1,0:T(8,128)(2,1)S(1)}, u32[]{:S(2)}, u32[]{:S(2)}) collective-permute-start(bf16[48,2048]{1,0:T(8,128)(2,1)S(1)} %get-tuple-element.33), channel_id=1, source_target_pairs={{0,2},{1,3},{2,0},{3,1},{4,6},{5,7},{6,4},{7,5},{8,10},{9,11},{10,... | collective-permute-start | bytes 589832 | tf_op jit(solution)/shard_map/ppermute | solution.py:149
  87.7 16.3 %collective-permute-start.15 = (bf16[48,2048]{1,0:T(8,128)(2,1)S(1)}, bf16[48,2048]{1,0:T(8,128)(2,1)S(1)}, u32[]{:S(2)}, u32[]{:S(2)}) collective-permute-start(bf16[48,2048]{1,0:T(8,128)(2,1)S(1)} %get-tuple-element.34), channel_id=1, source_target_pairs={{0,2},{1,3},{2,0},{3,1},{4,6},{5,7},{6,4},{7,5},{8,10},{9,11},{10,... | collective-permute-start | bytes 589832 | tf_op jit(solution)/shard_map/ppermute | solution.py:149
  88.0 6.3 %collective-permute-start.6 = (bf16[48,2048]{1,0:T(8,128)(2,1)S(1)}, bf16[48,2048]{1,0:T(8,128)(2,1)S(1)}, u32[]{:S(2)}, u32[]{:S(2)}) collective-permute-start(bf16[48,2048]{1,0:T(8,128)(2,1)S(1)} %get-tuple-element.28), channel_id=1, source_target_pairs={{0,4},{1,5},{2,6},{3,7},{4,0},{5,1},{6,2},{7,3},{8,12},{9,13},{10,... | collective-permute-start | bytes 589832 | tf_op jit(solution)/shard_map/ppermute | solution.py:149
  90.0 18.0 %collective-permute-start.8 = (bf16[48,2048]{1,0:T(8,128)(2,1)S(1)}, bf16[48,2048]{1,0:T(8,128)(2,1)S(1)}, u32[]{:S(2)}, u32[]{:S(2)}) collective-permute-start(bf16[48,2048]{1,0:T(8,128)(2,1)S(1)} %get-tuple-element.29), channel_id=1, source_target_pairs={{0,4},{1,5},{2,6},{3,7},{4,0},{5,1},{6,2},{7,3},{8,12},{9,13},{10,... | collective-permute-start | bytes 589832 | tf_op jit(solution)/shard_map/ppermute | solution.py:149
  94.3 6.3 %collective-permute-start.30 = (bf16[48,2048]{1,0:T(8,128)(2,1)S(1)}, bf16[48,2048]{1,0:T(8,128)(2,1)S(1)}, u32[]{:S(2)}, u32[]{:S(2)}) collective-permute-start(bf16[48,2048]{1,0:T(8,128)(2,1)S(1)} %add_convert_fusion.1), channel_id=1, source_target_pairs={{0,4},{1,5},{2,6},{3,7},{4,0},{5,1},{6,2},{7,3},{8,12},{9,13},{10,... | collective-permute-start | bytes 589832 | tf_op jit(solution)/shard_map/ppermute | solution.py:149
  96.0 7.9 %collective-permute-start.22 = (bf16[48,2048]{1,0:T(8,128)(2,1)S(1)}, bf16[48,2048]{1,0:T(8,128)(2,1)S(1)}, u32[]{:S(2)}, u32[]{:S(2)}) collective-permute-start(bf16[48,2048]{1,0:T(8,128)(2,1)S(1)} %add_convert_fusion.3), channel_id=1, source_target_pairs={{0,2},{1,3},{2,0},{3,1},{4,6},{5,7},{6,4},{7,5},{8,10},{9,11},{10,... | collective-permute-start | bytes 589832 | tf_op jit(solution)/shard_map/ppermute | solution.py:149
  100.6 5.7 %collective-permute-start.14 = (bf16[48,2048]{1,0:T(8,128)(2,1)S(1)}, bf16[48,2048]{1,0:T(8,128)(2,1)S(1)}, u32[]{:S(2)}, u32[]{:S(2)}) collective-permute-start(bf16[48,2048]{1,0:T(8,128)(2,1)S(1)} %add_convert_fusion.5), channel_id=1, source_target_pairs={{0,4},{1,5},{2,6},{3,7},{4,0},{5,1},{6,2},{7,3},{8,12},{9,13},{10,... | collective-permute-start | bytes 589832 | tf_op jit(solution)/shard_map/ppermute | solution.py:149
  102.3 5.7 %collective-permute-start.7 = (bf16[48,2048]{1,0:T(8,128)(2,1)S(1)}, bf16[48,2048]{1,0:T(8,128)(2,1)S(1)}, u32[]{:S(2)}, u32[]{:S(2)}) collective-permute-start(bf16[48,2048]{1,0:T(8,128)(2,1)S(1)} %add_convert_fusion.7), channel_id=1, source_target_pairs={{0,2},{1,3},{2,0},{3,1},{4,6},{5,7},{6,4},{7,5},{8,10},{9,11},{10,... | collective-permute-start | bytes 589832 | tf_op jit(solution)/shard_map/ppermute | solution.py:149
  103.9 7.7 %collective-permute-start.32 = (bf16[48,2048]{1,0:T(8,128)(2,1)S(1)}, bf16[48,2048]{1,0:T(8,128)(2,1)S(1)}, u32[]{:S(2)}, u32[]{:S(2)}) collective-permute-start(bf16[48,2048]{1,0:T(8,128)(2,1)S(1)} %add_convert_fusion), channel_id=1, source_target_pairs={{0,8},{1,9},{2,10},{3,11},{4,12},{5,13},{6,14},{7,15},{8,16},{9,17... | collective-permute-start | bytes 589832 | tf_op jit(solution)/shard_map/ppermute | solution.py:152
  104.0 10.8 %collective-permute-start.24 = (bf16[48,2048]{1,0:T(8,128)(2,1)S(1)}, bf16[48,2048]{1,0:T(8,128)(2,1)S(1)}, u32[]{:S(2)}, u32[]{:S(2)}) collective-permute-start(bf16[48,2048]{1,0:T(8,128)(2,1)S(1)} %add_convert_fusion.2), channel_id=1, source_target_pairs={{0,16},{1,17},{2,18},{3,19},{4,20},{5,21},{6,22},{7,23},{8,24},{9,... | collective-permute-start | bytes 589832 | tf_op jit(solution)/shard_map/ppermute | solution.py:152
  106.3 8.5 %collective-permute-start.16 = (bf16[48,2048]{1,0:T(8,128)(2,1)S(1)}, bf16[48,2048]{1,0:T(8,128)(2,1)S(1)}, u32[]{:S(2)}, u32[]{:S(2)}) collective-permute-start(bf16[48,2048]{1,0:T(8,128)(2,1)S(1)} %add_convert_fusion.4), channel_id=1, source_target_pairs={{0,24},{1,25},{2,26},{3,27},{4,28},{5,29},{6,30},{7,31},{8,0},{9,1... | collective-permute-start | bytes 589832 | tf_op jit(solution)/shard_map/ppermute | solution.py:152
  (13 other events, 100.4 us)

commit v3 on v2

--- a/solution.py
+++ b/solution.py
@@ -10,6 +10,10 @@
 
 def in_vmem(value):
     return pltpu.with_memory_space_constraint(value, pltpu.VMEM)
+
+
+def in_hbm(value):
+    return pltpu.with_memory_space_constraint(value, pltpu.HBM)
 
 
 def dispatch_kernel(cap, experts, plane_ref, ids_ref, tokens_ref, gain_ref, bias_ref, *out_refs):
@@ -48,30 +52,39 @@
         out_specs=[vmem] * experts,
         compiler_params=pltpu.CompilerParams(vmem_limit_bytes=8 << 20),
         name="dispatch",
-    )(plane, ids.T, tokens, gain[None, :], bias[None, :])
+    )(plane, in_hbm(ids.T), in_hbm(tokens), in_hbm(gain[None, :]), in_hbm(bias[None, :]))
 
 
 def combine_kernel(cap, experts, plane_ref, ids_ref, gates_ref, tokens_ref, b_out_ref, *refs):
     row_refs, out_ref = refs[:-1], refs[-1]
-    tok, top = ids_ref.shape
-    lanes = 128
-    named = lax.rem(plane_ref[0] + lax.broadcasted_iota(jnp.int32, (tok, lanes), 1), experts)
-    member = jnp.zeros((tok, lanes), jnp.float32)
-    gate = jnp.zeros((tok, lanes), jnp.float32)
+    top, tok = ids_ref.shape
+    named = lax.rem(plane_ref[0] + lax.broadcasted_iota(jnp.int32, (8, tok), 0), experts)
+    member = jnp.zeros((8, tok), jnp.float32)
+    gate = jnp.zeros((8, tok), jnp.float32)
     for k in range(top):
-        hit = named == ids_ref[:, k : k + 1]
+        hit = named == ids_ref[k : k + 1, :]
         member = jnp.where(hit, 1.0, member)
-        gate = jnp.where(hit, gates_ref[:, k : k + 1], gate)
-    before = lax.broadcasted_iota(jnp.int32, (tok, tok), 1) < lax.broadcasted_iota(jnp.int32, (tok, tok), 0)
+        gate = jnp.where(hit, gates_ref[k : k + 1, :], gate)
+    row, column = (lax.broadcasted_iota(jnp.int32, (tok, tok), axis) for axis in (0, 1))
     rank = jnp.dot(
-        jnp.where(before, 1.0, 0.0).astype(jnp.bfloat16),
         member.astype(jnp.bfloat16),
+        jnp.where(row < column, 1.0, 0.0).astype(jnp.bfloat16),
         preferred_element_type=jnp.float32,
     )
+    rank = jnp.where(member > 0.0, rank, -1.0)
+    turn = jnp.where(row == column, 1.0, 0.0)
+    flip = functools.partial(
+        lax.dot_general,
+        turn,
+        dimension_numbers=(((1,), (1,)), ((), ())),
+        precision=lax.Precision.HIGHEST,
+        preferred_element_type=jnp.float32,
+    )
+    rank, gate = flip(rank), flip(gate)
     slot = lax.broadcasted_iota(jnp.int32, (tok, cap), 1).astype(jnp.float32)
     total = None
     for d in range(experts):
-        pick = jnp.where(slot == rank[:, d : d + 1], member[:, d : d + 1], 0.0).astype(jnp.bfloat16)
+        pick = jnp.where(slot == rank[:, d : d + 1], 1.0, 0.0).astype(jnp.bfloat16)
         rows = jnp.dot(pick, row_refs[d][...], preferred_element_type=jnp.float32)
         bias = b_out_ref[pl.ds(lax.rem(plane_ref[0] + d, experts), 1), :]
         term = gate[:, d : d + 1] * (rows + bias)
@@ -89,7 +102,33 @@
         out_specs=vmem,
         compiler_params=pltpu.CompilerParams(vmem_limit_bytes=8 << 20),
         name="combine",
-    )(plane, ids, gates, in_vmem(tokens), b_out, *[in_vmem(value) for value in rows])
+    )(plane, ids.T, gates.T, in_vmem(tokens), b_out, *[in_vmem(value) for value in rows])
+
+
+def after(value, *earlier):
+    return lax.optimization_barrier((value, *earlier))[0]
+
+
+def stage_kernel(*refs):
+    count = len(refs) // 3
+    sources, targets, sems = refs[:count], refs[count : 2 * count], refs[2 * count :]
+    copies = [pltpu.make_async_copy(*three) for three in zip(sources, targets, sems)]
+    for copy in copies:
+        copy.start()
+    for copy in copies:
+        copy.wait()
+
+
+def stage(*arrays):
+    return pl.pallas_call(
+        stage_kernel,
+        out_shape=[pltpu.VMEM(array.shape, array.dtype) for array in arrays],
+        in_specs=[pl.BlockSpec(memory_space=pl.ANY)] * len(arrays),
+        out_specs=[pl.BlockSpec(memory_space=pltpu.VMEM)] * len(arrays),
+        scratch_shapes=[pltpu.SemaphoreType.DMA] * len(arrays),
+        compiler_params=pltpu.CompilerParams(vmem_limit_bytes=4 << 20),
+        name="stage",
+    )(*[in_hbm(array) for array in arrays])
 
 
 def expert_kernel(tile, *refs):
@@ -152,22 +191,86 @@
         return lax.ppermute(value, "local", [(i, (i + planes * shared) % devices) for i in range(devices)])
 
     w_in, w_out = w_in[0], w_out[0]
-    weights = (w_in, across(w_in, 1), b_in, across(b_in, 1), w_out, across(w_out, 1))
     kinds = (jnp.float32, jnp.float32, jnp.bfloat16, jnp.bfloat16)
+    peer_in, peer_out, peer_bias = across(w_in, 1), across(w_out, 1), across(b_in, 1)
 
     blocks = dispatch(plane, expert_ids, tokens, norm_gain, norm_bias, slot_cap, experts)
-    results = []
-    for d in range(experts):
-        near, far = (2, 4) if d % 2 == 0 else (4, 2)
-        block = blocks[d] if d == 0 else along(blocks[d], d)
-        first = across(block, near)
-        second = across(block, far)
-        third = across(first, far)
-        part = expert_rows([block, first, second, third], weights, kinds)
-        part_first = part[1] + across(part[3], far).astype(jnp.float32)
-        summed = part[0] + across(part_first.astype(jnp.bfloat16), near).astype(jnp.float32)
-        summed = (summed + across(part[2], far).astype(jnp.float32)).astype(jnp.bfloat16)
-        results.append(summed if d == 0 else along(summed, -d))
+    mark = [None]
+
+    def then(*values):
+        if mark[0] is not None:
+            values = lax.optimization_barrier((*values, mark[0]))[:-1]
+        mark[0] = values[0]
+        return values if len(values) > 1 else values[0]
+
+    class Block:
+        def __init__(self, d, near, far):
+            self.d, self.near, self.far = d, near, far
+
+        def spread(self, rows):
+            self.rows = rows
+            self.first, self.second = across(rows, self.near), across(rows, self.far)
+
+        def pass_on(self):
+            self.first = then(self.first)
+            self.third = across(self.first, self.far)
+
+        def compute(self):
+            rows = then(self.rows, self.first, self.second, self.third)
+            self.part = expert_rows(rows, weights, kinds)
+            self.back_third = across(self.part[3], self.far)
+            self.back_second = across(self.part[2], self.far)
+
+        def fold(self):
+            self.back_third = then(self.back_third)
+            both = self.part[1] + self.back_third.astype(jnp.float32)
+            self.back_first = across(both.astype(jnp.bfloat16), self.near)
+
+        def finish(self):
+            first, second = then(self.back_first, self.back_second)
+            summed = self.part[0] + first.astype(jnp.float32) + second.astype(jnp.float32)
+            self.out = summed.astype(jnp.bfloat16)
+            if self.d:
+                self.out = along(self.out, -self.d)
+
+    order = [0] + sorted(range(1, experts), key=lambda d: min(d, experts - d))
+    units = [Block(d, *((2, 4) if i % 2 == 0 else (4, 2))) for i, d in enumerate(order)]
+    own, rest = units[0], units[1:]
+    moved = {}
+    for unit in rest:
+        steps = min(unit.d, experts - unit.d)
+        moved[unit.d] = [along(blocks[unit.d], 1 if unit.d == steps else -1), steps - 1]
+    own.spread(blocks[0])
+    weights = None
+    for turn in range(experts):
+        for unit in rest:
+            if unit.d in moved:
+                value, left = moved[unit.d]
+                value = then(value)
+                if left:
+                    moved[unit.d] = [along(value, 1 if 2 * unit.d <= experts else -1), left - 1]
+                else:
+                    del moved[unit.d]
+                    unit.spread(value)
+                    if unit is rest[0]:
+                        own.pass_on()
+                    else:
+                        rest[rest.index(unit) - 1].pass_on()
+        if turn == 0:
+            w_in, w_out = stage(then(w_in), w_out)
+    peer_in, peer_out = stage(then(peer_in), peer_out)
+    weights = (w_in, peer_in, b_in, peer_bias, w_out, peer_out)
+    rest[0].compute()
+    rest[-1].pass_on()
+    for i, unit in enumerate(rest[1:] + [own]):
+        unit.compute()
+        units[i + 1].fold()
+    for i, unit in enumerate(rest):
+        unit.finish()
+        if i == 0:
+            own.fold()
+    own.finish()
+    results = [next(unit.out for unit in units if unit.d == d) for d in range(experts)]
     return combine(plane, expert_ids, gate_weights, tokens, b_out, results, slot_cap)
 
 

time: 117 us -> 102 us (0.87)
  local copies, waits for them, and re-layouts: 9.64 us -> 0.03 us
  Pallas kernels: 30.4 us -> 23.9 us
  waiting for transfers between devices: 38.4 us -> 42.6 us
  starting transfers between devices: 37.3 us -> 34.9 us
    pallas_call x4, Pallas kernels: 28.4 us -> 13.8 us  [expert_rows(): pl.pallas_call(functools.partial(expert_kernel, 512), out_shape=[pltpu.VM...]
    unnamed x26 -> x10, local copies, waits for them, and re-layouts: 9.64 us -> 0.03 us
    pallas_call x0 -> x2, Pallas kernels: none -> 6.97 us  [stage(): pl.pallas_call(stage_kernel, out_shape=[pltpu.VMEM(array.shape, array.dty...]
    ppermute x6 -> x7, waiting for transfers between devices: 17.6 us -> 22.6 us  [along(): lax.ppermute(value, 'local', [(i, (i + planes * shared) % devices) for i...]
    ppermute x27, starting transfers between devices: 29.5 us -> 26 us  [across(): return lax.ppermute(value, 'local', [(i, i ^ bit) for i in range(devices)])]
    ppermute x6 -> x7, starting transfers between devices: 7.82 us -> 8.91 us  [along(): lax.ppermute(value, 'local', [(i, (i + planes * shared) % devices) for i...]
  transfers between devices with their start and end apart: 33 -> 34, of which waited for: 12 -> 16; matrix products, arithmetic and copies ran while one was open for 2% -> 0% of each run, Pallas kernels for 25% -> 22%
where the time goes in v3:
time: 102 us
  waiting for transfers between devices  42.6 us (42%)
  starting transfers between devices  34.9 us (34%)
  Pallas kernels  23.9 us (23%)
    ppermute x27, starting transfers between devices, across(): return lax.ppermute(value, 'local', [(i, i ^ bit) for i in range(devices)])  26 us
    ppermute x7, waiting for transfers between devices, along(): lax.ppermute(value, 'local', [(i, (i + planes * shared) % devices) for i...  22.6 us
    ppermute x27, waiting for transfers between devices, across(): return lax.ppermute(value, 'local', [(i, i ^ bit) for i in range(devices)])  19.9 us
    pallas_call x4, Pallas kernels, expert_rows(): pl.pallas_call(functools.partial(expert_kernel, 512), out_shape=[pltpu.VM...  13.8 us
    ppermute x7, starting transfers between devices, along(): lax.ppermute(value, 'local', [(i, (i + planes * shared) % devices) for i...  8.91 us
    pallas_call x2, Pallas kernels, stage(): pl.pallas_call(stage_kernel, out_shape=[pltpu.VMEM(array.shape, array.dty...  6.97 us
  transfers between devices with their start and end apart: 34, of which 16 were waited for; matrix products, arithmetic and copies ran while one was open for 0% of the time, Pallas kernels for 22%

profile of v3, /device:TPU:0, one launch (start us, length us, event | category | flops | bytes accessed | tf_op | source)
XLA Modules:
  0.0 102.0 jit_solution(2921529296333033827)
XLA Ops:
  0.5 1.6 %dispatch.1 = (bf16[48,2048]{1,0:T(8,128)(2,1)S(1)}, bf16[48,2048]{1,0:T(8,128)(2,1)S(1)}, bf16[48,2048]{1,0:T(8,128)(2,1)S(1)}, bf16[48,2048]{1,0:T(8,128)(2,1)S(1)}) custom-call(s32[1]{0:T(128)} %bitcast.plane_ref, s32[2,64]{1,0:T(2,128)} %bitcast.7, bf16[64,2048]{1,0:T(8,128)(2,1)} %tokens_ref.3, f32[1,2048]{1,0:T(1,128)} %bitcast.14, f32[1,2048]{1,0:T(1,128)} %bitcast.15), custom_call_target="tpu_custom_call" | custom-call | tf_op jit(solution)/shard_map/dispatch/pallas_call | solution.py:48
  2.1 3.1 %collective-permute-start.1 = (bf16[48,2048]{1,0:T(8,128)(2,1)S(1)}, bf16[48,2048]{1,0:T(8,128)(2,1)S(1)}, u32[]{:S(2)}, u32[]{:S(2)}) collective-permute-start(bf16[48,2048]{1,0:T(8,128)(2,1)S(1)} %get-tuple-element.67), channel_id=1, source_target_pairs={{0,8},{1,9},{2,10},{3,11},{4,12},{5,13},{6,14},{7,15},{8,16},{9,17... | collective-permute-start | bytes 589832 | tf_op jit(solution)/shard_map/ppermute | solution.py:191
  5.2 1.5 %collective-permute-start = (bf16[48,2048]{1,0:T(8,128)(2,1)S(1)}, bf16[48,2048]{1,0:T(8,128)(2,1)S(1)}, u32[]{:S(2)}, u32[]{:S(2)}) collective-permute-start(bf16[48,2048]{1,0:T(8,128)(2,1)S(1)} %get-tuple-element.96.refs_0_), channel_id=1, source_target_pairs={{0,2},{1,3},{2,0},{3,1},{4,6},{5,7},{6,4},{7,5},{8,10},{9,11},{10,... | collective-permute-start | bytes 589832 | tf_op jit(solution)/shard_map/ppermute | solution.py:188
  6.7 2.2 %collective-permute-start.4 = (bf16[48,2048]{1,0:T(8,128)(2,1)S(1)}, bf16[48,2048]{1,0:T(8,128)(2,1)S(1)}, u32[]{:S(2)}, u32[]{:S(2)}) collective-permute-start(bf16[48,2048]{1,0:T(8,128)(2,1)S(1)} %get-tuple-element.69), channel_id=1, source_target_pairs={{0,24},{1,25},{2,26},{3,27},{4,28},{5,29},{6,30},{7,31},{8,0},{9,1... | collective-permute-start | bytes 589832 | tf_op jit(solution)/shard_map/ppermute | solution.py:191
  8.9 4.0 %collective-permute-done.1.refs_0_ = bf16[48,2048]{1,0:T(8,128)(2,1)S(1)} collective-permute-done((bf16[48,2048]{1,0:T(8,128)(2,1)S(1)}, bf16[48,2048]{1,0:T(8,128)(2,1)S(1)}, u32[]{:S(2)}, u32[]{:S(2)}) %collective-permute-start.1) | collective-permute-done | bytes 196640 | tf_op jit(solution)/shard_map/ppermute | solution.py:191
  12.9 1.7 %collective-permute-start.7 = (bf16[48,2048]{1,0:T(8,128)(2,1)S(1)}, bf16[48,2048]{1,0:T(8,128)(2,1)S(1)}, u32[]{:S(2)}, u32[]{:S(2)}) collective-permute-start(bf16[48,2048]{1,0:T(8,128)(2,1)S(1)} %collective-permute-done.1.refs_0_), channel_id=1, source_target_pairs={{0,4},{1,5},{2,6},{3,7},{4,0},{5,1},{6,2},{7,3},{8,12},{9,13},{10,... | collective-permute-start | bytes 589832 | tf_op jit(solution)/shard_map/ppermute | solution.py:188
  14.7 1.8 %collective-permute-done.4.refs_0_ = bf16[48,2048]{1,0:T(8,128)(2,1)S(1)} collective-permute-done((bf16[48,2048]{1,0:T(8,128)(2,1)S(1)}, bf16[48,2048]{1,0:T(8,128)(2,1)S(1)}, u32[]{:S(2)}, u32[]{:S(2)}) %collective-permute-start.4) | collective-permute-done | bytes 196640 | tf_op jit(solution)/shard_map/ppermute | solution.py:191
  16.5 2.1 %collective-permute-done.7.refs_1_ = bf16[48,2048]{1,0:T(8,128)(2,1)S(1)} collective-permute-done((bf16[48,2048]{1,0:T(8,128)(2,1)S(1)}, bf16[48,2048]{1,0:T(8,128)(2,1)S(1)}, u32[]{:S(2)}, u32[]{:S(2)}) %collective-permute-start.7) | collective-permute-done | bytes 196640 | tf_op jit(solution)/shard_map/ppermute | solution.py:188
  18.6 4.1 %collective-permute-done.6 = bf16[48,2048]{1,0:T(8,128)(2,1)S(1)} collective-permute-done((bf16[48,2048]{1,0:T(8,128)(2,1)S(1)}, bf16[48,2048]{1,0:T(8,128)(2,1)S(1)}, u32[]{:S(2)}, u32[]{:S(2)}) %collective-permute-start.6) | collective-permute-done | bytes 196640 | tf_op jit(solution)/shard_map/ppermute | solution.py:191
  23.6 1.2 %collective-permute-start.5 = (bf16[48,2048]{1,0:T(8,128)(2,1)S(1)}, bf16[48,2048]{1,0:T(8,128)(2,1)S(1)}, u32[]{:S(2)}, u32[]{:S(2)}) collective-permute-start(bf16[48,2048]{1,0:T(8,128)(2,1)S(1)} %collective-permute-done.4.refs_0_), channel_id=1, source_target_pairs={{0,2},{1,3},{2,0},{3,1},{4,6},{5,7},{6,4},{7,5},{8,10},{9,11},{10,... | collective-permute-start | bytes 589832 | tf_op jit(solution)/shard_map/ppermute | solution.py:188
  25.6 4.8 %collective-permute-done.8.refs_0_ = bf16[48,2048]{1,0:T(8,128)(2,1)S(1)} collective-permute-done((bf16[48,2048]{1,0:T(8,128)(2,1)S(1)}, bf16[48,2048]{1,0:T(8,128)(2,1)S(1)}, u32[]{:S(2)}, u32[]{:S(2)}) %collective-permute-start.8) | collective-permute-done | bytes 196640 | tf_op jit(solution)/shard_map/ppermute | solution.py:191
  30.4 1.2 %collective-permute-start.13 = (bf16[48,2048]{1,0:T(8,128)(2,1)S(1)}, bf16[48,2048]{1,0:T(8,128)(2,1)S(1)}, u32[]{:S(2)}, u32[]{:S(2)}) collective-permute-start(bf16[48,2048]{1,0:T(8,128)(2,1)S(1)} %collective-permute-done.7.refs_1_), channel_id=1, source_target_pairs={{0,2},{1,3},{2,0},{3,1},{4,6},{5,7},{6,4},{7,5},{8,10},{9,11},{10,... | collective-permute-start | bytes 589832 | tf_op jit(solution)/shard_map/ppermute | solution.py:188
  34.1 2.0 %collective-permute-done.13.refs_3_ = bf16[48,2048]{1,0:T(8,128)(2,1)S(1)} collective-permute-done((bf16[48,2048]{1,0:T(8,128)(2,1)S(1)}, bf16[48,2048]{1,0:T(8,128)(2,1)S(1)}, u32[]{:S(2)}, u32[]{:S(2)}) %collective-permute-start.13) | collective-permute-done | bytes 196640 | tf_op jit(solution)/shard_map/ppermute | solution.py:188
  36.7 3.5 %stage.2 = (bf16[2048,1024]{1,0:T(8,128)(2,1)S(1)}, bf16[1024,2048]{1,0:T(8,128)(2,1)S(1)}) custom-call(bf16[2048,1024]{1,0:T(8,128)(2,1)} %bitcast.11, bf16[1024,2048]{1,0:T(8,128)(2,1)} %bitcast.13), custom_call_target="tpu_custom_call" | custom-call | tf_op jit(solution)/shard_map/stage/pallas_call | solution.py:123
  40.2 1.5 %collective-permute-start.2 = (bf16[48,2048]{1,0:T(8,128)(2,1)S(1)}, bf16[48,2048]{1,0:T(8,128)(2,1)S(1)}, u32[]{:S(2)}, u32[]{:S(2)}) collective-permute-start(bf16[48,2048]{1,0:T(8,128)(2,1)S(1)} %get-tuple-element.96.refs_0_), channel_id=1, source_target_pairs={{0,4},{1,5},{2,6},{3,7},{4,0},{5,1},{6,2},{7,3},{8,12},{9,13},{10,... | collective-permute-start | bytes 589832 | tf_op jit(solution)/shard_map/ppermute | solution.py:188
  45.3 3.5 %stage.3 = (bf16[2048,1024]{1,0:T(8,128)(2,1)S(1)}, bf16[1024,2048]{1,0:T(8,128)(2,1)S(1)}) custom-call(bf16[2048,1024]{1,0:T(8,128)(2,1)} %collective-permute-done.14.refs_0_, bf16[1024,2048]{1,0:T(8,128)(2,1)} %collective-permute-done.15.refs_1_), custom_call_target="tpu_custom_call" | custom-call | tf_op jit(solution)/shard_map/stage/pallas_call | solution.py:123
  48.8 3.5 %expert.5 = (f32[48,2048]{1,0:T(8,128)S(1)}, f32[48,2048]{1,0:T(8,128)S(1)}, bf16[48,2048]{1,0:T(8,128)(2,1)S(1)}, bf16[48,2048]{1,0:T(8,128)(2,1)S(1)}) custom-call(bf16[48,2048]{1,0:T(8,128)(2,1)S(1)} %collective-permute-done.1.refs_0_, bf16[48,2048]{1,0:T(8,128)(2,1)S(1)} %collective-permute-done.7.refs_1_, ...), custom_call_target="tpu_custom_call" | custom-call | flops 3221225472 | bytes 16777216 | tf_op jit(solution)/shard_map/expert/pallas_call | solution.py:160
  53.5 3.5 %expert.4 = (f32[48,2048]{1,0:T(8,128)S(1)}, f32[48,2048]{1,0:T(8,128)S(1)}, bf16[48,2048]{1,0:T(8,128)(2,1)S(1)}, bf16[48,2048]{1,0:T(8,128)(2,1)S(1)}) custom-call(bf16[48,2048]{1,0:T(8,128)(2,1)S(1)} %collective-permute-done.4.refs_0_, bf16[48,2048]{1,0:T(8,128)(2,1)S(1)} %collective-permute-done.5.refs_1_, ...), custom_call_target="tpu_custom_call" | custom-call | flops 3221225472 | bytes 16777216 | tf_op jit(solution)/shard_map/expert/pallas_call | solution.py:160
  59.1 1.3 %collective-permute-start.23 = (bf16[48,2048]{1,0:T(8,128)(2,1)S(1)}, bf16[48,2048]{1,0:T(8,128)(2,1)S(1)}, u32[]{:S(2)}, u32[]{:S(2)}) collective-permute-start(bf16[48,2048]{1,0:T(8,128)(2,1)S(1)} %get-tuple-element.104), channel_id=1, source_target_pairs={{0,2},{1,3},{2,0},{3,1},{4,6},{5,7},{6,4},{7,5},{8,10},{9,11},{10,... | collective-permute-start | bytes 589832 | tf_op jit(solution)/shard_map/ppermute | solution.py:188
  61.3 4.4 %collective-permute-done.17 = bf16[48,2048]{1,0:T(8,128)(2,1)S(1)} collective-permute-done((bf16[48,2048]{1,0:T(8,128)(2,1)S(1)}, bf16[48,2048]{1,0:T(8,128)(2,1)S(1)}, u32[]{:S(2)}, u32[]{:S(2)}) %collective-permute-start.17) | collective-permute-done | bytes 196640 | tf_op jit(solution)/shard_map/ppermute | solution.py:188
  66.9 3.5 %expert.7 = (f32[48,2048]{1,0:T(8,128)S(1)}, f32[48,2048]{1,0:T(8,128)S(1)}, bf16[48,2048]{1,0:T(8,128)(2,1)S(1)}, bf16[48,2048]{1,0:T(8,128)(2,1)S(1)}) custom-call(bf16[48,2048]{1,0:T(8,128)(2,1)S(1)} %collective-permute-done.8.refs_0_, bf16[48,2048]{1,0:T(8,128)(2,1)S(1)} %collective-permute-done.11.refs_1_, ...), custom_call_target="tpu_custom_call" | custom-call | flops 3221225472 | bytes 16777216 | tf_op jit(solution)/shard_map/expert/pallas_call | solution.py:160
  70.4 1.3 %collective-permute-start.24 = (bf16[48,2048]{1,0:T(8,128)(2,1)S(1)}, bf16[48,2048]{1,0:T(8,128)(2,1)S(1)}, u32[]{:S(2)}, u32[]{:S(2)}) collective-permute-start(bf16[48,2048]{1,0:T(8,128)(2,1)S(1)} %get-tuple-element.108), channel_id=1, source_target_pairs={{0,2},{1,3},{2,0},{3,1},{4,6},{5,7},{6,4},{7,5},{8,10},{9,11},{10,... | collective-permute-start | bytes 589832 | tf_op jit(solution)/shard_map/ppermute | solution.py:188
  72.5 3.5 %expert.6 = (f32[48,2048]{1,0:T(8,128)S(1)}, f32[48,2048]{1,0:T(8,128)S(1)}, bf16[48,2048]{1,0:T(8,128)(2,1)S(1)}, bf16[48,2048]{1,0:T(8,128)(2,1)S(1)}) custom-call(bf16[48,2048]{1,0:T(8,128)(2,1)S(1)} %get-tuple-element.96.refs_0_, bf16[48,2048]{1,0:T(8,128)(2,1)S(1)} %collective-permute-done.refs_1_, bf16[48,2048]{1,0:T(8,128)(2,1)S(1)} %collective-permute-done.2.refs_2_, ...), custom_call_target="tpu_custom_call" | custom-call | flops 3221225472 | bytes 16777216 | tf_op jit(solution)/shard_map/expert/pallas_call | solution.py:160
  76.0 2.2 %collective-permute-done.24 = bf16[48,2048]{1,0:T(8,128)(2,1)S(1)} collective-permute-done((bf16[48,2048]{1,0:T(8,128)(2,1)S(1)}, bf16[48,2048]{1,0:T(8,128)(2,1)S(1)}, u32[]{:S(2)}, u32[]{:S(2)}) %collective-permute-start.24) | collective-permute-done | bytes 196640 | tf_op jit(solution)/shard_map/ppermute | solution.py:188
  78.7 1.5 %collective-permute-start.26 = (bf16[48,2048]{1,0:T(8,128)(2,1)S(1)}, bf16[48,2048]{1,0:T(8,128)(2,1)S(1)}, u32[]{:S(2)}, u32[]{:S(2)}) collective-permute-start(bf16[48,2048]{1,0:T(8,128)(2,1)S(1)} %get-tuple-element.112), channel_id=1, source_target_pairs={{0,4},{1,5},{2,6},{3,7},{4,0},{5,1},{6,2},{7,3},{8,12},{9,13},{10,... | collective-permute-start | bytes 589832 | tf_op jit(solution)/shard_map/ppermute | solution.py:188
  81.3 2.6 %collective-permute-done.21 = bf16[48,2048]{1,0:T(8,128)(2,1)S(1)} collective-permute-done((bf16[48,2048]{1,0:T(8,128)(2,1)S(1)}, bf16[48,2048]{1,0:T(8,128)(2,1)S(1)}, u32[]{:S(2)}, u32[]{:S(2)}) %collective-permute-start.21) | collective-permute-done | bytes 196640 | tf_op jit(solution)/shard_map/ppermute | solution.py:188
  83.8 1.7 %collective-permute-start.31 = (bf16[48,2048]{1,0:T(8,128)(2,1)S(1)}, bf16[48,2048]{1,0:T(8,128)(2,1)S(1)}, u32[]{:S(2)}, u32[]{:S(2)}) collective-permute-start(bf16[48,2048]{1,0:T(8,128)(2,1)S(1)} %add_convert_fusion.2), channel_id=1, source_target_pairs={{0,24},{1,25},{2,26},{3,27},{4,28},{5,29},{6,30},{7,31},{8,0},{9,1... | collective-permute-start | bytes 589832 | tf_op jit(solution)/shard_map/ppermute | solution.py:191
  86.1 1.6 %collective-permute-start.25 = (bf16[48,2048]{1,0:T(8,128)(2,1)S(1)}, bf16[48,2048]{1,0:T(8,128)(2,1)S(1)}, u32[]{:S(2)}, u32[]{:S(2)}) collective-permute-start(bf16[48,2048]{1,0:T(8,128)(2,1)S(1)} %add_convert_fusion.6), channel_id=1, source_target_pairs={{0,2},{1,3},{2,0},{3,1},{4,6},{5,7},{6,4},{7,5},{8,10},{9,11},{10,... | collective-permute-start | bytes 589832 | tf_op jit(solution)/shard_map/ppermute | solution.py:188
  88.2 3.1 %collective-permute-done.27 = bf16[48,2048]{1,0:T(8,128)(2,1)S(1)} collective-permute-done((bf16[48,2048]{1,0:T(8,128)(2,1)S(1)}, bf16[48,2048]{1,0:T(8,128)(2,1)S(1)}, u32[]{:S(2)}, u32[]{:S(2)}) %collective-permute-start.27) | collective-permute-done | bytes 196640 | tf_op jit(solution)/shard_map/ppermute | solution.py:188
  92.6 2.8 %collective-permute-done.33.refs_3_ = bf16[48,2048]{1,0:T(8,128)(2,1)S(1)} collective-permute-done((bf16[48,2048]{1,0:T(8,128)(2,1)S(1)}, bf16[48,2048]{1,0:T(8,128)(2,1)S(1)}, u32[]{:S(2)}, u32[]{:S(2)}) %collective-permute-start.33) | collective-permute-done | bytes 196640 | tf_op jit(solution)/shard_map/ppermute | solution.py:191
  95.4 5.1 %collective-permute-done.32.refs_2_ = bf16[48,2048]{1,0:T(8,128)(2,1)S(1)} collective-permute-done((bf16[48,2048]{1,0:T(8,128)(2,1)S(1)}, bf16[48,2048]{1,0:T(8,128)(2,1)S(1)}, u32[]{:S(2)}, u32[]{:S(2)}) %collective-permute-start.32) | collective-permute-done | bytes 196640 | tf_op jit(solution)/shard_map/ppermute | solution.py:191
  100.5 1.5 %combine.1 = bf16[64,2048]{1,0:T(8,128)(2,1)} custom-call(s32[1]{0:T(128)} %bitcast.plane_ref, s32[2,64]{1,0:T(2,128)S(1)} %bitcast.8, f32[2,64]{1,0:T(2,128)S(1)} %bitcast.9, bf16[64,2048]{1,0:T(8,128)(2,1)S(1)} %copy-done, f32[4,2048]{1,0:T(4,128)S(1)} %copy-done.2, bf16[48,2048]{1,0:T(8,128)(2,1)S(1)} %add_convert_fusion.3.refs_0_, ...), custom_call_target="tpu_custom_call" | custom-call | tf_op jit(solution)/shard_map/combine/pallas_call | solution.py:98
  (62 shorter events, 18.9 us)
Async XLA Ops:
  0.0 36.7 %collective-permute-start.14 = (bf16[2048,1024]{1,0:T(8,128)(2,1)}, bf16[2048,1024]{1,0:T(8,128)(2,1)}, u32[]{:S(2)}, u32[]{:S(2)}) collective-permute-start(bf16[2048,1024]{1,0:T(8,128)(2,1)} %bitcast.10), channel_id=1, source_target_pairs={{0,1},{1,0},{2,3},{3,2},{4,5},{5,4},{6,7},{7,6},{8,9},{9,8},{10,11... | collective-permute-start | bytes 12582920 | tf_op jit(solution)/shard_map/ppermute | solution.py:188
  0.5 44.0 %collective-permute-start.15 = (bf16[1024,2048]{1,0:T(8,128)(2,1)}, bf16[1024,2048]{1,0:T(8,128)(2,1)}, u32[]{:S(2)}, u32[]{:S(2)}) collective-permute-start(bf16[1024,2048]{1,0:T(8,128)(2,1)} %bitcast.12), channel_id=1, source_target_pairs={{0,1},{1,0},{2,3},{3,2},{4,5},{5,4},{6,7},{7,6},{8,9},{9,8},{10,11... | collective-permute-start | bytes 12582920 | tf_op jit(solution)/shard_map/ppermute | solution.py:188
  2.1 10.9 %collective-permute-start.1 = (bf16[48,2048]{1,0:T(8,128)(2,1)S(1)}, bf16[48,2048]{1,0:T(8,128)(2,1)S(1)}, u32[]{:S(2)}, u32[]{:S(2)}) collective-permute-start(bf16[48,2048]{1,0:T(8,128)(2,1)S(1)} %get-tuple-element.67), channel_id=1, source_target_pairs={{0,8},{1,9},{2,10},{3,11},{4,12},{5,13},{6,14},{7,15},{8,16},{9,17... | collective-permute-start | bytes 589832 | tf_op jit(solution)/shard_map/ppermute | solution.py:191
  5.2 9.5 %collective-permute-start = (bf16[48,2048]{1,0:T(8,128)(2,1)S(1)}, bf16[48,2048]{1,0:T(8,128)(2,1)S(1)}, u32[]{:S(2)}, u32[]{:S(2)}) collective-permute-start(bf16[48,2048]{1,0:T(8,128)(2,1)S(1)} %get-tuple-element.96.refs_0_), channel_id=1, source_target_pairs={{0,2},{1,3},{2,0},{3,1},{4,6},{5,7},{6,4},{7,5},{8,10},{9,11},{10,... | collective-permute-start | bytes 589832 | tf_op jit(solution)/shard_map/ppermute | solution.py:188
  6.7 9.8 %collective-permute-start.4 = (bf16[48,2048]{1,0:T(8,128)(2,1)S(1)}, bf16[48,2048]{1,0:T(8,128)(2,1)S(1)}, u32[]{:S(2)}, u32[]{:S(2)}) collective-permute-start(bf16[48,2048]{1,0:T(8,128)(2,1)S(1)} %get-tuple-element.69), channel_id=1, source_target_pairs={{0,24},{1,25},{2,26},{3,27},{4,28},{5,29},{6,30},{7,31},{8,0},{9,1... | collective-permute-start | bytes 589832 | tf_op jit(solution)/shard_map/ppermute | solution.py:191
  12.9 5.7 %collective-permute-start.7 = (bf16[48,2048]{1,0:T(8,128)(2,1)S(1)}, bf16[48,2048]{1,0:T(8,128)(2,1)S(1)}, u32[]{:S(2)}, u32[]{:S(2)}) collective-permute-start(bf16[48,2048]{1,0:T(8,128)(2,1)S(1)} %collective-permute-done.1.refs_0_), channel_id=1, source_target_pairs={{0,4},{1,5},{2,6},{3,7},{4,0},{5,1},{6,2},{7,3},{8,12},{9,13},{10,... | collective-permute-start | bytes 589832 | tf_op jit(solution)/shard_map/ppermute | solution.py:188
  14.7 8.0 %collective-permute-start.6 = (bf16[48,2048]{1,0:T(8,128)(2,1)S(1)}, bf16[48,2048]{1,0:T(8,128)(2,1)S(1)}, u32[]{:S(2)}, u32[]{:S(2)}) collective-permute-start(bf16[48,2048]{1,0:T(8,128)(2,1)S(1)} %get-tuple-element.71), channel_id=1, source_target_pairs={{0,8},{1,9},{2,10},{3,11},{4,12},{5,13},{6,14},{7,15},{8,16},{9,17... | collective-permute-start | bytes 589832 | tf_op jit(solution)/shard_map/ppermute | solution.py:191
  22.7 7.7 %collective-permute-start.8 = (bf16[48,2048]{1,0:T(8,128)(2,1)S(1)}, bf16[48,2048]{1,0:T(8,128)(2,1)S(1)}, u32[]{:S(2)}, u32[]{:S(2)}) collective-permute-start(bf16[48,2048]{1,0:T(8,128)(2,1)S(1)} %collective-permute-done.6), channel_id=1, source_target_pairs={{0,8},{1,9},{2,10},{3,11},{4,12},{5,13},{6,14},{7,15},{8,16},{9,17... | collective-permute-start | bytes 589832 | tf_op jit(solution)/shard_map/ppermute | solution.py:191
  23.6 8.1 %collective-permute-start.5 = (bf16[48,2048]{1,0:T(8,128)(2,1)S(1)}, bf16[48,2048]{1,0:T(8,128)(2,1)S(1)}, u32[]{:S(2)}, u32[]{:S(2)}) collective-permute-start(bf16[48,2048]{1,0:T(8,128)(2,1)S(1)} %collective-permute-done.4.refs_0_), channel_id=1, source_target_pairs={{0,2},{1,3},{2,0},{3,1},{4,6},{5,7},{6,4},{7,5},{8,10},{9,11},{10,... | collective-permute-start | bytes 589832 | tf_op jit(solution)/shard_map/ppermute | solution.py:188
  24.8 8.7 %collective-permute-start.12 = (bf16[48,2048]{1,0:T(8,128)(2,1)S(1)}, bf16[48,2048]{1,0:T(8,128)(2,1)S(1)}, u32[]{:S(2)}, u32[]{:S(2)}) collective-permute-start(bf16[48,2048]{1,0:T(8,128)(2,1)S(1)} %collective-permute-done.1.refs_0_), channel_id=1, source_target_pairs={{0,2},{1,3},{2,0},{3,1},{4,6},{5,7},{6,4},{7,5},{8,10},{9,11},{10,... | collective-permute-start | bytes 589832 | tf_op jit(solution)/shard_map/ppermute | solution.py:188
  31.7 8.5 %collective-permute-start.11 = (bf16[48,2048]{1,0:T(8,128)(2,1)S(1)}, bf16[48,2048]{1,0:T(8,128)(2,1)S(1)}, u32[]{:S(2)}, u32[]{:S(2)}) collective-permute-start(bf16[48,2048]{1,0:T(8,128)(2,1)S(1)} %collective-permute-done.8.refs_0_), channel_id=1, source_target_pairs={{0,4},{1,5},{2,6},{3,7},{4,0},{5,1},{6,2},{7,3},{8,12},{9,13},{10,... | collective-permute-start | bytes 589832 | tf_op jit(solution)/shard_map/ppermute | solution.py:188
  33.5 8.2 %collective-permute-start.9 = (bf16[48,2048]{1,0:T(8,128)(2,1)S(1)}, bf16[48,2048]{1,0:T(8,128)(2,1)S(1)}, u32[]{:S(2)}, u32[]{:S(2)}) collective-permute-start(bf16[48,2048]{1,0:T(8,128)(2,1)S(1)} %collective-permute-done.4.refs_0_), channel_id=1, source_target_pairs={{0,4},{1,5},{2,6},{3,7},{4,0},{5,1},{6,2},{7,3},{8,12},{9,13},{10,... | collective-permute-start | bytes 589832 | tf_op jit(solution)/shard_map/ppermute | solution.py:188
  36.1 7.2 %collective-permute-start.10 = (bf16[48,2048]{1,0:T(8,128)(2,1)S(1)}, bf16[48,2048]{1,0:T(8,128)(2,1)S(1)}, u32[]{:S(2)}, u32[]{:S(2)}) collective-permute-start(bf16[48,2048]{1,0:T(8,128)(2,1)S(1)} %collective-permute-done.5.refs_1_), channel_id=1, source_target_pairs={{0,4},{1,5},{2,6},{3,7},{4,0},{5,1},{6,2},{7,3},{8,12},{9,13},{10,... | collective-permute-start | bytes 589832 | tf_op jit(solution)/shard_map/ppermute | solution.py:188
  36.7 12.1 %collective-permute-start.16 = (f32[1,1024]{1,0:T(1,128)}, f32[1,1024]{1,0:T(1,128)S(1)}, u32[]{:S(2)}, u32[]{:S(2)}) collective-permute-start(f32[1,1024]{1,0:T(1,128)} %refs_6_.7), channel_id=1, source_target_pairs={{0,1},{1,0},{2,3},{3,2},{4,5},{5,4},{6,7},{7,6},{8,9},{9,8},{10,11... | collective-permute-start | bytes 12296 | tf_op jit(solution)/shard_map/ppermute | solution.py:188
  40.2 30.2 %collective-permute-start.2 = (bf16[48,2048]{1,0:T(8,128)(2,1)S(1)}, bf16[48,2048]{1,0:T(8,128)(2,1)S(1)}, u32[]{:S(2)}, u32[]{:S(2)}) collective-permute-start(bf16[48,2048]{1,0:T(8,128)(2,1)S(1)} %get-tuple-element.96.refs_0_), channel_id=1, source_target_pairs={{0,4},{1,5},{2,6},{3,7},{4,0},{5,1},{6,2},{7,3},{8,12},{9,13},{10,... | collective-permute-start | bytes 589832 | tf_op jit(solution)/shard_map/ppermute | solution.py:188
  41.7 30.0 %collective-permute-start.3 = (bf16[48,2048]{1,0:T(8,128)(2,1)S(1)}, bf16[48,2048]{1,0:T(8,128)(2,1)S(1)}, u32[]{:S(2)}, u32[]{:S(2)}) collective-permute-start(bf16[48,2048]{1,0:T(8,128)(2,1)S(1)} %collective-permute-done.refs_1_), channel_id=1, source_target_pairs={{0,4},{1,5},{2,6},{3,7},{4,0},{5,1},{6,2},{7,3},{8,12},{9,13},{10,... | collective-permute-start | bytes 589832 | tf_op jit(solution)/shard_map/ppermute | solution.py:188
  43.3 15.8 %collective-permute-start.18 = (bf16[48,2048]{1,0:T(8,128)(2,1)S(1)}, bf16[48,2048]{1,0:T(8,128)(2,1)S(1)}, u32[]{:S(2)}, u32[]{:S(2)}) collective-permute-start(bf16[48,2048]{1,0:T(8,128)(2,1)S(1)} %collective-permute-done.8.refs_0_), channel_id=1, source_target_pairs={{0,2},{1,3},{2,0},{3,1},{4,6},{5,7},{6,4},{7,5},{8,10},{9,11},{10,... | collective-permute-start | bytes 589832 | tf_op jit(solution)/shard_map/ppermute | solution.py:188
  44.4 15.9 %collective-permute-start.19 = (bf16[48,2048]{1,0:T(8,128)(2,1)S(1)}, bf16[48,2048]{1,0:T(8,128)(2,1)S(1)}, u32[]{:S(2)}, u32[]{:S(2)}) collective-permute-start(bf16[48,2048]{1,0:T(8,128)(2,1)S(1)} %collective-permute-done.11.refs_1_), channel_id=1, source_target_pairs={{0,2},{1,3},{2,0},{3,1},{4,6},{5,7},{6,4},{7,5},{8,10},{9,11},{10,... | collective-permute-start | bytes 589832 | tf_op jit(solution)/shard_map/ppermute | solution.py:188
  52.3 5.7 %collective-permute-start.20 = (bf16[48,2048]{1,0:T(8,128)(2,1)S(1)}, bf16[48,2048]{1,0:T(8,128)(2,1)S(1)}, u32[]{:S(2)}, u32[]{:S(2)}) collective-permute-start(bf16[48,2048]{1,0:T(8,128)(2,1)S(1)} %get-tuple-element.92), channel_id=1, source_target_pairs={{0,2},{1,3},{2,0},{3,1},{4,6},{5,7},{6,4},{7,5},{8,10},{9,11},{10,... | collective-permute-start | bytes 589832 | tf_op jit(solution)/shard_map/ppermute | solution.py:188
  58.0 7.7 %collective-permute-start.17 = (bf16[48,2048]{1,0:T(8,128)(2,1)S(1)}, bf16[48,2048]{1,0:T(8,128)(2,1)S(1)}, u32[]{:S(2)}, u32[]{:S(2)}) collective-permute-start(bf16[48,2048]{1,0:T(8,128)(2,1)S(1)} %get-tuple-element.88), channel_id=1, source_target_pairs={{0,4},{1,5},{2,6},{3,7},{4,0},{5,1},{6,2},{7,3},{8,12},{9,13},{10,... | collective-permute-start | bytes 589832 | tf_op jit(solution)/shard_map/ppermute | solution.py:188
  59.1 19.6 %collective-permute-start.23 = (bf16[48,2048]{1,0:T(8,128)(2,1)S(1)}, bf16[48,2048]{1,0:T(8,128)(2,1)S(1)}, u32[]{:S(2)}, u32[]{:S(2)}) collective-permute-start(bf16[48,2048]{1,0:T(8,128)(2,1)S(1)} %get-tuple-element.104), channel_id=1, source_target_pairs={{0,2},{1,3},{2,0},{3,1},{4,6},{5,7},{6,4},{7,5},{8,10},{9,11},{10,... | collective-permute-start | bytes 589832 | tf_op jit(solution)/shard_map/ppermute | solution.py:188
  60.4 25.2 %collective-permute-start.30 = (bf16[48,2048]{1,0:T(8,128)(2,1)S(1)}, bf16[48,2048]{1,0:T(8,128)(2,1)S(1)}, u32[]{:S(2)}, u32[]{:S(2)}) collective-permute-start(bf16[48,2048]{1,0:T(8,128)(2,1)S(1)} %get-tuple-element.116), channel_id=1, source_target_pairs={{0,4},{1,5},{2,6},{3,7},{4,0},{5,1},{6,2},{7,3},{8,12},{9,13},{10,... | collective-permute-start | bytes 589832 | tf_op jit(solution)/shard_map/ppermute | solution.py:188
  65.8 14.4 %collective-permute-start.22 = (bf16[48,2048]{1,0:T(8,128)(2,1)S(1)}, bf16[48,2048]{1,0:T(8,128)(2,1)S(1)}, u32[]{:S(2)}, u32[]{:S(2)}) collective-permute-start(bf16[48,2048]{1,0:T(8,128)(2,1)S(1)} %add_convert_fusion.7), channel_id=1, source_target_pairs={{0,4},{1,5},{2,6},{3,7},{4,0},{5,1},{6,2},{7,3},{8,12},{9,13},{10,... | collective-permute-start | bytes 589832 | tf_op jit(solution)/shard_map/ppermute | solution.py:188
  70.4 7.8 %collective-permute-start.24 = (bf16[48,2048]{1,0:T(8,128)(2,1)S(1)}, bf16[48,2048]{1,0:T(8,128)(2,1)S(1)}, u32[]{:S(2)}, u32[]{:S(2)}) collective-permute-start(bf16[48,2048]{1,0:T(8,128)(2,1)S(1)} %get-tuple-element.108), channel_id=1, source_target_pairs={{0,2},{1,3},{2,0},{3,1},{4,6},{5,7},{6,4},{7,5},{8,10},{9,11},{10,... | collective-permute-start | bytes 589832 | tf_op jit(solution)/shard_map/ppermute | solution.py:188
  71.7 16.2 %collective-permute-start.28 = (bf16[48,2048]{1,0:T(8,128)(2,1)S(1)}, bf16[48,2048]{1,0:T(8,128)(2,1)S(1)}, u32[]{:S(2)}, u32[]{:S(2)}) collective-permute-start(bf16[48,2048]{1,0:T(8,128)(2,1)S(1)} %get-tuple-element.114), channel_id=1, source_target_pairs={{0,2},{1,3},{2,0},{3,1},{4,6},{5,7},{6,4},{7,5},{8,10},{9,11},{10,... | collective-permute-start | bytes 589832 | tf_op jit(solution)/shard_map/ppermute | solution.py:188
  78.7 12.6 %collective-permute-start.26 = (bf16[48,2048]{1,0:T(8,128)(2,1)S(1)}, bf16[48,2048]{1,0:T(8,128)(2,1)S(1)}, u32[]{:S(2)}, u32[]{:S(2)}) collective-permute-start(bf16[48,2048]{1,0:T(8,128)(2,1)S(1)} %get-tuple-element.112), channel_id=1, source_target_pairs={{0,4},{1,5},{2,6},{3,7},{4,0},{5,1},{6,2},{7,3},{8,12},{9,13},{10,... | collective-permute-start | bytes 589832 | tf_op jit(solution)/shard_map/ppermute | solution.py:188
  80.2 5.9 %collective-permute-start.29 = (bf16[48,2048]{1,0:T(8,128)(2,1)S(1)}, bf16[48,2048]{1,0:T(8,128)(2,1)S(1)}, u32[]{:S(2)}, u32[]{:S(2)}) collective-permute-start(bf16[48,2048]{1,0:T(8,128)(2,1)S(1)} %add_convert_fusion.4), channel_id=1, source_target_pairs={{0,2},{1,3},{2,0},{3,1},{4,6},{5,7},{6,4},{7,5},{8,10},{9,11},{10,... | collective-permute-start | bytes 589832 | tf_op jit(solution)/shard_map/ppermute | solution.py:188
  83.8 8.7 %collective-permute-start.31 = (bf16[48,2048]{1,0:T(8,128)(2,1)S(1)}, bf16[48,2048]{1,0:T(8,128)(2,1)S(1)}, u32[]{:S(2)}, u32[]{:S(2)}) collective-permute-start(bf16[48,2048]{1,0:T(8,128)(2,1)S(1)} %add_convert_fusion.2), channel_id=1, source_target_pairs={{0,24},{1,25},{2,26},{3,27},{4,28},{5,29},{6,30},{7,31},{8,0},{9,1... | collective-permute-start | bytes 589832 | tf_op jit(solution)/shard_map/ppermute | solution.py:191
  85.6 5.7 %collective-permute-start.27 = (bf16[48,2048]{1,0:T(8,128)(2,1)S(1)}, bf16[48,2048]{1,0:T(8,128)(2,1)S(1)}, u32[]{:S(2)}, u32[]{:S(2)}) collective-permute-start(bf16[48,2048]{1,0:T(8,128)(2,1)S(1)} %add_convert_fusion.5), channel_id=1, source_target_pairs={{0,4},{1,5},{2,6},{3,7},{4,0},{5,1},{6,2},{7,3},{8,12},{9,13},{10,... | collective-permute-start | bytes 589832 | tf_op jit(solution)/shard_map/ppermute | solution.py:188
  86.1 5.7 %collective-permute-start.25 = (bf16[48,2048]{1,0:T(8,128)(2,1)S(1)}, bf16[48,2048]{1,0:T(8,128)(2,1)S(1)}, u32[]{:S(2)}, u32[]{:S(2)}) collective-permute-start(bf16[48,2048]{1,0:T(8,128)(2,1)S(1)} %add_convert_fusion.6), channel_id=1, source_target_pairs={{0,2},{1,3},{2,0},{3,1},{4,6},{5,7},{6,4},{7,5},{8,10},{9,11},{10,... | collective-permute-start | bytes 589832 | tf_op jit(solution)/shard_map/ppermute | solution.py:188
  87.8 7.5 %collective-permute-start.33 = (bf16[48,2048]{1,0:T(8,128)(2,1)S(1)}, bf16[48,2048]{1,0:T(8,128)(2,1)S(1)}, u32[]{:S(2)}, u32[]{:S(2)}) collective-permute-start(bf16[48,2048]{1,0:T(8,128)(2,1)S(1)} %add_convert_fusion), channel_id=1, source_target_pairs={{0,8},{1,9},{2,10},{3,11},{4,12},{5,13},{6,14},{7,15},{8,16},{9,17... | collective-permute-start | bytes 589832 | tf_op jit(solution)/shard_map/ppermute | solution.py:191
  91.9 8.6 %collective-permute-start.32 = (bf16[48,2048]{1,0:T(8,128)(2,1)S(1)}, bf16[48,2048]{1,0:T(8,128)(2,1)S(1)}, u32[]{:S(2)}, u32[]{:S(2)}) collective-permute-start(bf16[48,2048]{1,0:T(8,128)(2,1)S(1)} %add_convert_fusion.1), channel_id=1, source_target_pairs={{0,16},{1,17},{2,18},{3,19},{4,20},{5,21},{6,22},{7,23},{8,24},{9,... | collective-permute-start | bytes 589832 | tf_op jit(solution)/shard_map/ppermute | solution.py:191
  (7 other events, 118.1 us)

commit v4 on v3

--- a/solution.py
+++ b/solution.py
@@ -105,10 +105,6 @@
     )(plane, ids.T, gates.T, in_vmem(tokens), b_out, *[in_vmem(value) for value in rows])
 
 
-def after(value, *earlier):
-    return lax.optimization_barrier((value, *earlier))[0]
-
-
 def stage_kernel(*refs):
     count = len(refs) // 3
     sources, targets, sems = refs[:count], refs[count : 2 * count], refs[2 * count :]
@@ -131,42 +127,55 @@
     )(*[in_hbm(array) for array in arrays])
 
 
-def expert_kernel(tile, *refs):
-    blocks = (len(refs) - 8) // 2
-    row_refs, (in_0, in_1, bias_0, bias_1, out_0, out_1) = refs[:blocks], refs[blocks : blocks + 6]
-    part_refs, (rows, hidden) = refs[blocks + 6 : -2], refs[-2:]
-    cap = row_refs[0].shape[0]
-    units = in_0.shape[1]
-    for b in range(blocks):
-        rows[b * cap : (b + 1) * cap, :] = row_refs[b][...]
+def feed_forward(count, tile, weights, rows, hidden, put):
+    in_0, in_1, bias_0, bias_1, out_0, out_1 = weights
+    units, width = out_0.shape
     for k, (w_in, bias) in enumerate(((in_0, bias_0), (in_1, bias_1))):
-        for start in range(0, units, tile):
-            cols = slice(start, start + tile)
+        for t in range(units // tile):
+            cols = slice(t * tile, (t + 1) * tile)
             sums = jnp.dot(rows[...], w_in[:, cols], preferred_element_type=jnp.float32) + bias[:, cols]
-            hidden[:, k * units + start : k * units + start + tile] = jnp.maximum(sums, 0.0).astype(jnp.bfloat16)
-    for start in range(0, out_0.shape[1], tile):
-        cols = slice(start, start + tile)
+            hidden[:, k * units + t * tile : k * units + (t + 1) * tile] = jnp.maximum(sums, 0.0).astype(jnp.bfloat16)
+    for t in range(width // tile):
+        cols = slice(t * tile, (t + 1) * tile)
         sums = jnp.dot(hidden[:, :units], out_0[:, cols], preferred_element_type=jnp.float32)
         sums += jnp.dot(hidden[:, units:], out_1[:, cols], preferred_element_type=jnp.float32)
-        for b in range(blocks):
-            part_refs[b][:, cols] = sums[b * cap : (b + 1) * cap, :].astype(part_refs[b].dtype)
-
-
-def expert_rows(rows, weights, types):
-    cap, width = rows[0].shape
+        put(t * tile, (t + 1) * tile, sums)
+
+
+def expert_kernel(tile, *refs):
+    pieces = (len(refs) - 8) // 2
+    row_refs, weights, sum_refs, (rows, hidden) = refs[:pieces], refs[pieces : pieces + 6], refs[pieces + 6 : -2], refs[-2:]
+    count = row_refs[0].shape[0]
+    width = rows.shape[1]
+    places = []
+    start = column = 0
+    for ref in row_refs:
+        places.append((start, column))
+        rows[start : start + count, column : column + ref.shape[1]] = ref[...]
+        column = (column + ref.shape[1]) % width
+        start += 0 if column else count
+
+    def put(first, last, sums):
+        for ref, (start, column) in zip(sum_refs, places):
+            if column <= first < column + ref.shape[1]:
+                piece = sums[start : start + count, :].astype(ref.dtype)
+                ref[:, first - column : last - column] = piece
+
+    feed_forward(count, tile, weights, rows, hidden, put)
+
+
+def expert_rows(rows, weights, kinds):
+    count, width = rows[0].shape[0], weights[0].shape[0]
     units = weights[0].shape[1]
-    count = len(rows) * cap
+    total = count * sum(value.shape[1] for value in rows) // width
     vmem = pl.BlockSpec(memory_space=pltpu.VMEM)
     return pl.pallas_call(
         functools.partial(expert_kernel, 512),
-        out_shape=[pltpu.VMEM((cap, width), kind) for kind in types],
+        out_shape=[pltpu.VMEM(value.shape, kind) for value, kind in zip(rows, kinds)],
         in_specs=[vmem] * (len(rows) + 6),
         out_specs=[vmem] * len(rows),
-        scratch_shapes=[pltpu.VMEM((count, width), jnp.bfloat16), pltpu.VMEM((count, 2 * units), jnp.bfloat16)],
-        compiler_params=pltpu.CompilerParams(vmem_limit_bytes=12 << 20),
-        cost_estimate=pl.CostEstimate(
-            flops=8 * count * width * units, bytes_accessed=8 * width * units, transcendentals=0
-        ),
+        scratch_shapes=[pltpu.VMEM((total, width), jnp.bfloat16), pltpu.VMEM((total, 2 * units), jnp.bfloat16)],
+        compiler_params=pltpu.CompilerParams(vmem_limit_bytes=16 << 20),
         name="expert",
     )(*[in_vmem(value) for value in (*rows, *weights)])
 
@@ -191,86 +200,91 @@
         return lax.ppermute(value, "local", [(i, (i + planes * shared) % devices) for i in range(devices)])
 
     w_in, w_out = w_in[0], w_out[0]
-    kinds = (jnp.float32, jnp.float32, jnp.bfloat16, jnp.bfloat16)
-    peer_in, peer_out, peer_bias = across(w_in, 1), across(w_out, 1), across(b_in, 1)
-
+    half = tokens.shape[1] // 2
+    sent = {}
+
+    def put(name, make, *args):
+        with jax.named_scope(name):
+            sent[name] = make(*args)
+
+    def join(*names, ordered=()):
+        for early, late in zip(ordered, ordered[1:]):
+            sent[late] = lax.optimization_barrier((sent[late], sent[early]))[0]
+        names += ordered
+        values = lax.optimization_barrier([sent[name] for name in names])
+        sent.update(zip(names, values))
+
+    def fold(sums, low, high):
+        to_x = jnp.concatenate([sums[1][:, :half] + low.astype(jnp.float32), sums[1][:, half:]], axis=1)
+        to_y = jnp.concatenate([sums[2][:, :half], sums[2][:, half:] + high.astype(jnp.float32)], axis=1)
+        return to_x.astype(jnp.bfloat16), to_y.astype(jnp.bfloat16)
+
+    def total(sums, *others):
+        return (sums[0] + sum(value.astype(jnp.float32) for value in others)).astype(jnp.bfloat16)
+
+    near = sorted({1, experts - 1})
+    far = list(range(2, experts - 1))
+    wide, short = jnp.float32, jnp.bfloat16
     blocks = dispatch(plane, expert_ids, tokens, norm_gain, norm_bias, slot_cap, experts)
-    mark = [None]
-
-    def then(*values):
-        if mark[0] is not None:
-            values = lax.optimization_barrier((*values, mark[0]))[:-1]
-        mark[0] = values[0]
-        return values if len(values) > 1 else values[0]
-
-    class Block:
-        def __init__(self, d, near, far):
-            self.d, self.near, self.far = d, near, far
-
-        def spread(self, rows):
-            self.rows = rows
-            self.first, self.second = across(rows, self.near), across(rows, self.far)
-
-        def pass_on(self):
-            self.first = then(self.first)
-            self.third = across(self.first, self.far)
-
-        def compute(self):
-            rows = then(self.rows, self.first, self.second, self.third)
-            self.part = expert_rows(rows, weights, kinds)
-            self.back_third = across(self.part[3], self.far)
-            self.back_second = across(self.part[2], self.far)
-
-        def fold(self):
-            self.back_third = then(self.back_third)
-            both = self.part[1] + self.back_third.astype(jnp.float32)
-            self.back_first = across(both.astype(jnp.bfloat16), self.near)
-
-        def finish(self):
-            first, second = then(self.back_first, self.back_second)
-            summed = self.part[0] + first.astype(jnp.float32) + second.astype(jnp.float32)
-            self.out = summed.astype(jnp.bfloat16)
-            if self.d:
-                self.out = along(self.out, -self.d)
-
-    order = [0] + sorted(range(1, experts), key=lambda d: min(d, experts - d))
-    units = [Block(d, *((2, 4) if i % 2 == 0 else (4, 2))) for i, d in enumerate(order)]
-    own, rest = units[0], units[1:]
-    moved = {}
-    for unit in rest:
-        steps = min(unit.d, experts - unit.d)
-        moved[unit.d] = [along(blocks[unit.d], 1 if unit.d == steps else -1), steps - 1]
-    own.spread(blocks[0])
-    weights = None
-    for turn in range(experts):
-        for unit in rest:
-            if unit.d in moved:
-                value, left = moved[unit.d]
-                value = then(value)
-                if left:
-                    moved[unit.d] = [along(value, 1 if 2 * unit.d <= experts else -1), left - 1]
-                else:
-                    del moved[unit.d]
-                    unit.spread(value)
-                    if unit is rest[0]:
-                        own.pass_on()
-                    else:
-                        rest[rest.index(unit) - 1].pass_on()
-        if turn == 0:
-            w_in, w_out = stage(then(w_in), w_out)
-    peer_in, peer_out = stage(then(peer_in), peer_out)
-    weights = (w_in, peer_in, b_in, peer_bias, w_out, peer_out)
-    rest[0].compute()
-    rest[-1].pass_on()
-    for i, unit in enumerate(rest[1:] + [own]):
-        unit.compute()
-        units[i + 1].fold()
-    for i, unit in enumerate(rest):
-        unit.finish()
-        if i == 0:
-            own.fold()
-    own.finish()
-    results = [next(unit.out for unit in units if unit.d == d) for d in range(experts)]
+    own = blocks[0]
+    put("w1", across, w_in, 1)
+    put("z1", along, blocks[near[0]], near[0])
+    put("z3", along, blocks[near[-1]], near[-1])
+    put("ox", across, own, 2)
+    put("oy", across, own, 4)
+    put("od", across, own, 6)
+    sent["mine"], sent["own"] = [w_in, w_out], own
+    join("mine", "own")
+    put("K", stage, *sent["mine"])
+    sent["out"], sent["bias"], sent["blocks"] = w_out, b_in, [blocks[d] for d in far]
+    join("own", "out", "bias", "blocks", ordered=("z1", "z3", "ox", "oy", "w1", "K"))
+    mine_in, mine_out = sent["K"]
+    near_rows = jnp.concatenate([sent["z1"], sent["z3"]][: len(near)])
+    put("w2", across, sent["out"], 1)
+    put("A1x", across, near_rows, 2)
+    put("A1y", across, near_rows, 4)
+    put("z2", lambda: [along(block, d) for block, d in zip(sent["blocks"], far)])
+    put("b", across, sent["bias"], 1)
+    put("K2", stage, sent["w1"], sent["w2"])
+    join("A1x", "A1y", "K2", "b")
+    peer_in, peer_out = sent["K2"]
+    weights = (mine_in, peer_in, b_in, sent["b"], mine_out, peer_out)
+    far_rows = jnp.concatenate(sent["z2"]) if len(far) > 1 else sent["z2"][0]
+    put("A2a", across, sent["A1x"][:, :half], 4)
+    put("A2b", across, sent["A1y"][:, half:], 2)
+    put("B1x", across, far_rows, 2)
+    put("B1y", across, far_rows, 4)
+    put("bd", across, far_rows, 6)
+    put("EA1", expert_rows, [near_rows, sent["A1x"], sent["A1y"]], weights, [wide] * 3)
+    join("EA1", "A2a", "A2b", "od")
+    put("EA2", expert_rows, [sent["A2a"], sent["A2b"]], weights, [short] * 2)
+    join("EA2", "B1x", "B1y")
+    put("AR1a", across, sent["EA2"][0], 4)
+    put("AR1b", across, sent["EA2"][1], 2)
+    rows = [far_rows, *(sent[name] for name in ("B1x", "B1y", "bd"))]
+    put("EB", expert_rows, rows, weights, [wide] + [short] * 3)
+    join("EB", "AR1a", "AR1b")
+    to_x, to_y = fold(sent["EA1"], sent["AR1a"], sent["AR1b"])
+    put("AR2x", across, to_x, 2)
+    put("AR2y", across, to_y, 4)
+    for part, piece, bits in zip("xyd", sent["EB"][1:], (2, 4, 6)):
+        put("BR" + part, across, piece, bits)
+    rows = [sent["own"], sent["ox"], sent["oy"], sent["od"]]
+    rows, sent["EB"] = lax.optimization_barrier((rows, list(sent["EB"])))
+    put("EO", expert_rows, rows, weights, [wide] + [short] * 3)
+    join("AR2x", "AR2y", "EO")
+    value = total(sent["EA1"], sent["AR2x"], sent["AR2y"])
+    for i, d in enumerate(near):
+        put("c1" if i == 0 else "c3", along, value[i * slot_cap : (i + 1) * slot_cap], -d)
+    join("BRx", "BRy", "BRd")
+    value = total(sent["EB"], *(sent[name] for name in ("BRx", "BRy", "BRd")))
+    put("c2", lambda: [along(value[i * slot_cap : (i + 1) * slot_cap], -d) for i, d in enumerate(far)])
+    for part, piece, bits in zip("xyd", sent["EO"][1:], (2, 4, 6)):
+        put("OR" + part, across, piece, bits)
+    rows = dict(zip(far, sent["c2"]))
+    rows[near[0]], rows[near[-1]] = sent["c1"], sent["c3"]
+    rows[0] = total(sent["EO"], sent["ORx"], sent["ORy"], sent["ORd"])
+    results = [rows[d] for d in range(experts)]
     return combine(plane, expert_ids, gate_weights, tokens, b_out, results, slot_cap)
 
 

time: 102 us -> 87.4 us (0.86)
  waiting for transfers between devices: 42.6 us -> 20.2 us
  starting transfers between devices: 34.9 us -> 40.9 us
  Pallas kernels: 23.9 us -> 25.2 us
    ppermute x7 -> x6, waiting for transfers between devices: 22.6 us -> 6.73 us  [along(): lax.ppermute(value, 'local', [(i, (i + planes * shared) % devices) for i...]
    ppermute x27 -> x23, waiting for transfers between devices: 19.9 us -> 13.5 us  [across(): return lax.ppermute(value, 'local', [(i, i ^ bit) for i in range(devices)])]
    ppermute x27 -> x23, starting transfers between devices: 26 us -> 30 us  [across(): return lax.ppermute(value, 'local', [(i, i ^ bit) for i in range(devices)])]
    ppermute x7 -> x6, starting transfers between devices: 8.91 us -> 10.8 us  [along(): lax.ppermute(value, 'local', [(i, (i + planes * shared) % devices) for i...]
    pallas_call x4, Pallas kernels: 13.8 us -> 15 us  [expert_rows(): pl.pallas_call(functools.partial(expert_kernel, 512), out_shape=[pltpu.VM...]
  transfers between devices with their start and end apart: 34 -> 29, of which waited for: 16 -> 10; matrix products, arithmetic and copies ran while one was open for 0% -> 1% of each run, Pallas kernels for 22% -> 27%
where the time goes in v4:
time: 87.4 us; the launch traced here: 87.2 us
  starting transfers between devices  40.9 us (47%)
  Pallas kernels  25.2 us (29%)
  waiting for transfers between devices  20.2 us (23%)
    ppermute x23, starting transfers between devices, across(): return lax.ppermute(value, 'local', [(i, i ^ bit) for i in range(devices)])  30 us
    pallas_call x4, Pallas kernels, expert_rows(): pl.pallas_call(functools.partial(expert_kernel, 512), out_shape=[pltpu.VM...  15 us
    ppermute x23, waiting for transfers between devices, across(): return lax.ppermute(value, 'local', [(i, i ^ bit) for i in range(devices)])  13.5 us
    ppermute x6, starting transfers between devices, along(): lax.ppermute(value, 'local', [(i, (i + planes * shared) % devices) for i...  10.8 us
    pallas_call x2, Pallas kernels, stage(): pl.pallas_call(stage_kernel, out_shape=[pltpu.VMEM(array.shape, array.dty...  7.1 us
    ppermute x6, waiting for transfers between devices, along(): lax.ppermute(value, 'local', [(i, (i + planes * shared) % devices) for i...  6.73 us
  transfers between devices with their start and end apart: 29, of which 10 were waited for; matrix products, arithmetic and copies ran while one was open for 1% of the time, Pallas kernels for 27%

profile of v4, /device:TPU:0, one launch (start us, length us, event | category | flops | bytes accessed | tf_op | source)
XLA Modules:
  0.0 87.2 jit_solution(14227634869164547445)
XLA Ops:
  0.5 1.6 %dispatch.1 = (bf16[48,2048]{1,0:T(8,128)(2,1)S(1)}, bf16[48,2048]{1,0:T(8,128)(2,1)S(1)}, bf16[48,2048]{1,0:T(8,128)(2,1)S(1)}, bf16[48,2048]{1,0:T(8,128)(2,1)S(1)}) custom-call(s32[1]{0:T(128)} %bitcast.plane_ref, s32[2,64]{1,0:T(2,128)} %bitcast.7, bf16[64,2048]{1,0:T(8,128)(2,1)} %tokens_ref.3, f32[1,2048]{1,0:T(1,128)} %bitcast.14, f32[1,2048]{1,0:T(1,128)} %bitcast.15), custom_call_target="tpu_custom_call" | custom-call | tf_op jit(solution)/shard_map/dispatch/pallas_call | solution.py:48
  2.0 2.6 %collective-permute-start = (bf16[48,2048]{1,0:T(8,128)(2,1)S(1)}, bf16[48,2048]{1,0:T(8,128)(2,1)S(1)}, u32[]{:S(2)}, u32[]{:S(2)}) collective-permute-start(bf16[48,2048]{1,0:T(8,128)(2,1)S(1)} %get-tuple-element.84), channel_id=1, source_target_pairs={{0,8},{1,9},{2,10},{3,11},{4,12},{5,13},{6,14},{7,15},{8,16},{9,17... | collective-permute-start | bytes 589832 | tf_op jit(solution)/shard_map/z1/ppermute | solution.py:200
  4.6 2.1 %collective-permute-start.1 = (bf16[48,2048]{1,0:T(8,128)(2,1)S(1)}, bf16[48,2048]{1,0:T(8,128)(2,1)S(1)}, u32[]{:S(2)}, u32[]{:S(2)}) collective-permute-start(bf16[48,2048]{1,0:T(8,128)(2,1)S(1)} %get-tuple-element.85), channel_id=1, source_target_pairs={{0,24},{1,25},{2,26},{3,27},{4,28},{5,29},{6,30},{7,31},{8,0},{9,1... | collective-permute-start | bytes 589832 | tf_op jit(solution)/shard_map/z3/ppermute | solution.py:200
  6.7 1.6 %collective-permute-start.2 = (bf16[48,2048]{1,0:T(8,128)(2,1)S(1)}, bf16[48,2048]{1,0:T(8,128)(2,1)S(1)}, u32[]{:S(2)}, u32[]{:S(2)}) collective-permute-start(bf16[48,2048]{1,0:T(8,128)(2,1)S(1)} %get-tuple-element.138.refs_0_), channel_id=1, source_target_pairs={{0,2},{1,3},{2,0},{3,1},{4,6},{5,7},{6,4},{7,5},{8,10},{9,11},{10,... | collective-permute-start | bytes 589832 | tf_op jit(solution)/shard_map/ox/ppermute | solution.py:197
  8.4 1.5 %collective-permute-start.3 = (bf16[48,2048]{1,0:T(8,128)(2,1)S(1)}, bf16[48,2048]{1,0:T(8,128)(2,1)S(1)}, u32[]{:S(2)}, u32[]{:S(2)}) collective-permute-start(bf16[48,2048]{1,0:T(8,128)(2,1)S(1)} %get-tuple-element.138.refs_0_), channel_id=1, source_target_pairs={{0,4},{1,5},{2,6},{3,7},{4,0},{5,1},{6,2},{7,3},{8,12},{9,13},{10,... | collective-permute-start | bytes 589832 | tf_op jit(solution)/shard_map/oy/ppermute | solution.py:197
  9.9 3.6 %stage.2 = (bf16[2048,1024]{1,0:T(8,128)(2,1)S(1)}, bf16[1024,2048]{1,0:T(8,128)(2,1)S(1)}) custom-call(bf16[2048,1024]{1,0:T(8,128)(2,1)} %bitcast.11, bf16[1024,2048]{1,0:T(8,128)(2,1)} %bitcast.12), custom_call_target="tpu_custom_call" | custom-call | tf_op jit(solution)/shard_map/K/stage/pallas_call | solution.py:119
  13.5 2.3 %collective-permute-done.1 = bf16[48,2048]{1,0:T(8,128)(2,1)S(1)} collective-permute-done((bf16[48,2048]{1,0:T(8,128)(2,1)S(1)}, bf16[48,2048]{1,0:T(8,128)(2,1)S(1)}, u32[]{:S(2)}, u32[]{:S(2)}) %collective-permute-start.1) | collective-permute-done | bytes 196640 | tf_op jit(solution)/shard_map/z3/ppermute | solution.py:200
  16.0 1.6 %collective-permute-start.5 = (bf16[96,2048]{1,0:T(8,128)(2,1)S(1)}, bf16[96,2048]{1,0:T(8,128)(2,1)S(1)}, u32[]{:S(2)}, u32[]{:S(2)}) collective-permute-start(bf16[96,2048]{1,0:T(8,128)(2,1)S(1)} %constant_dynamic-update-slice_fusion.refs_0_), channel_id=1, source_target_pairs={{0,2},{1,3},{2,0},{3,1},{4,6},{5,7},{6,4},{7,5},{8,10},{9,11},{10,... | collective-permute-start | bytes 1179656 | tf_op jit(solution)/shard_map/A1x/ppermute | solution.py:197
  17.6 1.5 %collective-permute-start.6 = (bf16[96,2048]{1,0:T(8,128)(2,1)S(1)}, bf16[96,2048]{1,0:T(8,128)(2,1)S(1)}, u32[]{:S(2)}, u32[]{:S(2)}) collective-permute-start(bf16[96,2048]{1,0:T(8,128)(2,1)S(1)} %constant_dynamic-update-slice_fusion.refs_0_), channel_id=1, source_target_pairs={{0,4},{1,5},{2,6},{3,7},{4,0},{5,1},{6,2},{7,3},{8,12},{9,13},{10,... | collective-permute-start | bytes 1179656 | tf_op jit(solution)/shard_map/A1y/ppermute | solution.py:197
  20.4 2.7 %collective-permute-done.7.refs_1_ = bf16[1024,2048]{1,0:T(8,128)(2,1)S(1)} collective-permute-done((bf16[1024,2048]{1,0:T(8,128)(2,1)S(1)}, bf16[1024,2048]{1,0:T(8,128)(2,1)S(1)}, u32[]{:S(2)}, u32[]{:S(2)}) %collective-permute-start.7) | collective-permute-done | bytes 4194336 | tf_op jit(solution)/shard_map/w2/ppermute | solution.py:197
  23.1 2.4 %collective-permute-start.11 = (bf16[48,2048]{1,0:T(8,128)(2,1)S(1)}, bf16[48,2048]{1,0:T(8,128)(2,1)S(1)}, u32[]{:S(2)}, u32[]{:S(2)}) collective-permute-start(bf16[48,2048]{1,0:T(8,128)(2,1)S(1)} %get-tuple-element.138.refs_0_), channel_id=1, source_target_pairs={{0,6},{1,7},{2,4},{3,5},{4,2},{5,3},{6,0},{7,1},{8,14},{9,15},{10,... | collective-permute-start | bytes 589832 | tf_op jit(solution)/shard_map/od/ppermute | solution.py:197
  25.6 3.5 %stage.3 = (bf16[2048,1024]{1,0:T(8,128)(2,1)S(1)}, bf16[1024,2048]{1,0:T(8,128)(2,1)S(1)}) custom-call(bf16[2048,1024]{1,0:T(8,128)(2,1)} %collective-permute-done.4.refs_0_, bf16[1024,2048]{1,0:T(8,128)(2,1)} %copy-done.6), custom_call_target="tpu_custom_call" | custom-call | tf_op jit(solution)/shard_map/K2/stage/pallas_call | solution.py:119
  29.1 3.9 %collective-permute-done.6.refs_2_ = bf16[96,2048]{1,0:T(8,128)(2,1)S(1)} collective-permute-done((bf16[96,2048]{1,0:T(8,128)(2,1)S(1)}, bf16[96,2048]{1,0:T(8,128)(2,1)S(1)}, u32[]{:S(2)}, u32[]{:S(2)}) %collective-permute-start.6) | collective-permute-done | bytes 393248 | tf_op jit(solution)/shard_map/A1y/ppermute | solution.py:197
  33.2 2.1 %collective-permute-start.9 = (bf16[96,1024]{1,0:T(8,128)(2,1)S(1)}, bf16[96,1024]{1,0:T(8,128)(2,1)S(1)}, u32[]{:S(2)}, u32[]{:S(2)}) collective-permute-start(bf16[96,1024]{1,0:T(8,128)(2,1)S(1)} %slice.26), channel_id=1, source_target_pairs={{0,4},{1,5},{2,6},{3,7},{4,0},{5,1},{6,2},{7,3},{8,12},{9,13},{10,... | collective-permute-start | bytes 589832 | tf_op jit(solution)/shard_map/A2a/ppermute | solution.py:197
  35.3 1.5 %collective-permute-start.13 = (bf16[48,2048]{1,0:T(8,128)(2,1)S(1)}, bf16[48,2048]{1,0:T(8,128)(2,1)S(1)}, u32[]{:S(2)}, u32[]{:S(2)}) collective-permute-start(bf16[48,2048]{1,0:T(8,128)(2,1)S(1)} %collective-permute-done.12.refs_0_), channel_id=1, source_target_pairs={{0,2},{1,3},{2,0},{3,1},{4,6},{5,7},{6,4},{7,5},{8,10},{9,11},{10,... | collective-permute-start | bytes 589832 | tf_op jit(solution)/shard_map/B1x/ppermute | solution.py:197
  37.3 5.1 %expert.4 = (f32[96,2048]{1,0:T(8,128)S(1)}, f32[96,2048]{1,0:T(8,128)S(1)}, f32[96,2048]{1,0:T(8,128)S(1)}) custom-call(bf16[96,2048]{1,0:T(8,128)(2,1)S(1)} %constant_dynamic-update-slice_fusion.refs_0_, bf16[96,2048]{1,0:T(8,128)(2,1)S(1)} %collective-permute-done.5.refs_1_, bf16[96,2048]{1,0:T(8,128)(2,1)S(1)} %collective-permute-done.6.refs_2_, ...), custom_call_target="tpu_custom_call" | custom-call | tf_op jit(solution)/shard_map/EA1/expert/pallas_call | solution.py:172
  42.4 1.5 %collective-permute-start.15 = (bf16[48,2048]{1,0:T(8,128)(2,1)S(1)}, bf16[48,2048]{1,0:T(8,128)(2,1)S(1)}, u32[]{:S(2)}, u32[]{:S(2)}) collective-permute-start(bf16[48,2048]{1,0:T(8,128)(2,1)S(1)} %collective-permute-done.12.refs_0_), channel_id=1, source_target_pairs={{0,6},{1,7},{2,4},{3,5},{4,2},{5,3},{6,0},{7,1},{8,14},{9,15},{10,... | collective-permute-start | bytes 589832 | tf_op jit(solution)/shard_map/bd/ppermute | solution.py:197
  43.9 2.8 %expert.5 = (bf16[96,1024]{1,0:T(8,128)(2,1)S(1)}, bf16[96,1024]{1,0:T(8,128)(2,1)S(1)}) custom-call(bf16[96,1024]{1,0:T(8,128)(2,1)S(1)} %collective-permute-done.9.refs_0_, bf16[96,1024]{1,0:T(8,128)(2,1)S(1)} %collective-permute-done.10.refs_1_, bf16[2048,1024]{1,0:T(8,128)(2,1)S(1)} %get-tuple-element.105.refs_3_.refs_2_.refs_4_, ...), custom_call_target="tpu_custom_call" | custom-call | tf_op jit(solution)/shard_map/EA2/expert/pallas_call | solution.py:172
  46.9 2.6 %collective-permute-start.17 = (bf16[96,1024]{1,0:T(8,128)(2,1)S(1)}, bf16[96,1024]{1,0:T(8,128)(2,1)S(1)}, u32[]{:S(2)}, u32[]{:S(2)}) collective-permute-start(bf16[96,1024]{1,0:T(8,128)(2,1)S(1)} %get-tuple-element.126), channel_id=1, source_target_pairs={{0,2},{1,3},{2,0},{3,1},{4,6},{5,7},{6,4},{7,5},{8,10},{9,11},{10,... | collective-permute-start | bytes 589832 | tf_op jit(solution)/shard_map/AR1b/ppermute | solution.py:197
  49.6 3.5 %expert.6 = (f32[48,2048]{1,0:T(8,128)S(1)}, bf16[48,2048]{1,0:T(8,128)(2,1)S(1)}, bf16[48,2048]{1,0:T(8,128)(2,1)S(1)}, bf16[48,2048]{1,0:T(8,128)(2,1)S(1)}) custom-call(bf16[48,2048]{1,0:T(8,128)(2,1)S(1)} %collective-permute-done.12.refs_0_, bf16[48,2048]{1,0:T(8,128)(2,1)S(1)} %collective-permute-done.13.refs_1_, ...), custom_call_target="tpu_custom_call" | custom-call | tf_op jit(solution)/shard_map/EB/expert/pallas_call | solution.py:172
  53.2 2.3 %collective-permute-start.24 = (bf16[48,2048]{1,0:T(8,128)(2,1)S(1)}, bf16[48,2048]{1,0:T(8,128)(2,1)S(1)}, u32[]{:S(2)}, u32[]{:S(2)}) collective-permute-start(bf16[48,2048]{1,0:T(8,128)(2,1)S(1)} %get-tuple-element.135), channel_id=1, source_target_pairs={{0,2},{1,3},{2,0},{3,1},{4,6},{5,7},{6,4},{7,5},{8,10},{9,11},{10,... | collective-permute-start | bytes 589832 | tf_op jit(solution)/shard_map/BRx/ppermute | solution.py:197
  55.6 2.9 %collective-permute-start.25 = (bf16[48,2048]{1,0:T(8,128)(2,1)S(1)}, bf16[48,2048]{1,0:T(8,128)(2,1)S(1)}, u32[]{:S(2)}, u32[]{:S(2)}) collective-permute-start(bf16[48,2048]{1,0:T(8,128)(2,1)S(1)} %get-tuple-element.136), channel_id=1, source_target_pairs={{0,4},{1,5},{2,6},{3,7},{4,0},{5,1},{6,2},{7,3},{8,12},{9,13},{10,... | collective-permute-start | bytes 589832 | tf_op jit(solution)/shard_map/BRy/ppermute | solution.py:197
  58.6 1.5 %collective-permute-start.19 = (bf16[96,2048]{1,0:T(8,128)(2,1)S(1)}, bf16[96,2048]{1,0:T(8,128)(2,1)S(1)}, u32[]{:S(2)}, u32[]{:S(2)}) collective-permute-start(bf16[96,2048]{1,0:T(8,128)(2,1)S(1)} %pad_maximum_fusion.1), channel_id=1, source_target_pairs={{0,4},{1,5},{2,6},{3,7},{4,0},{5,1},{6,2},{7,3},{8,12},{9,13},{10,... | collective-permute-start | bytes 1179656 | tf_op jit(solution)/shard_map/AR2y/ppermute | solution.py:197
  60.2 2.1 %collective-permute-start.18 = (bf16[96,2048]{1,0:T(8,128)(2,1)S(1)}, bf16[96,2048]{1,0:T(8,128)(2,1)S(1)}, u32[]{:S(2)}, u32[]{:S(2)}) collective-permute-start(bf16[96,2048]{1,0:T(8,128)(2,1)S(1)} %pad_maximum_fusion), channel_id=1, source_target_pairs={{0,2},{1,3},{2,0},{3,1},{4,6},{5,7},{6,4},{7,5},{8,10},{9,11},{10,... | collective-permute-start | bytes 1179656 | tf_op jit(solution)/shard_map/AR2x/ppermute | solution.py:197
  62.2 3.7 %expert.7 = (f32[48,2048]{1,0:T(8,128)S(1)}, bf16[48,2048]{1,0:T(8,128)(2,1)S(1)}, bf16[48,2048]{1,0:T(8,128)(2,1)S(1)}, bf16[48,2048]{1,0:T(8,128)(2,1)S(1)}) custom-call(bf16[48,2048]{1,0:T(8,128)(2,1)S(1)} %get-tuple-element.138.refs_0_, bf16[48,2048]{1,0:T(8,128)(2,1)S(1)} %collective-permute-done.2.refs_1_, ...), custom_call_target="tpu_custom_call" | custom-call | tf_op jit(solution)/shard_map/EO/expert/pallas_call | solution.py:172
  66.0 1.6 %collective-permute-done.26 = bf16[48,2048]{1,0:T(8,128)(2,1)S(1)} collective-permute-done((bf16[48,2048]{1,0:T(8,128)(2,1)S(1)}, bf16[48,2048]{1,0:T(8,128)(2,1)S(1)}, u32[]{:S(2)}, u32[]{:S(2)}) %collective-permute-start.26) | collective-permute-done | bytes 196640 | tf_op jit(solution)/shard_map/BRd/ppermute | solution.py:197
  69.0 2.6 %collective-permute-done.19 = bf16[96,2048]{1,0:T(8,128)(2,1)S(1)} collective-permute-done((bf16[96,2048]{1,0:T(8,128)(2,1)S(1)}, bf16[96,2048]{1,0:T(8,128)(2,1)S(1)}, u32[]{:S(2)}, u32[]{:S(2)}) %collective-permute-start.19) | collective-permute-done | bytes 393248 | tf_op jit(solution)/shard_map/AR2y/ppermute | solution.py:197
  71.7 1.4 %collective-permute-start.20 = (bf16[48,2048]{1,0:T(8,128)(2,1)S(1)}, bf16[48,2048]{1,0:T(8,128)(2,1)S(1)}, u32[]{:S(2)}, u32[]{:S(2)}) collective-permute-start(bf16[48,2048]{1,0:T(8,128)(2,1)S(1)} %get-tuple-element.147), channel_id=1, source_target_pairs={{0,2},{1,3},{2,0},{3,1},{4,6},{5,7},{6,4},{7,5},{8,10},{9,11},{10,... | collective-permute-start | bytes 589832 | tf_op jit(solution)/shard_map/ORx/ppermute | solution.py:197
  75.3 2.4 %collective-permute-start.23 = (bf16[48,2048]{1,0:T(8,128)(2,1)S(1)}, bf16[48,2048]{1,0:T(8,128)(2,1)S(1)}, u32[]{:S(2)}, u32[]{:S(2)}) collective-permute-start(bf16[48,2048]{1,0:T(8,128)(2,1)S(1)} %get-tuple-element.158), channel_id=1, source_target_pairs={{0,24},{1,25},{2,26},{3,27},{4,28},{5,29},{6,30},{7,31},{8,0},{9,1... | collective-permute-start | bytes 589832 | tf_op jit(solution)/shard_map/c1/ppermute | solution.py:200
  79.3 1.9 %collective-permute-done.21 = bf16[48,2048]{1,0:T(8,128)(2,1)S(1)} collective-permute-done((bf16[48,2048]{1,0:T(8,128)(2,1)S(1)}, bf16[48,2048]{1,0:T(8,128)(2,1)S(1)}, u32[]{:S(2)}, u32[]{:S(2)}) %collective-permute-start.21) | collective-permute-done | bytes 196640 | tf_op jit(solution)/shard_map/ORy/ppermute | solution.py:197
  82.3 3.3 %collective-permute-done.28.refs_3_ = bf16[48,2048]{1,0:T(8,128)(2,1)S(1)} collective-permute-done((bf16[48,2048]{1,0:T(8,128)(2,1)S(1)}, bf16[48,2048]{1,0:T(8,128)(2,1)S(1)}, u32[]{:S(2)}, u32[]{:S(2)}) %collective-permute-start.28) | collective-permute-done | bytes 196640 | tf_op jit(solution)/shard_map/c3/ppermute | solution.py:200
  85.7 1.5 %combine.1 = bf16[64,2048]{1,0:T(8,128)(2,1)} custom-call(s32[1]{0:T(128)} %bitcast.plane_ref, s32[2,64]{1,0:T(2,128)S(1)} %bitcast.8, f32[2,64]{1,0:T(2,128)S(1)} %bitcast.9, bf16[64,2048]{1,0:T(8,128)(2,1)S(1)} %copy-done, f32[4,2048]{1,0:T(4,128)S(1)} %copy-done.2, bf16[48,2048]{1,0:T(8,128)(2,1)S(1)} %add_convert_fusion.2.refs_0_, ...), custom_call_target="tpu_custom_call" | custom-call | tf_op jit(solution)/shard_map/combine/pallas_call | solution.py:98
  (62 shorter events, 9.5 us)
Async XLA Ops:
  0.0 15.9 %collective-permute-start.4 = (bf16[2048,1024]{1,0:T(8,128)(2,1)}, bf16[2048,1024]{1,0:T(8,128)(2,1)}, u32[]{:S(2)}, u32[]{:S(2)}) collective-permute-start(bf16[2048,1024]{1,0:T(8,128)(2,1)} %bitcast.10), channel_id=1, source_target_pairs={{0,1},{1,0},{2,3},{3,2},{4,5},{5,4},{6,7},{7,6},{8,9},{9,8},{10,11... | collective-permute-start | bytes 12582920 | tf_op jit(solution)/shard_map/w1/ppermute | solution.py:197
  2.0 11.5 %collective-permute-start = (bf16[48,2048]{1,0:T(8,128)(2,1)S(1)}, bf16[48,2048]{1,0:T(8,128)(2,1)S(1)}, u32[]{:S(2)}, u32[]{:S(2)}) collective-permute-start(bf16[48,2048]{1,0:T(8,128)(2,1)S(1)} %get-tuple-element.84), channel_id=1, source_target_pairs={{0,8},{1,9},{2,10},{3,11},{4,12},{5,13},{6,14},{7,15},{8,16},{9,17... | collective-permute-start | bytes 589832 | tf_op jit(solution)/shard_map/z1/ppermute | solution.py:200
  4.6 11.2 %collective-permute-start.1 = (bf16[48,2048]{1,0:T(8,128)(2,1)S(1)}, bf16[48,2048]{1,0:T(8,128)(2,1)S(1)}, u32[]{:S(2)}, u32[]{:S(2)}) collective-permute-start(bf16[48,2048]{1,0:T(8,128)(2,1)S(1)} %get-tuple-element.85), channel_id=1, source_target_pairs={{0,24},{1,25},{2,26},{3,27},{4,28},{5,29},{6,30},{7,31},{8,0},{9,1... | collective-permute-start | bytes 589832 | tf_op jit(solution)/shard_map/z3/ppermute | solution.py:200
  6.7 9.2 %collective-permute-start.2 = (bf16[48,2048]{1,0:T(8,128)(2,1)S(1)}, bf16[48,2048]{1,0:T(8,128)(2,1)S(1)}, u32[]{:S(2)}, u32[]{:S(2)}) collective-permute-start(bf16[48,2048]{1,0:T(8,128)(2,1)S(1)} %get-tuple-element.138.refs_0_), channel_id=1, source_target_pairs={{0,2},{1,3},{2,0},{3,1},{4,6},{5,7},{6,4},{7,5},{8,10},{9,11},{10,... | collective-permute-start | bytes 589832 | tf_op jit(solution)/shard_map/ox/ppermute | solution.py:197
  8.4 7.5 %collective-permute-start.3 = (bf16[48,2048]{1,0:T(8,128)(2,1)S(1)}, bf16[48,2048]{1,0:T(8,128)(2,1)S(1)}, u32[]{:S(2)}, u32[]{:S(2)}) collective-permute-start(bf16[48,2048]{1,0:T(8,128)(2,1)S(1)} %get-tuple-element.138.refs_0_), channel_id=1, source_target_pairs={{0,4},{1,5},{2,6},{3,7},{4,0},{5,1},{6,2},{7,3},{8,12},{9,13},{10,... | collective-permute-start | bytes 589832 | tf_op jit(solution)/shard_map/oy/ppermute | solution.py:197
  15.9 7.2 %collective-permute-start.7 = (bf16[1024,2048]{1,0:T(8,128)(2,1)S(1)}, bf16[1024,2048]{1,0:T(8,128)(2,1)S(1)}, u32[]{:S(2)}, u32[]{:S(2)}) collective-permute-start(bf16[1024,2048]{1,0:T(8,128)(2,1)S(1)} %bitcast.13), channel_id=1, source_target_pairs={{0,1},{1,0},{2,3},{3,2},{4,5},{5,4},{6,7},{7,6},{8,9},{9,8},{10,11... | collective-permute-start | bytes 12582920 | tf_op jit(solution)/shard_map/w2/ppermute | solution.py:197
  16.0 13.1 %collective-permute-start.5 = (bf16[96,2048]{1,0:T(8,128)(2,1)S(1)}, bf16[96,2048]{1,0:T(8,128)(2,1)S(1)}, u32[]{:S(2)}, u32[]{:S(2)}) collective-permute-start(bf16[96,2048]{1,0:T(8,128)(2,1)S(1)} %constant_dynamic-update-slice_fusion.refs_0_), channel_id=1, source_target_pairs={{0,2},{1,3},{2,0},{3,1},{4,6},{5,7},{6,4},{7,5},{8,10},{9,11},{10,... | collective-permute-start | bytes 1179656 | tf_op jit(solution)/shard_map/A1x/ppermute | solution.py:197
  17.6 15.4 %collective-permute-start.6 = (bf16[96,2048]{1,0:T(8,128)(2,1)S(1)}, bf16[96,2048]{1,0:T(8,128)(2,1)S(1)}, u32[]{:S(2)}, u32[]{:S(2)}) collective-permute-start(bf16[96,2048]{1,0:T(8,128)(2,1)S(1)} %constant_dynamic-update-slice_fusion.refs_0_), channel_id=1, source_target_pairs={{0,4},{1,5},{2,6},{3,7},{4,0},{5,1},{6,2},{7,3},{8,12},{9,13},{10,... | collective-permute-start | bytes 1179656 | tf_op jit(solution)/shard_map/A1y/ppermute | solution.py:197
  19.1 16.1 %collective-permute-start.12 = (bf16[48,2048]{1,0:T(8,128)(2,1)S(1)}, bf16[48,2048]{1,0:T(8,128)(2,1)S(1)}, u32[]{:S(2)}, u32[]{:S(2)}) collective-permute-start(bf16[48,2048]{1,0:T(8,128)(2,1)S(1)} %get-tuple-element.114), channel_id=1, source_target_pairs={{0,16},{1,17},{2,18},{3,19},{4,20},{5,21},{6,22},{7,23},{8,24},{9,... | collective-permute-start | bytes 589832 | tf_op jit(solution)/shard_map/z2/ppermute | solution.py:200
  20.4 8.7 %collective-permute-start.8 = (f32[1,1024]{1,0:T(1,128)S(1)}, f32[1,1024]{1,0:T(1,128)S(1)}, u32[]{:S(2)}, u32[]{:S(2)}) collective-permute-start(f32[1,1024]{1,0:T(1,128)S(1)} %copy-done.1), channel_id=1, source_target_pairs={{0,1},{1,0},{2,3},{3,2},{4,5},{5,4},{6,7},{7,6},{8,9},{9,8},{10,11... | collective-permute-start | bytes 12296 | tf_op jit(solution)/shard_map/b/ppermute | solution.py:197
  23.1 19.2 %collective-permute-start.11 = (bf16[48,2048]{1,0:T(8,128)(2,1)S(1)}, bf16[48,2048]{1,0:T(8,128)(2,1)S(1)}, u32[]{:S(2)}, u32[]{:S(2)}) collective-permute-start(bf16[48,2048]{1,0:T(8,128)(2,1)S(1)} %get-tuple-element.138.refs_0_), channel_id=1, source_target_pairs={{0,6},{1,7},{2,4},{3,5},{4,2},{5,3},{6,0},{7,1},{8,14},{9,15},{10,... | collective-permute-start | bytes 589832 | tf_op jit(solution)/shard_map/od/ppermute | solution.py:197
  33.1 10.8 %collective-permute-start.10 = (bf16[96,1024]{1,0:T(8,128)(2,1)S(1)}, bf16[96,1024]{1,0:T(8,128)(2,1)S(1)}, u32[]{:S(2)}, u32[]{:S(2)}) collective-permute-start(bf16[96,1024]{1,0:T(8,128)(2,1)S(1)} %slice.27), channel_id=1, source_target_pairs={{0,2},{1,3},{2,0},{3,1},{4,6},{5,7},{6,4},{7,5},{8,10},{9,11},{10,... | collective-permute-start | bytes 589832 | tf_op jit(solution)/shard_map/A2b/ppermute | solution.py:197
  33.2 10.7 %collective-permute-start.9 = (bf16[96,1024]{1,0:T(8,128)(2,1)S(1)}, bf16[96,1024]{1,0:T(8,128)(2,1)S(1)}, u32[]{:S(2)}, u32[]{:S(2)}) collective-permute-start(bf16[96,1024]{1,0:T(8,128)(2,1)S(1)} %slice.26), channel_id=1, source_target_pairs={{0,4},{1,5},{2,6},{3,7},{4,0},{5,1},{6,2},{7,3},{8,12},{9,13},{10,... | collective-permute-start | bytes 589832 | tf_op jit(solution)/shard_map/A2a/ppermute | solution.py:197
  35.3 11.5 %collective-permute-start.13 = (bf16[48,2048]{1,0:T(8,128)(2,1)S(1)}, bf16[48,2048]{1,0:T(8,128)(2,1)S(1)}, u32[]{:S(2)}, u32[]{:S(2)}) collective-permute-start(bf16[48,2048]{1,0:T(8,128)(2,1)S(1)} %collective-permute-done.12.refs_0_), channel_id=1, source_target_pairs={{0,2},{1,3},{2,0},{3,1},{4,6},{5,7},{6,4},{7,5},{8,10},{9,11},{10,... | collective-permute-start | bytes 589832 | tf_op jit(solution)/shard_map/B1x/ppermute | solution.py:197
  36.8 10.0 %collective-permute-start.14 = (bf16[48,2048]{1,0:T(8,128)(2,1)S(1)}, bf16[48,2048]{1,0:T(8,128)(2,1)S(1)}, u32[]{:S(2)}, u32[]{:S(2)}) collective-permute-start(bf16[48,2048]{1,0:T(8,128)(2,1)S(1)} %collective-permute-done.12.refs_0_), channel_id=1, source_target_pairs={{0,4},{1,5},{2,6},{3,7},{4,0},{5,1},{6,2},{7,3},{8,12},{9,13},{10,... | collective-permute-start | bytes 589832 | tf_op jit(solution)/shard_map/B1y/ppermute | solution.py:197
  42.4 7.2 %collective-permute-start.15 = (bf16[48,2048]{1,0:T(8,128)(2,1)S(1)}, bf16[48,2048]{1,0:T(8,128)(2,1)S(1)}, u32[]{:S(2)}, u32[]{:S(2)}) collective-permute-start(bf16[48,2048]{1,0:T(8,128)(2,1)S(1)} %collective-permute-done.12.refs_0_), channel_id=1, source_target_pairs={{0,6},{1,7},{2,4},{3,5},{4,2},{5,3},{6,0},{7,1},{8,14},{9,15},{10,... | collective-permute-start | bytes 589832 | tf_op jit(solution)/shard_map/bd/ppermute | solution.py:197
  46.8 6.4 %collective-permute-start.16 = (bf16[96,1024]{1,0:T(8,128)(2,1)S(1)}, bf16[96,1024]{1,0:T(8,128)(2,1)S(1)}, u32[]{:S(2)}, u32[]{:S(2)}) collective-permute-start(bf16[96,1024]{1,0:T(8,128)(2,1)S(1)} %get-tuple-element.125), channel_id=1, source_target_pairs={{0,4},{1,5},{2,6},{3,7},{4,0},{5,1},{6,2},{7,3},{8,12},{9,13},{10,... | collective-permute-start | bytes 589832 | tf_op jit(solution)/shard_map/AR1a/ppermute | solution.py:197
  46.9 6.3 %collective-permute-start.17 = (bf16[96,1024]{1,0:T(8,128)(2,1)S(1)}, bf16[96,1024]{1,0:T(8,128)(2,1)S(1)}, u32[]{:S(2)}, u32[]{:S(2)}) collective-permute-start(bf16[96,1024]{1,0:T(8,128)(2,1)S(1)} %get-tuple-element.126), channel_id=1, source_target_pairs={{0,2},{1,3},{2,0},{3,1},{4,6},{5,7},{6,4},{7,5},{8,10},{9,11},{10,... | collective-permute-start | bytes 589832 | tf_op jit(solution)/shard_map/AR1b/ppermute | solution.py:197
  53.2 12.7 %collective-permute-start.24 = (bf16[48,2048]{1,0:T(8,128)(2,1)S(1)}, bf16[48,2048]{1,0:T(8,128)(2,1)S(1)}, u32[]{:S(2)}, u32[]{:S(2)}) collective-permute-start(bf16[48,2048]{1,0:T(8,128)(2,1)S(1)} %get-tuple-element.135), channel_id=1, source_target_pairs={{0,2},{1,3},{2,0},{3,1},{4,6},{5,7},{6,4},{7,5},{8,10},{9,11},{10,... | collective-permute-start | bytes 589832 | tf_op jit(solution)/shard_map/BRx/ppermute | solution.py:197
  55.6 10.4 %collective-permute-start.25 = (bf16[48,2048]{1,0:T(8,128)(2,1)S(1)}, bf16[48,2048]{1,0:T(8,128)(2,1)S(1)}, u32[]{:S(2)}, u32[]{:S(2)}) collective-permute-start(bf16[48,2048]{1,0:T(8,128)(2,1)S(1)} %get-tuple-element.136), channel_id=1, source_target_pairs={{0,4},{1,5},{2,6},{3,7},{4,0},{5,1},{6,2},{7,3},{8,12},{9,13},{10,... | collective-permute-start | bytes 589832 | tf_op jit(solution)/shard_map/BRy/ppermute | solution.py:197
  58.5 9.1 %collective-permute-start.26 = (bf16[48,2048]{1,0:T(8,128)(2,1)S(1)}, bf16[48,2048]{1,0:T(8,128)(2,1)S(1)}, u32[]{:S(2)}, u32[]{:S(2)}) collective-permute-start(bf16[48,2048]{1,0:T(8,128)(2,1)S(1)} %get-tuple-element.137), channel_id=1, source_target_pairs={{0,6},{1,7},{2,4},{3,5},{4,2},{5,3},{6,0},{7,1},{8,14},{9,15},{10,... | collective-permute-start | bytes 589832 | tf_op jit(solution)/shard_map/BRd/ppermute | solution.py:197
  58.6 13.1 %collective-permute-start.19 = (bf16[96,2048]{1,0:T(8,128)(2,1)S(1)}, bf16[96,2048]{1,0:T(8,128)(2,1)S(1)}, u32[]{:S(2)}, u32[]{:S(2)}) collective-permute-start(bf16[96,2048]{1,0:T(8,128)(2,1)S(1)} %pad_maximum_fusion.1), channel_id=1, source_target_pairs={{0,4},{1,5},{2,6},{3,7},{4,0},{5,1},{6,2},{7,3},{8,12},{9,13},{10,... | collective-permute-start | bytes 1179656 | tf_op jit(solution)/shard_map/AR2y/ppermute | solution.py:197
  60.2 11.5 %collective-permute-start.18 = (bf16[96,2048]{1,0:T(8,128)(2,1)S(1)}, bf16[96,2048]{1,0:T(8,128)(2,1)S(1)}, u32[]{:S(2)}, u32[]{:S(2)}) collective-permute-start(bf16[96,2048]{1,0:T(8,128)(2,1)S(1)} %pad_maximum_fusion), channel_id=1, source_target_pairs={{0,2},{1,3},{2,0},{3,1},{4,6},{5,7},{6,4},{7,5},{8,10},{9,11},{10,... | collective-permute-start | bytes 1179656 | tf_op jit(solution)/shard_map/AR2x/ppermute | solution.py:197
  65.9 19.8 %copy-start = (bf16[64,2048]{1,0:T(8,128)(2,1)S(1)}, bf16[64,2048]{1,0:T(8,128)(2,1)}, u32[]{:S(2)}) copy-start(bf16[64,2048]{1,0:T(8,128)(2,1)} %tokens_ref.3) | copy-start | bytes 786436
  65.9 19.8 %copy-start.2 = (f32[4,2048]{1,0:T(4,128)S(1)}, f32[4,2048]{1,0:T(4,128)}, u32[]{:S(2)}) copy-start(f32[4,2048]{1,0:T(4,128)} %b_out_ref.1) | copy-start | bytes 98308
  65.9 19.7 %copy-start.3 = (s32[64,2]{0,1:T(2,128)S(1)}, s32[64,2]{0,1:T(2,128)}, u32[]{:S(2)}) copy-start(s32[64,2]{0,1:T(2,128)} %param.10) | copy-start | bytes 1540
  67.7 13.6 %collective-permute-start.27 = (bf16[48,2048]{1,0:T(8,128)(2,1)S(1)}, bf16[48,2048]{1,0:T(8,128)(2,1)S(1)}, u32[]{:S(2)}, u32[]{:S(2)}) collective-permute-start(bf16[48,2048]{1,0:T(8,128)(2,1)S(1)} %add_convert_fusion.1), channel_id=1, source_target_pairs={{0,16},{1,17},{2,18},{3,19},{4,20},{5,21},{6,22},{7,23},{8,24},{9,... | collective-permute-start | bytes 589832 | tf_op jit(solution)/shard_map/c2/ppermute | solution.py:200
  71.7 6.5 %collective-permute-start.20 = (bf16[48,2048]{1,0:T(8,128)(2,1)S(1)}, bf16[48,2048]{1,0:T(8,128)(2,1)S(1)}, u32[]{:S(2)}, u32[]{:S(2)}) collective-permute-start(bf16[48,2048]{1,0:T(8,128)(2,1)S(1)} %get-tuple-element.147), channel_id=1, source_target_pairs={{0,2},{1,3},{2,0},{3,1},{4,6},{5,7},{6,4},{7,5},{8,10},{9,11},{10,... | collective-permute-start | bytes 589832 | tf_op jit(solution)/shard_map/ORx/ppermute | solution.py:197
  73.1 8.1 %collective-permute-start.21 = (bf16[48,2048]{1,0:T(8,128)(2,1)S(1)}, bf16[48,2048]{1,0:T(8,128)(2,1)S(1)}, u32[]{:S(2)}, u32[]{:S(2)}) collective-permute-start(bf16[48,2048]{1,0:T(8,128)(2,1)S(1)} %get-tuple-element.148), channel_id=1, source_target_pairs={{0,4},{1,5},{2,6},{3,7},{4,0},{5,1},{6,2},{7,3},{8,12},{9,13},{10,... | collective-permute-start | bytes 589832 | tf_op jit(solution)/shard_map/ORy/ppermute | solution.py:197
  74.4 6.8 %collective-permute-start.22 = (bf16[48,2048]{1,0:T(8,128)(2,1)S(1)}, bf16[48,2048]{1,0:T(8,128)(2,1)S(1)}, u32[]{:S(2)}, u32[]{:S(2)}) collective-permute-start(bf16[48,2048]{1,0:T(8,128)(2,1)S(1)} %get-tuple-element.149), channel_id=1, source_target_pairs={{0,6},{1,7},{2,4},{3,5},{4,2},{5,3},{6,0},{7,1},{8,14},{9,15},{10,... | collective-permute-start | bytes 589832 | tf_op jit(solution)/shard_map/ORd/ppermute | solution.py:197
  75.3 7.0 %collective-permute-start.23 = (bf16[48,2048]{1,0:T(8,128)(2,1)S(1)}, bf16[48,2048]{1,0:T(8,128)(2,1)S(1)}, u32[]{:S(2)}, u32[]{:S(2)}) collective-permute-start(bf16[48,2048]{1,0:T(8,128)(2,1)S(1)} %get-tuple-element.158), channel_id=1, source_target_pairs={{0,24},{1,25},{2,26},{3,27},{4,28},{5,29},{6,30},{7,31},{8,0},{9,1... | collective-permute-start | bytes 589832 | tf_op jit(solution)/shard_map/c1/ppermute | solution.py:200
  78.2 7.5 %collective-permute-start.28 = (bf16[48,2048]{1,0:T(8,128)(2,1)S(1)}, bf16[48,2048]{1,0:T(8,128)(2,1)S(1)}, u32[]{:S(2)}, u32[]{:S(2)}) collective-permute-start(bf16[48,2048]{1,0:T(8,128)(2,1)S(1)} %get-tuple-element.157), channel_id=1, source_target_pairs={{0,8},{1,9},{2,10},{3,11},{4,12},{5,13},{6,14},{7,15},{8,16},{9,17... | collective-permute-start | bytes 589832 | tf_op jit(solution)/shard_map/c3/ppermute | solution.py:200
  (4 other events, 38.7 us)

commit v5 on v4

--- a/solution.py
+++ b/solution.py
@@ -55,8 +55,7 @@
     )(plane, in_hbm(ids.T), in_hbm(tokens), in_hbm(gain[None, :]), in_hbm(bias[None, :]))
 
 
-def combine_kernel(cap, experts, plane_ref, ids_ref, gates_ref, tokens_ref, b_out_ref, *refs):
-    row_refs, out_ref = refs[:-1], refs[-1]
+def routing_kernel(cap, experts, plane_ref, ids_ref, gates_ref, tokens_ref, b_out_ref, base_ref, gate_ref, *pick_refs):
     top, tok = ids_ref.shape
     named = lax.rem(plane_ref[0] + lax.broadcasted_iota(jnp.int32, (8, tok), 0), experts)
     member = jnp.zeros((8, tok), jnp.float32)
@@ -81,28 +80,49 @@
         preferred_element_type=jnp.float32,
     )
     rank, gate = flip(rank), flip(gate)
+    gate_ref[...] = gate
     slot = lax.broadcasted_iota(jnp.int32, (tok, cap), 1).astype(jnp.float32)
-    total = None
+    base = tokens_ref[...].astype(jnp.float32)
     for d in range(experts):
-        pick = jnp.where(slot == rank[:, d : d + 1], 1.0, 0.0).astype(jnp.bfloat16)
-        rows = jnp.dot(pick, row_refs[d][...], preferred_element_type=jnp.float32)
+        pick_refs[d][...] = jnp.where(slot == rank[:, d : d + 1], 1.0, 0.0).astype(jnp.bfloat16)
         bias = b_out_ref[pl.ds(lax.rem(plane_ref[0] + d, experts), 1), :]
-        term = gate[:, d : d + 1] * (rows + bias)
-        total = term if total is None else total + term
-    out_ref[...] = (tokens_ref[...].astype(jnp.float32) + total).astype(jnp.bfloat16)
-
-
-def combine(plane, ids, gates, tokens, b_out, rows, cap):
-    experts = b_out.shape[0]
+        base += gate[:, d : d + 1] * bias
+    base_ref[...] = base
+
+
+def routing(plane, ids, gates, tokens, b_out, cap):
+    experts, tok = b_out.shape[0], tokens.shape[0]
     vmem = pl.BlockSpec(memory_space=pltpu.VMEM)
     return pl.pallas_call(
-        functools.partial(combine_kernel, cap, experts),
-        out_shape=jax.ShapeDtypeStruct(tokens.shape, jnp.bfloat16),
-        in_specs=[pl.BlockSpec(memory_space=pltpu.SMEM)] + [vmem] * (4 + experts),
+        functools.partial(routing_kernel, cap, experts),
+        out_shape=[pltpu.VMEM(tokens.shape, jnp.float32), pltpu.VMEM((tok, 8), jnp.float32)]
+        + [pltpu.VMEM((tok, cap), jnp.bfloat16)] * experts,
+        in_specs=[pl.BlockSpec(memory_space=pltpu.SMEM)] + [vmem] * 4,
+        out_specs=[vmem] * (2 + experts),
+        compiler_params=pltpu.CompilerParams(vmem_limit_bytes=8 << 20),
+        name="routing",
+    )(plane, in_hbm(ids.T), in_hbm(gates.T), in_hbm(tokens), in_hbm(b_out))
+
+
+def combine_kernel(base_ref, gate_ref, *refs):
+    experts = len(refs) // 2
+    total = base_ref[...]
+    for d in range(experts):
+        rows = jnp.dot(refs[d][...], refs[experts + d][...], preferred_element_type=jnp.float32)
+        total += gate_ref[:, d : d + 1] * rows
+    refs[-1][...] = total.astype(jnp.bfloat16)
+
+
+def combine(routed, rows):
+    vmem = pl.BlockSpec(memory_space=pltpu.VMEM)
+    return pl.pallas_call(
+        combine_kernel,
+        out_shape=jax.ShapeDtypeStruct(routed[0].shape, jnp.bfloat16),
+        in_specs=[vmem] * (len(routed) + len(rows)),
         out_specs=vmem,
         compiler_params=pltpu.CompilerParams(vmem_limit_bytes=8 << 20),
         name="combine",
-    )(plane, ids.T, gates.T, in_vmem(tokens), b_out, *[in_vmem(value) for value in rows])
+    )(*[in_vmem(value) for value in (*routed, *rows)])
 
 
 def stage_kernel(*refs):
@@ -233,11 +253,12 @@
     put("ox", across, own, 2)
     put("oy", across, own, 4)
     put("od", across, own, 6)
-    sent["mine"], sent["own"] = [w_in, w_out], own
-    join("mine", "own")
+    sent["mine"], sent["own"], sent["plane"] = [w_in, w_out], own, plane
+    join("mine", "own", "plane")
     put("K", stage, *sent["mine"])
+    put("P", routing, sent["plane"], expert_ids, gate_weights, tokens, b_out, slot_cap)
     sent["out"], sent["bias"], sent["blocks"] = w_out, b_in, [blocks[d] for d in far]
-    join("own", "out", "bias", "blocks", ordered=("z1", "z3", "ox", "oy", "w1", "K"))
+    join("P", "own", "out", "bias", "blocks", ordered=("z1", "z3", "ox", "oy", "w1", "K"))
     mine_in, mine_out = sent["K"]
     near_rows = jnp.concatenate([sent["z1"], sent["z3"]][: len(near)])
     put("w2", across, sent["out"], 1)
@@ -285,7 +306,7 @@
     rows[near[0]], rows[near[-1]] = sent["c1"], sent["c3"]
     rows[0] = total(sent["EO"], sent["ORx"], sent["ORy"], sent["ORd"])
     results = [rows[d] for d in range(experts)]
-    return combine(plane, expert_ids, gate_weights, tokens, b_out, results, slot_cap)
+    return combine(sent["P"], results)
 
 
 def solution(mesh):

time: 87.4 us -> 87 us (level)
  waiting for transfers between devices: 20.2 us -> 18.7 us
  Pallas kernels: 25.2 us -> 26.4 us
    ppermute x6, waiting for transfers between devices: 6.73 us -> 5.12 us  [along(): lax.ppermute(value, 'local', [(i, (i + planes * shared) % devices) for i...]
    pallas_call x1 -> x2, Pallas kernels: 1.53 us -> 2.75 us  [the longest x1 1.61 us: routing(): pl.pallas_call(functools.partial(routing_kernel, cap, experts), out_shape...]
  transfers between devices with their start and end apart: 29 -> 29, of which waited for: 10 -> 10; matrix products, arithmetic and copies ran while one was open for 1% -> 1% of each run, Pallas kernels for 27% -> 29%
where the time goes in v5:
time: 87 us; the launch traced here: 86.8 us
  starting transfers between devices  40.9 us (47%)
  Pallas kernels  26.4 us (30%)
  waiting for transfers between devices  18.7 us (21%)
    ppermute x23, starting transfers between devices, across(): return lax.ppermute(value, 'local', [(i, i ^ bit) for i in range(devices)])  30 us
    pallas_call x4, Pallas kernels, expert_rows(): pl.pallas_call(functools.partial(expert_kernel, 512), out_shape=[pltpu.VM...  15 us
    ppermute x23, waiting for transfers between devices, across(): return lax.ppermute(value, 'local', [(i, i ^ bit) for i in range(devices)])  13.5 us
    ppermute x6, starting transfers between devices, along(): lax.ppermute(value, 'local', [(i, (i + planes * shared) % devices) for i...  10.8 us
    pallas_call x2, Pallas kernels, stage(): pl.pallas_call(stage_kernel, out_shape=[pltpu.VMEM(array.shape, array.dty...  7.1 us
    ppermute x6, waiting for transfers between devices, along(): lax.ppermute(value, 'local', [(i, (i + planes * shared) % devices) for i...  5.12 us
  transfers between devices with their start and end apart: 29, of which 10 were waited for; matrix products, arithmetic and copies ran while one was open for 1% of the time, Pallas kernels for 29%

profile of v5, /device:TPU:0, one launch (start us, length us, event | category | flops | bytes accessed | tf_op | source)
XLA Modules:
  0.0 86.8 jit_solution(637686321093622385)
XLA Ops:
  0.5 1.6 %dispatch.1 = (bf16[48,2048]{1,0:T(8,128)(2,1)S(1)}, bf16[48,2048]{1,0:T(8,128)(2,1)S(1)}, bf16[48,2048]{1,0:T(8,128)(2,1)S(1)}, bf16[48,2048]{1,0:T(8,128)(2,1)S(1)}) custom-call(s32[1]{0:T(128)} %bitcast.2.plane_ref, s32[2,64]{1,0:T(2,128)} %bitcast.13, bf16[64,2048]{1,0:T(8,128)(2,1)} %tokens_ref.3, f32[1,2048]{1,0:T(1,128)} %bitcast.11, f32[1,2048]{1,0:T(1,128)} %bitcast.12), custom_call_target="tpu_custom_call" | custom-call | tf_op jit(solution)/shard_map/dispatch/pallas_call | solution.py:48
  2.0 2.6 %collective-permute-start = (bf16[48,2048]{1,0:T(8,128)(2,1)S(1)}, bf16[48,2048]{1,0:T(8,128)(2,1)S(1)}, u32[]{:S(2)}, u32[]{:S(2)}) collective-permute-start(bf16[48,2048]{1,0:T(8,128)(2,1)S(1)} %get-tuple-element.104), channel_id=1, source_target_pairs={{0,8},{1,9},{2,10},{3,11},{4,12},{5,13},{6,14},{7,15},{8,16},{9,17... | collective-permute-start | bytes 589832 | tf_op jit(solution)/shard_map/z1/ppermute | solution.py:220
  4.6 2.1 %collective-permute-start.1 = (bf16[48,2048]{1,0:T(8,128)(2,1)S(1)}, bf16[48,2048]{1,0:T(8,128)(2,1)S(1)}, u32[]{:S(2)}, u32[]{:S(2)}) collective-permute-start(bf16[48,2048]{1,0:T(8,128)(2,1)S(1)} %get-tuple-element.105), channel_id=1, source_target_pairs={{0,24},{1,25},{2,26},{3,27},{4,28},{5,29},{6,30},{7,31},{8,0},{9,1... | collective-permute-start | bytes 589832 | tf_op jit(solution)/shard_map/z3/ppermute | solution.py:220
  6.7 1.6 %collective-permute-start.2 = (bf16[48,2048]{1,0:T(8,128)(2,1)S(1)}, bf16[48,2048]{1,0:T(8,128)(2,1)S(1)}, u32[]{:S(2)}, u32[]{:S(2)}) collective-permute-start(bf16[48,2048]{1,0:T(8,128)(2,1)S(1)} %get-tuple-element.164.refs_0_), channel_id=1, source_target_pairs={{0,2},{1,3},{2,0},{3,1},{4,6},{5,7},{6,4},{7,5},{8,10},{9,11},{10,... | collective-permute-start | bytes 589832 | tf_op jit(solution)/shard_map/ox/ppermute | solution.py:217
  8.4 1.5 %collective-permute-start.3 = (bf16[48,2048]{1,0:T(8,128)(2,1)S(1)}, bf16[48,2048]{1,0:T(8,128)(2,1)S(1)}, u32[]{:S(2)}, u32[]{:S(2)}) collective-permute-start(bf16[48,2048]{1,0:T(8,128)(2,1)S(1)} %get-tuple-element.164.refs_0_), channel_id=1, source_target_pairs={{0,4},{1,5},{2,6},{3,7},{4,0},{5,1},{6,2},{7,3},{8,12},{9,13},{10,... | collective-permute-start | bytes 589832 | tf_op jit(solution)/shard_map/oy/ppermute | solution.py:217
  9.9 3.6 %stage.2 = (bf16[2048,1024]{1,0:T(8,128)(2,1)S(1)}, bf16[1024,2048]{1,0:T(8,128)(2,1)S(1)}) custom-call(bf16[2048,1024]{1,0:T(8,128)(2,1)} %bitcast.8, bf16[1024,2048]{1,0:T(8,128)(2,1)} %bitcast.9), custom_call_target="tpu_custom_call" | custom-call | tf_op jit(solution)/shard_map/K/stage/pallas_call | solution.py:139
  13.5 1.6 %routing.1 = (f32[64,2048]{1,0:T(8,128)S(1)}, f32[64,8]{1,0:T(8,128)S(1)}, bf16[64,48]{1,0:T(8,128)(2,1)S(1)}, bf16[64,48]{1,0:T(8,128)(2,1)S(1)}, bf16[64,48]{1...) custom-call(s32[1]{0:T(128)} %bitcast.2.plane_ref, s32[2,64]{1,0:T(2,128)} %bitcast.14, f32[2,64]{1,0:T(2,128)} %bitcast.15, ...), custom_call_target="tpu_custom_call" | custom-call | tf_op jit(solution)/shard_map/P/routing/pallas_call | solution.py:96
  16.0 1.6 %collective-permute-start.5 = (bf16[96,2048]{1,0:T(8,128)(2,1)S(1)}, bf16[96,2048]{1,0:T(8,128)(2,1)S(1)}, u32[]{:S(2)}, u32[]{:S(2)}) collective-permute-start(bf16[96,2048]{1,0:T(8,128)(2,1)S(1)} %constant_dynamic-update-slice_fusion.refs_0_), channel_id=1, source_target_pairs={{0,2},{1,3},{2,0},{3,1},{4,6},{5,7},{6,4},{7,5},{8,10},{9,11},{10,... | collective-permute-start | bytes 1179656 | tf_op jit(solution)/shard_map/A1x/ppermute | solution.py:217
  17.6 1.5 %collective-permute-start.6 = (bf16[96,2048]{1,0:T(8,128)(2,1)S(1)}, bf16[96,2048]{1,0:T(8,128)(2,1)S(1)}, u32[]{:S(2)}, u32[]{:S(2)}) collective-permute-start(bf16[96,2048]{1,0:T(8,128)(2,1)S(1)} %constant_dynamic-update-slice_fusion.refs_0_), channel_id=1, source_target_pairs={{0,4},{1,5},{2,6},{3,7},{4,0},{5,1},{6,2},{7,3},{8,12},{9,13},{10,... | collective-permute-start | bytes 1179656 | tf_op jit(solution)/shard_map/A1y/ppermute | solution.py:217
  20.4 2.7 %collective-permute-done.7.refs_1_ = bf16[1024,2048]{1,0:T(8,128)(2,1)S(1)} collective-permute-done((bf16[1024,2048]{1,0:T(8,128)(2,1)S(1)}, bf16[1024,2048]{1,0:T(8,128)(2,1)S(1)}, u32[]{:S(2)}, u32[]{:S(2)}) %collective-permute-start.7) | collective-permute-done | bytes 4194336 | tf_op jit(solution)/shard_map/w2/ppermute | solution.py:217
  23.1 2.4 %collective-permute-start.11 = (bf16[48,2048]{1,0:T(8,128)(2,1)S(1)}, bf16[48,2048]{1,0:T(8,128)(2,1)S(1)}, u32[]{:S(2)}, u32[]{:S(2)}) collective-permute-start(bf16[48,2048]{1,0:T(8,128)(2,1)S(1)} %get-tuple-element.164.refs_0_), channel_id=1, source_target_pairs={{0,6},{1,7},{2,4},{3,5},{4,2},{5,3},{6,0},{7,1},{8,14},{9,15},{10,... | collective-permute-start | bytes 589832 | tf_op jit(solution)/shard_map/od/ppermute | solution.py:217
  25.6 3.5 %stage.3 = (bf16[2048,1024]{1,0:T(8,128)(2,1)S(1)}, bf16[1024,2048]{1,0:T(8,128)(2,1)S(1)}) custom-call(bf16[2048,1024]{1,0:T(8,128)(2,1)} %collective-permute-done.4.refs_0_, bf16[1024,2048]{1,0:T(8,128)(2,1)} %copy-done.2), custom_call_target="tpu_custom_call" | custom-call | tf_op jit(solution)/shard_map/K2/stage/pallas_call | solution.py:139
  29.1 3.9 %collective-permute-done.6.refs_2_ = bf16[96,2048]{1,0:T(8,128)(2,1)S(1)} collective-permute-done((bf16[96,2048]{1,0:T(8,128)(2,1)S(1)}, bf16[96,2048]{1,0:T(8,128)(2,1)S(1)}, u32[]{:S(2)}, u32[]{:S(2)}) %collective-permute-start.6) | collective-permute-done | bytes 393248 | tf_op jit(solution)/shard_map/A1y/ppermute | solution.py:217
  33.2 2.1 %collective-permute-start.9 = (bf16[96,1024]{1,0:T(8,128)(2,1)S(1)}, bf16[96,1024]{1,0:T(8,128)(2,1)S(1)}, u32[]{:S(2)}, u32[]{:S(2)}) collective-permute-start(bf16[96,1024]{1,0:T(8,128)(2,1)S(1)} %slice.26), channel_id=1, source_target_pairs={{0,4},{1,5},{2,6},{3,7},{4,0},{5,1},{6,2},{7,3},{8,12},{9,13},{10,... | collective-permute-start | bytes 589832 | tf_op jit(solution)/shard_map/A2a/ppermute | solution.py:217
  35.3 1.5 %collective-permute-start.13 = (bf16[48,2048]{1,0:T(8,128)(2,1)S(1)}, bf16[48,2048]{1,0:T(8,128)(2,1)S(1)}, u32[]{:S(2)}, u32[]{:S(2)}) collective-permute-start(bf16[48,2048]{1,0:T(8,128)(2,1)S(1)} %collective-permute-done.12.refs_0_), channel_id=1, source_target_pairs={{0,2},{1,3},{2,0},{3,1},{4,6},{5,7},{6,4},{7,5},{8,10},{9,11},{10,... | collective-permute-start | bytes 589832 | tf_op jit(solution)/shard_map/B1x/ppermute | solution.py:217
  37.3 5.1 %expert.4 = (f32[96,2048]{1,0:T(8,128)S(1)}, f32[96,2048]{1,0:T(8,128)S(1)}, f32[96,2048]{1,0:T(8,128)S(1)}) custom-call(bf16[96,2048]{1,0:T(8,128)(2,1)S(1)} %constant_dynamic-update-slice_fusion.refs_0_, bf16[96,2048]{1,0:T(8,128)(2,1)S(1)} %collective-permute-done.5.refs_1_, bf16[96,2048]{1,0:T(8,128)(2,1)S(1)} %collective-permute-done.6.refs_2_, ...), custom_call_target="tpu_custom_call" | custom-call | tf_op jit(solution)/shard_map/EA1/expert/pallas_call | solution.py:192
  42.4 1.5 %collective-permute-start.15 = (bf16[48,2048]{1,0:T(8,128)(2,1)S(1)}, bf16[48,2048]{1,0:T(8,128)(2,1)S(1)}, u32[]{:S(2)}, u32[]{:S(2)}) collective-permute-start(bf16[48,2048]{1,0:T(8,128)(2,1)S(1)} %collective-permute-done.12.refs_0_), channel_id=1, source_target_pairs={{0,6},{1,7},{2,4},{3,5},{4,2},{5,3},{6,0},{7,1},{8,14},{9,15},{10,... | collective-permute-start | bytes 589832 | tf_op jit(solution)/shard_map/bd/ppermute | solution.py:217
  43.9 2.8 %expert.5 = (bf16[96,1024]{1,0:T(8,128)(2,1)S(1)}, bf16[96,1024]{1,0:T(8,128)(2,1)S(1)}) custom-call(bf16[96,1024]{1,0:T(8,128)(2,1)S(1)} %collective-permute-done.9.refs_0_, bf16[96,1024]{1,0:T(8,128)(2,1)S(1)} %collective-permute-done.10.refs_1_, bf16[2048,1024]{1,0:T(8,128)(2,1)S(1)} %get-tuple-element.131.refs_3_.refs_2_.refs_4_, ...), custom_call_target="tpu_custom_call" | custom-call | tf_op jit(solution)/shard_map/EA2/expert/pallas_call | solution.py:192
  46.9 2.6 %collective-permute-start.17 = (bf16[96,1024]{1,0:T(8,128)(2,1)S(1)}, bf16[96,1024]{1,0:T(8,128)(2,1)S(1)}, u32[]{:S(2)}, u32[]{:S(2)}) collective-permute-start(bf16[96,1024]{1,0:T(8,128)(2,1)S(1)} %get-tuple-element.152), channel_id=1, source_target_pairs={{0,2},{1,3},{2,0},{3,1},{4,6},{5,7},{6,4},{7,5},{8,10},{9,11},{10,... | collective-permute-start | bytes 589832 | tf_op jit(solution)/shard_map/AR1b/ppermute | solution.py:217
  49.6 3.5 %expert.6 = (f32[48,2048]{1,0:T(8,128)S(1)}, bf16[48,2048]{1,0:T(8,128)(2,1)S(1)}, bf16[48,2048]{1,0:T(8,128)(2,1)S(1)}, bf16[48,2048]{1,0:T(8,128)(2,1)S(1)}) custom-call(bf16[48,2048]{1,0:T(8,128)(2,1)S(1)} %collective-permute-done.12.refs_0_, bf16[48,2048]{1,0:T(8,128)(2,1)S(1)} %collective-permute-done.13.refs_1_, ...), custom_call_target="tpu_custom_call" | custom-call | tf_op jit(solution)/shard_map/EB/expert/pallas_call | solution.py:192
  53.2 2.3 %collective-permute-start.24 = (bf16[48,2048]{1,0:T(8,128)(2,1)S(1)}, bf16[48,2048]{1,0:T(8,128)(2,1)S(1)}, u32[]{:S(2)}, u32[]{:S(2)}) collective-permute-start(bf16[48,2048]{1,0:T(8,128)(2,1)S(1)} %get-tuple-element.161), channel_id=1, source_target_pairs={{0,2},{1,3},{2,0},{3,1},{4,6},{5,7},{6,4},{7,5},{8,10},{9,11},{10,... | collective-permute-start | bytes 589832 | tf_op jit(solution)/shard_map/BRx/ppermute | solution.py:217
  55.6 2.9 %collective-permute-start.25 = (bf16[48,2048]{1,0:T(8,128)(2,1)S(1)}, bf16[48,2048]{1,0:T(8,128)(2,1)S(1)}, u32[]{:S(2)}, u32[]{:S(2)}) collective-permute-start(bf16[48,2048]{1,0:T(8,128)(2,1)S(1)} %get-tuple-element.162), channel_id=1, source_target_pairs={{0,4},{1,5},{2,6},{3,7},{4,0},{5,1},{6,2},{7,3},{8,12},{9,13},{10,... | collective-permute-start | bytes 589832 | tf_op jit(solution)/shard_map/BRy/ppermute | solution.py:217
  58.6 1.5 %collective-permute-start.19 = (bf16[96,2048]{1,0:T(8,128)(2,1)S(1)}, bf16[96,2048]{1,0:T(8,128)(2,1)S(1)}, u32[]{:S(2)}, u32[]{:S(2)}) collective-permute-start(bf16[96,2048]{1,0:T(8,128)(2,1)S(1)} %pad_maximum_fusion.1), channel_id=1, source_target_pairs={{0,4},{1,5},{2,6},{3,7},{4,0},{5,1},{6,2},{7,3},{8,12},{9,13},{10,... | collective-permute-start | bytes 1179656 | tf_op jit(solution)/shard_map/AR2y/ppermute | solution.py:217
  60.2 2.1 %collective-permute-start.18 = (bf16[96,2048]{1,0:T(8,128)(2,1)S(1)}, bf16[96,2048]{1,0:T(8,128)(2,1)S(1)}, u32[]{:S(2)}, u32[]{:S(2)}) collective-permute-start(bf16[96,2048]{1,0:T(8,128)(2,1)S(1)} %pad_maximum_fusion), channel_id=1, source_target_pairs={{0,2},{1,3},{2,0},{3,1},{4,6},{5,7},{6,4},{7,5},{8,10},{9,11},{10,... | collective-permute-start | bytes 1179656 | tf_op jit(solution)/shard_map/AR2x/ppermute | solution.py:217
  62.3 3.6 %expert.7 = (f32[48,2048]{1,0:T(8,128)S(1)}, bf16[48,2048]{1,0:T(8,128)(2,1)S(1)}, bf16[48,2048]{1,0:T(8,128)(2,1)S(1)}, bf16[48,2048]{1,0:T(8,128)(2,1)S(1)}) custom-call(bf16[48,2048]{1,0:T(8,128)(2,1)S(1)} %get-tuple-element.164.refs_0_, bf16[48,2048]{1,0:T(8,128)(2,1)S(1)} %collective-permute-done.2.refs_1_, ...), custom_call_target="tpu_custom_call" | custom-call | tf_op jit(solution)/shard_map/EO/expert/pallas_call | solution.py:192
  65.9 1.6 %collective-permute-done.26 = bf16[48,2048]{1,0:T(8,128)(2,1)S(1)} collective-permute-done((bf16[48,2048]{1,0:T(8,128)(2,1)S(1)}, bf16[48,2048]{1,0:T(8,128)(2,1)S(1)}, u32[]{:S(2)}, u32[]{:S(2)}) %collective-permute-start.26) | collective-permute-done | bytes 196640 | tf_op jit(solution)/shard_map/BRd/ppermute | solution.py:217
  67.7 1.4 %collective-permute-start.27 = (bf16[48,2048]{1,0:T(8,128)(2,1)S(1)}, bf16[48,2048]{1,0:T(8,128)(2,1)S(1)}, u32[]{:S(2)}, u32[]{:S(2)}) collective-permute-start(bf16[48,2048]{1,0:T(8,128)(2,1)S(1)} %add_convert_fusion.1), channel_id=1, source_target_pairs={{0,16},{1,17},{2,18},{3,19},{4,20},{5,21},{6,22},{7,23},{8,24},{9,... | collective-permute-start | bytes 589832 | tf_op jit(solution)/shard_map/c2/ppermute | solution.py:220
  69.1 2.6 %collective-permute-done.19 = bf16[96,2048]{1,0:T(8,128)(2,1)S(1)} collective-permute-done((bf16[96,2048]{1,0:T(8,128)(2,1)S(1)}, bf16[96,2048]{1,0:T(8,128)(2,1)S(1)}, u32[]{:S(2)}, u32[]{:S(2)}) %collective-permute-start.19) | collective-permute-done | bytes 393248 | tf_op jit(solution)/shard_map/AR2y/ppermute | solution.py:217
  71.7 1.4 %collective-permute-start.20 = (bf16[48,2048]{1,0:T(8,128)(2,1)S(1)}, bf16[48,2048]{1,0:T(8,128)(2,1)S(1)}, u32[]{:S(2)}, u32[]{:S(2)}) collective-permute-start(bf16[48,2048]{1,0:T(8,128)(2,1)S(1)} %get-tuple-element.173), channel_id=1, source_target_pairs={{0,2},{1,3},{2,0},{3,1},{4,6},{5,7},{6,4},{7,5},{8,10},{9,11},{10,... | collective-permute-start | bytes 589832 | tf_op jit(solution)/shard_map/ORx/ppermute | solution.py:217
  75.3 2.4 %collective-permute-start.23 = (bf16[48,2048]{1,0:T(8,128)(2,1)S(1)}, bf16[48,2048]{1,0:T(8,128)(2,1)S(1)}, u32[]{:S(2)}, u32[]{:S(2)}) collective-permute-start(bf16[48,2048]{1,0:T(8,128)(2,1)S(1)} %get-tuple-element.184), channel_id=1, source_target_pairs={{0,24},{1,25},{2,26},{3,27},{4,28},{5,29},{6,30},{7,31},{8,0},{9,1... | collective-permute-start | bytes 589832 | tf_op jit(solution)/shard_map/c1/ppermute | solution.py:220
  79.3 1.9 %collective-permute-done.21 = bf16[48,2048]{1,0:T(8,128)(2,1)S(1)} collective-permute-done((bf16[48,2048]{1,0:T(8,128)(2,1)S(1)}, bf16[48,2048]{1,0:T(8,128)(2,1)S(1)}, u32[]{:S(2)}, u32[]{:S(2)}) %collective-permute-start.21) | collective-permute-done | bytes 196640 | tf_op jit(solution)/shard_map/ORy/ppermute | solution.py:217
  82.3 3.3 %collective-permute-done.28.refs_7_ = bf16[48,2048]{1,0:T(8,128)(2,1)S(1)} collective-permute-done((bf16[48,2048]{1,0:T(8,128)(2,1)S(1)}, bf16[48,2048]{1,0:T(8,128)(2,1)S(1)}, u32[]{:S(2)}, u32[]{:S(2)}) %collective-permute-start.28) | collective-permute-done | bytes 196640 | tf_op jit(solution)/shard_map/c3/ppermute | solution.py:220
  (55 shorter events, 10.0 us)
Async XLA Ops:
  0.0 15.9 %collective-permute-start.4 = (bf16[2048,1024]{1,0:T(8,128)(2,1)}, bf16[2048,1024]{1,0:T(8,128)(2,1)}, u32[]{:S(2)}, u32[]{:S(2)}) collective-permute-start(bf16[2048,1024]{1,0:T(8,128)(2,1)} %bitcast.7), channel_id=1, source_target_pairs={{0,1},{1,0},{2,3},{3,2},{4,5},{5,4},{6,7},{7,6},{8,9},{9,8},{10,11... | collective-permute-start | bytes 12582920 | tf_op jit(solution)/shard_map/w1/ppermute | solution.py:217
  2.0 13.1 %collective-permute-start = (bf16[48,2048]{1,0:T(8,128)(2,1)S(1)}, bf16[48,2048]{1,0:T(8,128)(2,1)S(1)}, u32[]{:S(2)}, u32[]{:S(2)}) collective-permute-start(bf16[48,2048]{1,0:T(8,128)(2,1)S(1)} %get-tuple-element.104), channel_id=1, source_target_pairs={{0,8},{1,9},{2,10},{3,11},{4,12},{5,13},{6,14},{7,15},{8,16},{9,17... | collective-permute-start | bytes 589832 | tf_op jit(solution)/shard_map/z1/ppermute | solution.py:220
  4.6 11.2 %collective-permute-start.1 = (bf16[48,2048]{1,0:T(8,128)(2,1)S(1)}, bf16[48,2048]{1,0:T(8,128)(2,1)S(1)}, u32[]{:S(2)}, u32[]{:S(2)}) collective-permute-start(bf16[48,2048]{1,0:T(8,128)(2,1)S(1)} %get-tuple-element.105), channel_id=1, source_target_pairs={{0,24},{1,25},{2,26},{3,27},{4,28},{5,29},{6,30},{7,31},{8,0},{9,1... | collective-permute-start | bytes 589832 | tf_op jit(solution)/shard_map/z3/ppermute | solution.py:220
  6.7 9.2 %collective-permute-start.2 = (bf16[48,2048]{1,0:T(8,128)(2,1)S(1)}, bf16[48,2048]{1,0:T(8,128)(2,1)S(1)}, u32[]{:S(2)}, u32[]{:S(2)}) collective-permute-start(bf16[48,2048]{1,0:T(8,128)(2,1)S(1)} %get-tuple-element.164.refs_0_), channel_id=1, source_target_pairs={{0,2},{1,3},{2,0},{3,1},{4,6},{5,7},{6,4},{7,5},{8,10},{9,11},{10,... | collective-permute-start | bytes 589832 | tf_op jit(solution)/shard_map/ox/ppermute | solution.py:217
  8.4 7.5 %collective-permute-start.3 = (bf16[48,2048]{1,0:T(8,128)(2,1)S(1)}, bf16[48,2048]{1,0:T(8,128)(2,1)S(1)}, u32[]{:S(2)}, u32[]{:S(2)}) collective-permute-start(bf16[48,2048]{1,0:T(8,128)(2,1)S(1)} %get-tuple-element.164.refs_0_), channel_id=1, source_target_pairs={{0,4},{1,5},{2,6},{3,7},{4,0},{5,1},{6,2},{7,3},{8,12},{9,13},{10,... | collective-permute-start | bytes 589832 | tf_op jit(solution)/shard_map/oy/ppermute | solution.py:217
  9.9 6.0 %copy-start.1 = (bf16[1,1024,2048]{2,1,0:T(8,128)(2,1)S(1)}, bf16[1,1024,2048]{2,1,0:T(8,128)(2,1)}, u32[]{:S(2)}) copy-start(bf16[1,1024,2048]{2,1,0:T(8,128)(2,1)} %param.16) | copy-start | bytes 12582916
  9.9 10.5 %copy-start = (f32[1,1024]{1,0:T(1,128)S(1)}, f32[1,1024]{1,0:T(1,128)}, u32[]{:S(2)}) copy-start(f32[1,1024]{1,0:T(1,128)} %refs_6_.3) | copy-start | bytes 12292
  15.9 7.2 %collective-permute-start.7 = (bf16[1024,2048]{1,0:T(8,128)(2,1)S(1)}, bf16[1024,2048]{1,0:T(8,128)(2,1)S(1)}, u32[]{:S(2)}, u32[]{:S(2)}) collective-permute-start(bf16[1024,2048]{1,0:T(8,128)(2,1)S(1)} %bitcast.10), channel_id=1, source_target_pairs={{0,1},{1,0},{2,3},{3,2},{4,5},{5,4},{6,7},{7,6},{8,9},{9,8},{10,11... | collective-permute-start | bytes 12582920 | tf_op jit(solution)/shard_map/w2/ppermute | solution.py:217
  16.0 13.1 %collective-permute-start.5 = (bf16[96,2048]{1,0:T(8,128)(2,1)S(1)}, bf16[96,2048]{1,0:T(8,128)(2,1)S(1)}, u32[]{:S(2)}, u32[]{:S(2)}) collective-permute-start(bf16[96,2048]{1,0:T(8,128)(2,1)S(1)} %constant_dynamic-update-slice_fusion.refs_0_), channel_id=1, source_target_pairs={{0,2},{1,3},{2,0},{3,1},{4,6},{5,7},{6,4},{7,5},{8,10},{9,11},{10,... | collective-permute-start | bytes 1179656 | tf_op jit(solution)/shard_map/A1x/ppermute | solution.py:217
  17.6 15.4 %collective-permute-start.6 = (bf16[96,2048]{1,0:T(8,128)(2,1)S(1)}, bf16[96,2048]{1,0:T(8,128)(2,1)S(1)}, u32[]{:S(2)}, u32[]{:S(2)}) collective-permute-start(bf16[96,2048]{1,0:T(8,128)(2,1)S(1)} %constant_dynamic-update-slice_fusion.refs_0_), channel_id=1, source_target_pairs={{0,4},{1,5},{2,6},{3,7},{4,0},{5,1},{6,2},{7,3},{8,12},{9,13},{10,... | collective-permute-start | bytes 1179656 | tf_op jit(solution)/shard_map/A1y/ppermute | solution.py:217
  19.1 16.1 %collective-permute-start.12 = (bf16[48,2048]{1,0:T(8,128)(2,1)S(1)}, bf16[48,2048]{1,0:T(8,128)(2,1)S(1)}, u32[]{:S(2)}, u32[]{:S(2)}) collective-permute-start(bf16[48,2048]{1,0:T(8,128)(2,1)S(1)} %get-tuple-element.140), channel_id=1, source_target_pairs={{0,16},{1,17},{2,18},{3,19},{4,20},{5,21},{6,22},{7,23},{8,24},{9,... | collective-permute-start | bytes 589832 | tf_op jit(solution)/shard_map/z2/ppermute | solution.py:220
  20.4 8.7 %collective-permute-start.8 = (f32[1,1024]{1,0:T(1,128)S(1)}, f32[1,1024]{1,0:T(1,128)S(1)}, u32[]{:S(2)}, u32[]{:S(2)}) collective-permute-start(f32[1,1024]{1,0:T(1,128)S(1)} %copy-done), channel_id=1, source_target_pairs={{0,1},{1,0},{2,3},{3,2},{4,5},{5,4},{6,7},{7,6},{8,9},{9,8},{10,11... | collective-permute-start | bytes 12296 | tf_op jit(solution)/shard_map/b/ppermute | solution.py:217
  23.1 2.5 %copy-start.2 = (bf16[1024,2048]{1,0:T(8,128)(2,1)}, bf16[1024,2048]{1,0:T(8,128)(2,1)S(1)}, u32[]{:S(2)}) copy-start(bf16[1024,2048]{1,0:T(8,128)(2,1)S(1)} %collective-permute-done.7.refs_1_) | copy-start | bytes 12582916
  23.1 19.2 %collective-permute-start.11 = (bf16[48,2048]{1,0:T(8,128)(2,1)S(1)}, bf16[48,2048]{1,0:T(8,128)(2,1)S(1)}, u32[]{:S(2)}, u32[]{:S(2)}) collective-permute-start(bf16[48,2048]{1,0:T(8,128)(2,1)S(1)} %get-tuple-element.164.refs_0_), channel_id=1, source_target_pairs={{0,6},{1,7},{2,4},{3,5},{4,2},{5,3},{6,0},{7,1},{8,14},{9,15},{10,... | collective-permute-start | bytes 589832 | tf_op jit(solution)/shard_map/od/ppermute | solution.py:217
  33.1 10.8 %collective-permute-start.10 = (bf16[96,1024]{1,0:T(8,128)(2,1)S(1)}, bf16[96,1024]{1,0:T(8,128)(2,1)S(1)}, u32[]{:S(2)}, u32[]{:S(2)}) collective-permute-start(bf16[96,1024]{1,0:T(8,128)(2,1)S(1)} %slice.27), channel_id=1, source_target_pairs={{0,2},{1,3},{2,0},{3,1},{4,6},{5,7},{6,4},{7,5},{8,10},{9,11},{10,... | collective-permute-start | bytes 589832 | tf_op jit(solution)/shard_map/A2b/ppermute | solution.py:217
  33.2 10.7 %collective-permute-start.9 = (bf16[96,1024]{1,0:T(8,128)(2,1)S(1)}, bf16[96,1024]{1,0:T(8,128)(2,1)S(1)}, u32[]{:S(2)}, u32[]{:S(2)}) collective-permute-start(bf16[96,1024]{1,0:T(8,128)(2,1)S(1)} %slice.26), channel_id=1, source_target_pairs={{0,4},{1,5},{2,6},{3,7},{4,0},{5,1},{6,2},{7,3},{8,12},{9,13},{10,... | collective-permute-start | bytes 589832 | tf_op jit(solution)/shard_map/A2a/ppermute | solution.py:217
  35.3 11.5 %collective-permute-start.13 = (bf16[48,2048]{1,0:T(8,128)(2,1)S(1)}, bf16[48,2048]{1,0:T(8,128)(2,1)S(1)}, u32[]{:S(2)}, u32[]{:S(2)}) collective-permute-start(bf16[48,2048]{1,0:T(8,128)(2,1)S(1)} %collective-permute-done.12.refs_0_), channel_id=1, source_target_pairs={{0,2},{1,3},{2,0},{3,1},{4,6},{5,7},{6,4},{7,5},{8,10},{9,11},{10,... | collective-permute-start | bytes 589832 | tf_op jit(solution)/shard_map/B1x/ppermute | solution.py:217
  36.8 10.0 %collective-permute-start.14 = (bf16[48,2048]{1,0:T(8,128)(2,1)S(1)}, bf16[48,2048]{1,0:T(8,128)(2,1)S(1)}, u32[]{:S(2)}, u32[]{:S(2)}) collective-permute-start(bf16[48,2048]{1,0:T(8,128)(2,1)S(1)} %collective-permute-done.12.refs_0_), channel_id=1, source_target_pairs={{0,4},{1,5},{2,6},{3,7},{4,0},{5,1},{6,2},{7,3},{8,12},{9,13},{10,... | collective-permute-start | bytes 589832 | tf_op jit(solution)/shard_map/B1y/ppermute | solution.py:217
  42.4 7.2 %collective-permute-start.15 = (bf16[48,2048]{1,0:T(8,128)(2,1)S(1)}, bf16[48,2048]{1,0:T(8,128)(2,1)S(1)}, u32[]{:S(2)}, u32[]{:S(2)}) collective-permute-start(bf16[48,2048]{1,0:T(8,128)(2,1)S(1)} %collective-permute-done.12.refs_0_), channel_id=1, source_target_pairs={{0,6},{1,7},{2,4},{3,5},{4,2},{5,3},{6,0},{7,1},{8,14},{9,15},{10,... | collective-permute-start | bytes 589832 | tf_op jit(solution)/shard_map/bd/ppermute | solution.py:217
  46.8 6.4 %collective-permute-start.16 = (bf16[96,1024]{1,0:T(8,128)(2,1)S(1)}, bf16[96,1024]{1,0:T(8,128)(2,1)S(1)}, u32[]{:S(2)}, u32[]{:S(2)}) collective-permute-start(bf16[96,1024]{1,0:T(8,128)(2,1)S(1)} %get-tuple-element.151), channel_id=1, source_target_pairs={{0,4},{1,5},{2,6},{3,7},{4,0},{5,1},{6,2},{7,3},{8,12},{9,13},{10,... | collective-permute-start | bytes 589832 | tf_op jit(solution)/shard_map/AR1a/ppermute | solution.py:217
  46.9 6.3 %collective-permute-start.17 = (bf16[96,1024]{1,0:T(8,128)(2,1)S(1)}, bf16[96,1024]{1,0:T(8,128)(2,1)S(1)}, u32[]{:S(2)}, u32[]{:S(2)}) collective-permute-start(bf16[96,1024]{1,0:T(8,128)(2,1)S(1)} %get-tuple-element.152), channel_id=1, source_target_pairs={{0,2},{1,3},{2,0},{3,1},{4,6},{5,7},{6,4},{7,5},{8,10},{9,11},{10,... | collective-permute-start | bytes 589832 | tf_op jit(solution)/shard_map/AR1b/ppermute | solution.py:217
  53.2 12.7 %collective-permute-start.24 = (bf16[48,2048]{1,0:T(8,128)(2,1)S(1)}, bf16[48,2048]{1,0:T(8,128)(2,1)S(1)}, u32[]{:S(2)}, u32[]{:S(2)}) collective-permute-start(bf16[48,2048]{1,0:T(8,128)(2,1)S(1)} %get-tuple-element.161), channel_id=1, source_target_pairs={{0,2},{1,3},{2,0},{3,1},{4,6},{5,7},{6,4},{7,5},{8,10},{9,11},{10,... | collective-permute-start | bytes 589832 | tf_op jit(solution)/shard_map/BRx/ppermute | solution.py:217
  55.6 10.4 %collective-permute-start.25 = (bf16[48,2048]{1,0:T(8,128)(2,1)S(1)}, bf16[48,2048]{1,0:T(8,128)(2,1)S(1)}, u32[]{:S(2)}, u32[]{:S(2)}) collective-permute-start(bf16[48,2048]{1,0:T(8,128)(2,1)S(1)} %get-tuple-element.162), channel_id=1, source_target_pairs={{0,4},{1,5},{2,6},{3,7},{4,0},{5,1},{6,2},{7,3},{8,12},{9,13},{10,... | collective-permute-start | bytes 589832 | tf_op jit(solution)/shard_map/BRy/ppermute | solution.py:217
  58.5 9.1 %collective-permute-start.26 = (bf16[48,2048]{1,0:T(8,128)(2,1)S(1)}, bf16[48,2048]{1,0:T(8,128)(2,1)S(1)}, u32[]{:S(2)}, u32[]{:S(2)}) collective-permute-start(bf16[48,2048]{1,0:T(8,128)(2,1)S(1)} %get-tuple-element.163), channel_id=1, source_target_pairs={{0,6},{1,7},{2,4},{3,5},{4,2},{5,3},{6,0},{7,1},{8,14},{9,15},{10,... | collective-permute-start | bytes 589832 | tf_op jit(solution)/shard_map/BRd/ppermute | solution.py:217
  58.6 13.1 %collective-permute-start.19 = (bf16[96,2048]{1,0:T(8,128)(2,1)S(1)}, bf16[96,2048]{1,0:T(8,128)(2,1)S(1)}, u32[]{:S(2)}, u32[]{:S(2)}) collective-permute-start(bf16[96,2048]{1,0:T(8,128)(2,1)S(1)} %pad_maximum_fusion.1), channel_id=1, source_target_pairs={{0,4},{1,5},{2,6},{3,7},{4,0},{5,1},{6,2},{7,3},{8,12},{9,13},{10,... | collective-permute-start | bytes 1179656 | tf_op jit(solution)/shard_map/AR2y/ppermute | solution.py:217
  60.2 11.5 %collective-permute-start.18 = (bf16[96,2048]{1,0:T(8,128)(2,1)S(1)}, bf16[96,2048]{1,0:T(8,128)(2,1)S(1)}, u32[]{:S(2)}, u32[]{:S(2)}) collective-permute-start(bf16[96,2048]{1,0:T(8,128)(2,1)S(1)} %pad_maximum_fusion), channel_id=1, source_target_pairs={{0,2},{1,3},{2,0},{3,1},{4,6},{5,7},{6,4},{7,5},{8,10},{9,11},{10,... | collective-permute-start | bytes 1179656 | tf_op jit(solution)/shard_map/AR2x/ppermute | solution.py:217
  67.7 13.6 %collective-permute-start.27 = (bf16[48,2048]{1,0:T(8,128)(2,1)S(1)}, bf16[48,2048]{1,0:T(8,128)(2,1)S(1)}, u32[]{:S(2)}, u32[]{:S(2)}) collective-permute-start(bf16[48,2048]{1,0:T(8,128)(2,1)S(1)} %add_convert_fusion.1), channel_id=1, source_target_pairs={{0,16},{1,17},{2,18},{3,19},{4,20},{5,21},{6,22},{7,23},{8,24},{9,... | collective-permute-start | bytes 589832 | tf_op jit(solution)/shard_map/c2/ppermute | solution.py:220
  71.7 6.5 %collective-permute-start.20 = (bf16[48,2048]{1,0:T(8,128)(2,1)S(1)}, bf16[48,2048]{1,0:T(8,128)(2,1)S(1)}, u32[]{:S(2)}, u32[]{:S(2)}) collective-permute-start(bf16[48,2048]{1,0:T(8,128)(2,1)S(1)} %get-tuple-element.173), channel_id=1, source_target_pairs={{0,2},{1,3},{2,0},{3,1},{4,6},{5,7},{6,4},{7,5},{8,10},{9,11},{10,... | collective-permute-start | bytes 589832 | tf_op jit(solution)/shard_map/ORx/ppermute | solution.py:217
  73.1 8.1 %collective-permute-start.21 = (bf16[48,2048]{1,0:T(8,128)(2,1)S(1)}, bf16[48,2048]{1,0:T(8,128)(2,1)S(1)}, u32[]{:S(2)}, u32[]{:S(2)}) collective-permute-start(bf16[48,2048]{1,0:T(8,128)(2,1)S(1)} %get-tuple-element.174), channel_id=1, source_target_pairs={{0,4},{1,5},{2,6},{3,7},{4,0},{5,1},{6,2},{7,3},{8,12},{9,13},{10,... | collective-permute-start | bytes 589832 | tf_op jit(solution)/shard_map/ORy/ppermute | solution.py:217
  74.4 6.8 %collective-permute-start.22 = (bf16[48,2048]{1,0:T(8,128)(2,1)S(1)}, bf16[48,2048]{1,0:T(8,128)(2,1)S(1)}, u32[]{:S(2)}, u32[]{:S(2)}) collective-permute-start(bf16[48,2048]{1,0:T(8,128)(2,1)S(1)} %get-tuple-element.175), channel_id=1, source_target_pairs={{0,6},{1,7},{2,4},{3,5},{4,2},{5,3},{6,0},{7,1},{8,14},{9,15},{10,... | collective-permute-start | bytes 589832 | tf_op jit(solution)/shard_map/ORd/ppermute | solution.py:217
  75.3 7.0 %collective-permute-start.23 = (bf16[48,2048]{1,0:T(8,128)(2,1)S(1)}, bf16[48,2048]{1,0:T(8,128)(2,1)S(1)}, u32[]{:S(2)}, u32[]{:S(2)}) collective-permute-start(bf16[48,2048]{1,0:T(8,128)(2,1)S(1)} %get-tuple-element.184), channel_id=1, source_target_pairs={{0,24},{1,25},{2,26},{3,27},{4,28},{5,29},{6,30},{7,31},{8,0},{9,1... | collective-permute-start | bytes 589832 | tf_op jit(solution)/shard_map/c1/ppermute | solution.py:220
  78.2 7.5 %collective-permute-start.28 = (bf16[48,2048]{1,0:T(8,128)(2,1)S(1)}, bf16[48,2048]{1,0:T(8,128)(2,1)S(1)}, u32[]{:S(2)}, u32[]{:S(2)}) collective-permute-start(bf16[48,2048]{1,0:T(8,128)(2,1)S(1)} %get-tuple-element.183), channel_id=1, source_target_pairs={{0,8},{1,9},{2,10},{3,11},{4,12},{5,13},{6,14},{7,15},{8,16},{9,17... | collective-permute-start | bytes 589832 | tf_op jit(solution)/shard_map/c3/ppermute | solution.py:220

commit v6 on v5

--- a/solution.py
+++ b/solution.py
@@ -266,9 +266,9 @@
     put("A1y", across, near_rows, 4)
     put("z2", lambda: [along(block, d) for block, d in zip(sent["blocks"], far)])
     put("b", across, sent["bias"], 1)
-    put("K2", stage, sent["w1"], sent["w2"])
+    put("K2", stage, sent["w1"])
     join("A1x", "A1y", "K2", "b")
-    peer_in, peer_out = sent["K2"]
+    (peer_in,), peer_out = sent["K2"], sent["w2"]
     weights = (mine_in, peer_in, b_in, sent["b"], mine_out, peer_out)
     far_rows = jnp.concatenate(sent["z2"]) if len(far) > 1 else sent["z2"][0]
     put("A2a", across, sent["A1x"][:, :half], 4)

time: 87 us -> 87 us (level)
  waiting for transfers between devices: 18.7 us -> 20 us
  Pallas kernels: 26.4 us -> 25.2 us
    ppermute x23, waiting for transfers between devices: 13.5 us -> 14.9 us  [across(): return lax.ppermute(value, 'local', [(i, i ^ bit) for i in range(devices)])]
    pallas_call x2, Pallas kernels: 7.1 us -> 5.81 us  [stage(): pl.pallas_call(stage_kernel, out_shape=[pltpu.VMEM(array.shape, array.dty...]
  transfers between devices with their start and end apart: 29 -> 29, of which waited for: 10 -> 12; matrix products, arithmetic and copies ran while one was open for 1% -> 1% of each run, Pallas kernels for 29% -> 28%
where the time goes in v6:
time: 87 us; the launch traced here: 86.8 us
  starting transfers between devices  40.8 us (47%)
  Pallas kernels  25.2 us (29%)
  waiting for transfers between devices  20 us (23%)
    ppermute x23, starting transfers between devices, across(): return lax.ppermute(value, 'local', [(i, i ^ bit) for i in range(devices)])  29.9 us
    pallas_call x4, Pallas kernels, expert_rows(): pl.pallas_call(functools.partial(expert_kernel, 512), out_shape=[pltpu.VM...  15.1 us
    ppermute x23, waiting for transfers between devices, across(): return lax.ppermute(value, 'local', [(i, i ^ bit) for i in range(devices)])  14.9 us
    ppermute x6, starting transfers between devices, along(): lax.ppermute(value, 'local', [(i, (i + planes * shared) % devices) for i...  10.9 us
    pallas_call x2, Pallas kernels, stage(): pl.pallas_call(stage_kernel, out_shape=[pltpu.VMEM(array.shape, array.dty...  5.81 us
    ppermute x6, waiting for transfers between devices, along(): lax.ppermute(value, 'local', [(i, (i + planes * shared) % devices) for i...  5.11 us
  transfers between devices with their start and end apart: 29, of which 12 were waited for; matrix products, arithmetic and copies ran while one was open for 1% of the time, Pallas kernels for 28%

profile of v6, /device:TPU:0, one launch (start us, length us, event | category | flops | bytes accessed | tf_op | source)
XLA Modules:
  0.0 86.8 jit_solution(13000015469060953219)
XLA Ops:
  0.5 1.6 %dispatch.1 = (bf16[48,2048]{1,0:T(8,128)(2,1)S(1)}, bf16[48,2048]{1,0:T(8,128)(2,1)S(1)}, bf16[48,2048]{1,0:T(8,128)(2,1)S(1)}, bf16[48,2048]{1,0:T(8,128)(2,1)S(1)}) custom-call(s32[1]{0:T(128)} %bitcast.2.plane_ref, s32[2,64]{1,0:T(2,128)} %bitcast.13, bf16[64,2048]{1,0:T(8,128)(2,1)} %tokens_ref.3, f32[1,2048]{1,0:T(1,128)} %bitcast.11, f32[1,2048]{1,0:T(1,128)} %bitcast.12), custom_call_target="tpu_custom_call" | custom-call | tf_op jit(solution)/shard_map/dispatch/pallas_call | solution.py:48
  2.0 2.6 %collective-permute-start = (bf16[48,2048]{1,0:T(8,128)(2,1)S(1)}, bf16[48,2048]{1,0:T(8,128)(2,1)S(1)}, u32[]{:S(2)}, u32[]{:S(2)}) collective-permute-start(bf16[48,2048]{1,0:T(8,128)(2,1)S(1)} %get-tuple-element.101), channel_id=1, source_target_pairs={{0,8},{1,9},{2,10},{3,11},{4,12},{5,13},{6,14},{7,15},{8,16},{9,17... | collective-permute-start | bytes 589832 | tf_op jit(solution)/shard_map/z1/ppermute | solution.py:220
  4.6 2.1 %collective-permute-start.1 = (bf16[48,2048]{1,0:T(8,128)(2,1)S(1)}, bf16[48,2048]{1,0:T(8,128)(2,1)S(1)}, u32[]{:S(2)}, u32[]{:S(2)}) collective-permute-start(bf16[48,2048]{1,0:T(8,128)(2,1)S(1)} %get-tuple-element.102), channel_id=1, source_target_pairs={{0,24},{1,25},{2,26},{3,27},{4,28},{5,29},{6,30},{7,31},{8,0},{9,1... | collective-permute-start | bytes 589832 | tf_op jit(solution)/shard_map/z3/ppermute | solution.py:220
  6.7 1.6 %collective-permute-start.2 = (bf16[48,2048]{1,0:T(8,128)(2,1)S(1)}, bf16[48,2048]{1,0:T(8,128)(2,1)S(1)}, u32[]{:S(2)}, u32[]{:S(2)}) collective-permute-start(bf16[48,2048]{1,0:T(8,128)(2,1)S(1)} %get-tuple-element.158.refs_0_), channel_id=1, source_target_pairs={{0,2},{1,3},{2,0},{3,1},{4,6},{5,7},{6,4},{7,5},{8,10},{9,11},{10,... | collective-permute-start | bytes 589832 | tf_op jit(solution)/shard_map/ox/ppermute | solution.py:217
  8.4 1.5 %collective-permute-start.3 = (bf16[48,2048]{1,0:T(8,128)(2,1)S(1)}, bf16[48,2048]{1,0:T(8,128)(2,1)S(1)}, u32[]{:S(2)}, u32[]{:S(2)}) collective-permute-start(bf16[48,2048]{1,0:T(8,128)(2,1)S(1)} %get-tuple-element.158.refs_0_), channel_id=1, source_target_pairs={{0,4},{1,5},{2,6},{3,7},{4,0},{5,1},{6,2},{7,3},{8,12},{9,13},{10,... | collective-permute-start | bytes 589832 | tf_op jit(solution)/shard_map/oy/ppermute | solution.py:217
  9.9 3.6 %stage.2 = (bf16[2048,1024]{1,0:T(8,128)(2,1)S(1)}, bf16[1024,2048]{1,0:T(8,128)(2,1)S(1)}) custom-call(bf16[2048,1024]{1,0:T(8,128)(2,1)} %bitcast.8, bf16[1024,2048]{1,0:T(8,128)(2,1)} %bitcast.9), custom_call_target="tpu_custom_call" | custom-call | tf_op jit(solution)/shard_map/K/stage/pallas_call | solution.py:139
  13.5 1.6 %routing.1 = (f32[64,2048]{1,0:T(8,128)S(1)}, f32[64,8]{1,0:T(8,128)S(1)}, bf16[64,48]{1,0:T(8,128)(2,1)S(1)}, bf16[64,48]{1,0:T(8,128)(2,1)S(1)}, bf16[64,48]{1...) custom-call(s32[1]{0:T(128)} %bitcast.2.plane_ref, s32[2,64]{1,0:T(2,128)} %bitcast.14, f32[2,64]{1,0:T(2,128)} %bitcast.15, ...), custom_call_target="tpu_custom_call" | custom-call | tf_op jit(solution)/shard_map/P/routing/pallas_call | solution.py:96
  16.0 1.6 %collective-permute-start.5 = (bf16[96,2048]{1,0:T(8,128)(2,1)S(1)}, bf16[96,2048]{1,0:T(8,128)(2,1)S(1)}, u32[]{:S(2)}, u32[]{:S(2)}) collective-permute-start(bf16[96,2048]{1,0:T(8,128)(2,1)S(1)} %constant_dynamic-update-slice_fusion.refs_0_), channel_id=1, source_target_pairs={{0,2},{1,3},{2,0},{3,1},{4,6},{5,7},{6,4},{7,5},{8,10},{9,11},{10,... | collective-permute-start | bytes 1179656 | tf_op jit(solution)/shard_map/A1x/ppermute | solution.py:217
  17.6 1.5 %collective-permute-start.6 = (bf16[96,2048]{1,0:T(8,128)(2,1)S(1)}, bf16[96,2048]{1,0:T(8,128)(2,1)S(1)}, u32[]{:S(2)}, u32[]{:S(2)}) collective-permute-start(bf16[96,2048]{1,0:T(8,128)(2,1)S(1)} %constant_dynamic-update-slice_fusion.refs_0_), channel_id=1, source_target_pairs={{0,4},{1,5},{2,6},{3,7},{4,0},{5,1},{6,2},{7,3},{8,12},{9,13},{10,... | collective-permute-start | bytes 1179656 | tf_op jit(solution)/shard_map/A1y/ppermute | solution.py:217
  20.4 2.2 %stage.3.refs_4_.refs_3_.refs_5_ = bf16[2048,1024]{1,0:T(8,128)(2,1)S(1)} custom-call(bf16[2048,1024]{1,0:T(8,128)(2,1)} %collective-permute-done.4.refs_0_), custom_call_target="tpu_custom_call" | custom-call | tf_op jit(solution)/shard_map/K2/stage/pallas_call | solution.py:139
  23.1 2.4 %collective-permute-start.11 = (bf16[48,2048]{1,0:T(8,128)(2,1)S(1)}, bf16[48,2048]{1,0:T(8,128)(2,1)S(1)}, u32[]{:S(2)}, u32[]{:S(2)}) collective-permute-start(bf16[48,2048]{1,0:T(8,128)(2,1)S(1)} %get-tuple-element.158.refs_0_), channel_id=1, source_target_pairs={{0,6},{1,7},{2,4},{3,5},{4,2},{5,3},{6,0},{7,1},{8,14},{9,15},{10,... | collective-permute-start | bytes 589832 | tf_op jit(solution)/shard_map/od/ppermute | solution.py:217
  25.6 2.4 %collective-permute-done.5.refs_1_ = bf16[96,2048]{1,0:T(8,128)(2,1)S(1)} collective-permute-done((bf16[96,2048]{1,0:T(8,128)(2,1)S(1)}, bf16[96,2048]{1,0:T(8,128)(2,1)S(1)}, u32[]{:S(2)}, u32[]{:S(2)}) %collective-permute-start.5) | collective-permute-done | bytes 393248 | tf_op jit(solution)/shard_map/A1x/ppermute | solution.py:217
  28.0 5.0 %collective-permute-done.6.refs_2_ = bf16[96,2048]{1,0:T(8,128)(2,1)S(1)} collective-permute-done((bf16[96,2048]{1,0:T(8,128)(2,1)S(1)}, bf16[96,2048]{1,0:T(8,128)(2,1)S(1)}, u32[]{:S(2)}, u32[]{:S(2)}) %collective-permute-start.6) | collective-permute-done | bytes 393248 | tf_op jit(solution)/shard_map/A1y/ppermute | solution.py:217
  33.2 2.1 %collective-permute-start.9 = (bf16[96,1024]{1,0:T(8,128)(2,1)S(1)}, bf16[96,1024]{1,0:T(8,128)(2,1)S(1)}, u32[]{:S(2)}, u32[]{:S(2)}) collective-permute-start(bf16[96,1024]{1,0:T(8,128)(2,1)S(1)} %slice.26), channel_id=1, source_target_pairs={{0,4},{1,5},{2,6},{3,7},{4,0},{5,1},{6,2},{7,3},{8,12},{9,13},{10,... | collective-permute-start | bytes 589832 | tf_op jit(solution)/shard_map/A2a/ppermute | solution.py:217
  35.3 1.5 %collective-permute-start.13 = (bf16[48,2048]{1,0:T(8,128)(2,1)S(1)}, bf16[48,2048]{1,0:T(8,128)(2,1)S(1)}, u32[]{:S(2)}, u32[]{:S(2)}) collective-permute-start(bf16[48,2048]{1,0:T(8,128)(2,1)S(1)} %collective-permute-done.12.refs_0_), channel_id=1, source_target_pairs={{0,2},{1,3},{2,0},{3,1},{4,6},{5,7},{6,4},{7,5},{8,10},{9,11},{10,... | collective-permute-start | bytes 589832 | tf_op jit(solution)/shard_map/B1x/ppermute | solution.py:217
  37.3 5.1 %expert.4 = (f32[96,2048]{1,0:T(8,128)S(1)}, f32[96,2048]{1,0:T(8,128)S(1)}, f32[96,2048]{1,0:T(8,128)S(1)}) custom-call(bf16[96,2048]{1,0:T(8,128)(2,1)S(1)} %constant_dynamic-update-slice_fusion.refs_0_, bf16[96,2048]{1,0:T(8,128)(2,1)S(1)} %collective-permute-done.5.refs_1_, bf16[96,2048]{1,0:T(8,128)(2,1)S(1)} %collective-permute-done.6.refs_2_, ...), custom_call_target="tpu_custom_call" | custom-call | tf_op jit(solution)/shard_map/EA1/expert/pallas_call | solution.py:192
  42.4 1.6 %collective-permute-start.15 = (bf16[48,2048]{1,0:T(8,128)(2,1)S(1)}, bf16[48,2048]{1,0:T(8,128)(2,1)S(1)}, u32[]{:S(2)}, u32[]{:S(2)}) collective-permute-start(bf16[48,2048]{1,0:T(8,128)(2,1)S(1)} %collective-permute-done.12.refs_0_), channel_id=1, source_target_pairs={{0,6},{1,7},{2,4},{3,5},{4,2},{5,3},{6,0},{7,1},{8,14},{9,15},{10,... | collective-permute-start | bytes 589832 | tf_op jit(solution)/shard_map/bd/ppermute | solution.py:217
  43.9 2.8 %expert.5 = (bf16[96,1024]{1,0:T(8,128)(2,1)S(1)}, bf16[96,1024]{1,0:T(8,128)(2,1)S(1)}) custom-call(bf16[96,1024]{1,0:T(8,128)(2,1)S(1)} %collective-permute-done.9.refs_0_, bf16[96,1024]{1,0:T(8,128)(2,1)S(1)} %collective-permute-done.10.refs_1_, bf16[2048,1024]{1,0:T(8,128)(2,1)S(1)} %get-tuple-element.125.refs_3_.refs_2_.refs_4_, ...), custom_call_target="tpu_custom_call" | custom-call | tf_op jit(solution)/shard_map/EA2/expert/pallas_call | solution.py:192
  46.9 2.6 %collective-permute-start.17 = (bf16[96,1024]{1,0:T(8,128)(2,1)S(1)}, bf16[96,1024]{1,0:T(8,128)(2,1)S(1)}, u32[]{:S(2)}, u32[]{:S(2)}) collective-permute-start(bf16[96,1024]{1,0:T(8,128)(2,1)S(1)} %get-tuple-element.146), channel_id=1, source_target_pairs={{0,2},{1,3},{2,0},{3,1},{4,6},{5,7},{6,4},{7,5},{8,10},{9,11},{10,... | collective-permute-start | bytes 589832 | tf_op jit(solution)/shard_map/AR1b/ppermute | solution.py:217
  49.6 3.5 %expert.6 = (f32[48,2048]{1,0:T(8,128)S(1)}, bf16[48,2048]{1,0:T(8,128)(2,1)S(1)}, bf16[48,2048]{1,0:T(8,128)(2,1)S(1)}, bf16[48,2048]{1,0:T(8,128)(2,1)S(1)}) custom-call(bf16[48,2048]{1,0:T(8,128)(2,1)S(1)} %collective-permute-done.12.refs_0_, bf16[48,2048]{1,0:T(8,128)(2,1)S(1)} %collective-permute-done.13.refs_1_, ...), custom_call_target="tpu_custom_call" | custom-call | tf_op jit(solution)/shard_map/EB/expert/pallas_call | solution.py:192
  53.3 2.3 %collective-permute-start.24 = (bf16[48,2048]{1,0:T(8,128)(2,1)S(1)}, bf16[48,2048]{1,0:T(8,128)(2,1)S(1)}, u32[]{:S(2)}, u32[]{:S(2)}) collective-permute-start(bf16[48,2048]{1,0:T(8,128)(2,1)S(1)} %get-tuple-element.155), channel_id=1, source_target_pairs={{0,2},{1,3},{2,0},{3,1},{4,6},{5,7},{6,4},{7,5},{8,10},{9,11},{10,... | collective-permute-start | bytes 589832 | tf_op jit(solution)/shard_map/BRx/ppermute | solution.py:217
  55.6 2.8 %collective-permute-start.25 = (bf16[48,2048]{1,0:T(8,128)(2,1)S(1)}, bf16[48,2048]{1,0:T(8,128)(2,1)S(1)}, u32[]{:S(2)}, u32[]{:S(2)}) collective-permute-start(bf16[48,2048]{1,0:T(8,128)(2,1)S(1)} %get-tuple-element.156), channel_id=1, source_target_pairs={{0,4},{1,5},{2,6},{3,7},{4,0},{5,1},{6,2},{7,3},{8,12},{9,13},{10,... | collective-permute-start | bytes 589832 | tf_op jit(solution)/shard_map/BRy/ppermute | solution.py:217
  58.5 1.5 %collective-permute-start.19 = (bf16[96,2048]{1,0:T(8,128)(2,1)S(1)}, bf16[96,2048]{1,0:T(8,128)(2,1)S(1)}, u32[]{:S(2)}, u32[]{:S(2)}) collective-permute-start(bf16[96,2048]{1,0:T(8,128)(2,1)S(1)} %pad_maximum_fusion.1), channel_id=1, source_target_pairs={{0,4},{1,5},{2,6},{3,7},{4,0},{5,1},{6,2},{7,3},{8,12},{9,13},{10,... | collective-permute-start | bytes 1179656 | tf_op jit(solution)/shard_map/AR2y/ppermute | solution.py:217
  60.1 2.1 %collective-permute-start.18 = (bf16[96,2048]{1,0:T(8,128)(2,1)S(1)}, bf16[96,2048]{1,0:T(8,128)(2,1)S(1)}, u32[]{:S(2)}, u32[]{:S(2)}) collective-permute-start(bf16[96,2048]{1,0:T(8,128)(2,1)S(1)} %pad_maximum_fusion), channel_id=1, source_target_pairs={{0,2},{1,3},{2,0},{3,1},{4,6},{5,7},{6,4},{7,5},{8,10},{9,11},{10,... | collective-permute-start | bytes 1179656 | tf_op jit(solution)/shard_map/AR2x/ppermute | solution.py:217
  62.2 3.7 %expert.7 = (f32[48,2048]{1,0:T(8,128)S(1)}, bf16[48,2048]{1,0:T(8,128)(2,1)S(1)}, bf16[48,2048]{1,0:T(8,128)(2,1)S(1)}, bf16[48,2048]{1,0:T(8,128)(2,1)S(1)}) custom-call(bf16[48,2048]{1,0:T(8,128)(2,1)S(1)} %get-tuple-element.158.refs_0_, bf16[48,2048]{1,0:T(8,128)(2,1)S(1)} %collective-permute-done.2.refs_1_, ...), custom_call_target="tpu_custom_call" | custom-call | tf_op jit(solution)/shard_map/EO/expert/pallas_call | solution.py:192
  65.9 1.7 %collective-permute-done.26 = bf16[48,2048]{1,0:T(8,128)(2,1)S(1)} collective-permute-done((bf16[48,2048]{1,0:T(8,128)(2,1)S(1)}, bf16[48,2048]{1,0:T(8,128)(2,1)S(1)}, u32[]{:S(2)}, u32[]{:S(2)}) %collective-permute-start.26) | collective-permute-done | bytes 196640 | tf_op jit(solution)/shard_map/BRd/ppermute | solution.py:217
  67.7 1.4 %collective-permute-start.27 = (bf16[48,2048]{1,0:T(8,128)(2,1)S(1)}, bf16[48,2048]{1,0:T(8,128)(2,1)S(1)}, u32[]{:S(2)}, u32[]{:S(2)}) collective-permute-start(bf16[48,2048]{1,0:T(8,128)(2,1)S(1)} %add_convert_fusion.1), channel_id=1, source_target_pairs={{0,16},{1,17},{2,18},{3,19},{4,20},{5,21},{6,22},{7,23},{8,24},{9,... | collective-permute-start | bytes 589832 | tf_op jit(solution)/shard_map/c2/ppermute | solution.py:220
  69.1 2.6 %collective-permute-done.19 = bf16[96,2048]{1,0:T(8,128)(2,1)S(1)} collective-permute-done((bf16[96,2048]{1,0:T(8,128)(2,1)S(1)}, bf16[96,2048]{1,0:T(8,128)(2,1)S(1)}, u32[]{:S(2)}, u32[]{:S(2)}) %collective-permute-start.19) | collective-permute-done | bytes 393248 | tf_op jit(solution)/shard_map/AR2y/ppermute | solution.py:217
  71.7 1.4 %collective-permute-start.20 = (bf16[48,2048]{1,0:T(8,128)(2,1)S(1)}, bf16[48,2048]{1,0:T(8,128)(2,1)S(1)}, u32[]{:S(2)}, u32[]{:S(2)}) collective-permute-start(bf16[48,2048]{1,0:T(8,128)(2,1)S(1)} %get-tuple-element.167), channel_id=1, source_target_pairs={{0,2},{1,3},{2,0},{3,1},{4,6},{5,7},{6,4},{7,5},{8,10},{9,11},{10,... | collective-permute-start | bytes 589832 | tf_op jit(solution)/shard_map/ORx/ppermute | solution.py:217
  75.3 2.4 %collective-permute-start.23 = (bf16[48,2048]{1,0:T(8,128)(2,1)S(1)}, bf16[48,2048]{1,0:T(8,128)(2,1)S(1)}, u32[]{:S(2)}, u32[]{:S(2)}) collective-permute-start(bf16[48,2048]{1,0:T(8,128)(2,1)S(1)} %get-tuple-element.178), channel_id=1, source_target_pairs={{0,24},{1,25},{2,26},{3,27},{4,28},{5,29},{6,30},{7,31},{8,0},{9,1... | collective-permute-start | bytes 589832 | tf_op jit(solution)/shard_map/c1/ppermute | solution.py:220
  79.3 1.8 %collective-permute-done.21 = bf16[48,2048]{1,0:T(8,128)(2,1)S(1)} collective-permute-done((bf16[48,2048]{1,0:T(8,128)(2,1)S(1)}, bf16[48,2048]{1,0:T(8,128)(2,1)S(1)}, u32[]{:S(2)}, u32[]{:S(2)}) %collective-permute-start.21) | collective-permute-done | bytes 196640 | tf_op jit(solution)/shard_map/ORy/ppermute | solution.py:217
  82.3 3.3 %collective-permute-done.28.refs_7_ = bf16[48,2048]{1,0:T(8,128)(2,1)S(1)} collective-permute-done((bf16[48,2048]{1,0:T(8,128)(2,1)S(1)}, bf16[48,2048]{1,0:T(8,128)(2,1)S(1)}, u32[]{:S(2)}, u32[]{:S(2)}) %collective-permute-start.28) | collective-permute-done | bytes 196640 | tf_op jit(solution)/shard_map/c3/ppermute | solution.py:220
  (53 shorter events, 10.6 us)
Async XLA Ops:
  0.0 15.9 %collective-permute-start.4 = (bf16[2048,1024]{1,0:T(8,128)(2,1)}, bf16[2048,1024]{1,0:T(8,128)(2,1)}, u32[]{:S(2)}, u32[]{:S(2)}) collective-permute-start(bf16[2048,1024]{1,0:T(8,128)(2,1)} %bitcast.7), channel_id=1, source_target_pairs={{0,1},{1,0},{2,3},{3,2},{4,5},{5,4},{6,7},{7,6},{8,9},{9,8},{10,11... | collective-permute-start | bytes 12582920 | tf_op jit(solution)/shard_map/w1/ppermute | solution.py:217
  2.0 13.1 %collective-permute-start = (bf16[48,2048]{1,0:T(8,128)(2,1)S(1)}, bf16[48,2048]{1,0:T(8,128)(2,1)S(1)}, u32[]{:S(2)}, u32[]{:S(2)}) collective-permute-start(bf16[48,2048]{1,0:T(8,128)(2,1)S(1)} %get-tuple-element.101), channel_id=1, source_target_pairs={{0,8},{1,9},{2,10},{3,11},{4,12},{5,13},{6,14},{7,15},{8,16},{9,17... | collective-permute-start | bytes 589832 | tf_op jit(solution)/shard_map/z1/ppermute | solution.py:220
  4.6 11.2 %collective-permute-start.1 = (bf16[48,2048]{1,0:T(8,128)(2,1)S(1)}, bf16[48,2048]{1,0:T(8,128)(2,1)S(1)}, u32[]{:S(2)}, u32[]{:S(2)}) collective-permute-start(bf16[48,2048]{1,0:T(8,128)(2,1)S(1)} %get-tuple-element.102), channel_id=1, source_target_pairs={{0,24},{1,25},{2,26},{3,27},{4,28},{5,29},{6,30},{7,31},{8,0},{9,1... | collective-permute-start | bytes 589832 | tf_op jit(solution)/shard_map/z3/ppermute | solution.py:220
  6.7 9.2 %collective-permute-start.2 = (bf16[48,2048]{1,0:T(8,128)(2,1)S(1)}, bf16[48,2048]{1,0:T(8,128)(2,1)S(1)}, u32[]{:S(2)}, u32[]{:S(2)}) collective-permute-start(bf16[48,2048]{1,0:T(8,128)(2,1)S(1)} %get-tuple-element.158.refs_0_), channel_id=1, source_target_pairs={{0,2},{1,3},{2,0},{3,1},{4,6},{5,7},{6,4},{7,5},{8,10},{9,11},{10,... | collective-permute-start | bytes 589832 | tf_op jit(solution)/shard_map/ox/ppermute | solution.py:217
  8.4 7.5 %collective-permute-start.3 = (bf16[48,2048]{1,0:T(8,128)(2,1)S(1)}, bf16[48,2048]{1,0:T(8,128)(2,1)S(1)}, u32[]{:S(2)}, u32[]{:S(2)}) collective-permute-start(bf16[48,2048]{1,0:T(8,128)(2,1)S(1)} %get-tuple-element.158.refs_0_), channel_id=1, source_target_pairs={{0,4},{1,5},{2,6},{3,7},{4,0},{5,1},{6,2},{7,3},{8,12},{9,13},{10,... | collective-permute-start | bytes 589832 | tf_op jit(solution)/shard_map/oy/ppermute | solution.py:217
  9.9 6.0 %copy-start.1 = (bf16[1,1024,2048]{2,1,0:T(8,128)(2,1)S(1)}, bf16[1,1024,2048]{2,1,0:T(8,128)(2,1)}, u32[]{:S(2)}) copy-start(bf16[1,1024,2048]{2,1,0:T(8,128)(2,1)} %param.16) | copy-start | bytes 12582916
  9.9 10.5 %copy-start = (f32[1,1024]{1,0:T(1,128)S(1)}, f32[1,1024]{1,0:T(1,128)}, u32[]{:S(2)}) copy-start(f32[1,1024]{1,0:T(1,128)} %refs_6_.3) | copy-start | bytes 12292
  15.9 20.8 %collective-permute-start.8 = (bf16[1024,2048]{1,0:T(8,128)(2,1)S(1)}, bf16[1024,2048]{1,0:T(8,128)(2,1)S(1)}, u32[]{:S(2)}, u32[]{:S(2)}) collective-permute-start(bf16[1024,2048]{1,0:T(8,128)(2,1)S(1)} %bitcast.10), channel_id=1, source_target_pairs={{0,1},{1,0},{2,3},{3,2},{4,5},{5,4},{6,7},{7,6},{8,9},{9,8},{10,11... | collective-permute-start | bytes 12582920 | tf_op jit(solution)/shard_map/w2/ppermute | solution.py:217
  16.0 12.0 %collective-permute-start.5 = (bf16[96,2048]{1,0:T(8,128)(2,1)S(1)}, bf16[96,2048]{1,0:T(8,128)(2,1)S(1)}, u32[]{:S(2)}, u32[]{:S(2)}) collective-permute-start(bf16[96,2048]{1,0:T(8,128)(2,1)S(1)} %constant_dynamic-update-slice_fusion.refs_0_), channel_id=1, source_target_pairs={{0,2},{1,3},{2,0},{3,1},{4,6},{5,7},{6,4},{7,5},{8,10},{9,11},{10,... | collective-permute-start | bytes 1179656 | tf_op jit(solution)/shard_map/A1x/ppermute | solution.py:217
  17.6 15.4 %collective-permute-start.6 = (bf16[96,2048]{1,0:T(8,128)(2,1)S(1)}, bf16[96,2048]{1,0:T(8,128)(2,1)S(1)}, u32[]{:S(2)}, u32[]{:S(2)}) collective-permute-start(bf16[96,2048]{1,0:T(8,128)(2,1)S(1)} %constant_dynamic-update-slice_fusion.refs_0_), channel_id=1, source_target_pairs={{0,4},{1,5},{2,6},{3,7},{4,0},{5,1},{6,2},{7,3},{8,12},{9,13},{10,... | collective-permute-start | bytes 1179656 | tf_op jit(solution)/shard_map/A1y/ppermute | solution.py:217
  19.1 16.1 %collective-permute-start.12 = (bf16[48,2048]{1,0:T(8,128)(2,1)S(1)}, bf16[48,2048]{1,0:T(8,128)(2,1)S(1)}, u32[]{:S(2)}, u32[]{:S(2)}) collective-permute-start(bf16[48,2048]{1,0:T(8,128)(2,1)S(1)} %get-tuple-element.134), channel_id=1, source_target_pairs={{0,16},{1,17},{2,18},{3,19},{4,20},{5,21},{6,22},{7,23},{8,24},{9,... | collective-permute-start | bytes 589832 | tf_op jit(solution)/shard_map/z2/ppermute | solution.py:220
  20.4 2.7 %collective-permute-start.7 = (f32[1,1024]{1,0:T(1,128)S(1)}, f32[1,1024]{1,0:T(1,128)S(1)}, u32[]{:S(2)}, u32[]{:S(2)}) collective-permute-start(f32[1,1024]{1,0:T(1,128)S(1)} %copy-done), channel_id=1, source_target_pairs={{0,1},{1,0},{2,3},{3,2},{4,5},{5,4},{6,7},{7,6},{8,9},{9,8},{10,11... | collective-permute-start | bytes 12296 | tf_op jit(solution)/shard_map/b/ppermute | solution.py:217
  23.1 19.2 %collective-permute-start.11 = (bf16[48,2048]{1,0:T(8,128)(2,1)S(1)}, bf16[48,2048]{1,0:T(8,128)(2,1)S(1)}, u32[]{:S(2)}, u32[]{:S(2)}) collective-permute-start(bf16[48,2048]{1,0:T(8,128)(2,1)S(1)} %get-tuple-element.158.refs_0_), channel_id=1, source_target_pairs={{0,6},{1,7},{2,4},{3,5},{4,2},{5,3},{6,0},{7,1},{8,14},{9,15},{10,... | collective-permute-start | bytes 589832 | tf_op jit(solution)/shard_map/od/ppermute | solution.py:217
  33.1 10.9 %collective-permute-start.10 = (bf16[96,1024]{1,0:T(8,128)(2,1)S(1)}, bf16[96,1024]{1,0:T(8,128)(2,1)S(1)}, u32[]{:S(2)}, u32[]{:S(2)}) collective-permute-start(bf16[96,1024]{1,0:T(8,128)(2,1)S(1)} %slice.27), channel_id=1, source_target_pairs={{0,2},{1,3},{2,0},{3,1},{4,6},{5,7},{6,4},{7,5},{8,10},{9,11},{10,... | collective-permute-start | bytes 589832 | tf_op jit(solution)/shard_map/A2b/ppermute | solution.py:217
  33.2 10.8 %collective-permute-start.9 = (bf16[96,1024]{1,0:T(8,128)(2,1)S(1)}, bf16[96,1024]{1,0:T(8,128)(2,1)S(1)}, u32[]{:S(2)}, u32[]{:S(2)}) collective-permute-start(bf16[96,1024]{1,0:T(8,128)(2,1)S(1)} %slice.26), channel_id=1, source_target_pairs={{0,4},{1,5},{2,6},{3,7},{4,0},{5,1},{6,2},{7,3},{8,12},{9,13},{10,... | collective-permute-start | bytes 589832 | tf_op jit(solution)/shard_map/A2a/ppermute | solution.py:217
  35.3 11.5 %collective-permute-start.13 = (bf16[48,2048]{1,0:T(8,128)(2,1)S(1)}, bf16[48,2048]{1,0:T(8,128)(2,1)S(1)}, u32[]{:S(2)}, u32[]{:S(2)}) collective-permute-start(bf16[48,2048]{1,0:T(8,128)(2,1)S(1)} %collective-permute-done.12.refs_0_), channel_id=1, source_target_pairs={{0,2},{1,3},{2,0},{3,1},{4,6},{5,7},{6,4},{7,5},{8,10},{9,11},{10,... | collective-permute-start | bytes 589832 | tf_op jit(solution)/shard_map/B1x/ppermute | solution.py:217
  36.8 10.0 %collective-permute-start.14 = (bf16[48,2048]{1,0:T(8,128)(2,1)S(1)}, bf16[48,2048]{1,0:T(8,128)(2,1)S(1)}, u32[]{:S(2)}, u32[]{:S(2)}) collective-permute-start(bf16[48,2048]{1,0:T(8,128)(2,1)S(1)} %collective-permute-done.12.refs_0_), channel_id=1, source_target_pairs={{0,4},{1,5},{2,6},{3,7},{4,0},{5,1},{6,2},{7,3},{8,12},{9,13},{10,... | collective-permute-start | bytes 589832 | tf_op jit(solution)/shard_map/B1y/ppermute | solution.py:217
  42.4 7.2 %collective-permute-start.15 = (bf16[48,2048]{1,0:T(8,128)(2,1)S(1)}, bf16[48,2048]{1,0:T(8,128)(2,1)S(1)}, u32[]{:S(2)}, u32[]{:S(2)}) collective-permute-start(bf16[48,2048]{1,0:T(8,128)(2,1)S(1)} %collective-permute-done.12.refs_0_), channel_id=1, source_target_pairs={{0,6},{1,7},{2,4},{3,5},{4,2},{5,3},{6,0},{7,1},{8,14},{9,15},{10,... | collective-permute-start | bytes 589832 | tf_op jit(solution)/shard_map/bd/ppermute | solution.py:217
  46.8 6.4 %collective-permute-start.16 = (bf16[96,1024]{1,0:T(8,128)(2,1)S(1)}, bf16[96,1024]{1,0:T(8,128)(2,1)S(1)}, u32[]{:S(2)}, u32[]{:S(2)}) collective-permute-start(bf16[96,1024]{1,0:T(8,128)(2,1)S(1)} %get-tuple-element.145), channel_id=1, source_target_pairs={{0,4},{1,5},{2,6},{3,7},{4,0},{5,1},{6,2},{7,3},{8,12},{9,13},{10,... | collective-permute-start | bytes 589832 | tf_op jit(solution)/shard_map/AR1a/ppermute | solution.py:217
  46.9 6.3 %collective-permute-start.17 = (bf16[96,1024]{1,0:T(8,128)(2,1)S(1)}, bf16[96,1024]{1,0:T(8,128)(2,1)S(1)}, u32[]{:S(2)}, u32[]{:S(2)}) collective-permute-start(bf16[96,1024]{1,0:T(8,128)(2,1)S(1)} %get-tuple-element.146), channel_id=1, source_target_pairs={{0,2},{1,3},{2,0},{3,1},{4,6},{5,7},{6,4},{7,5},{8,10},{9,11},{10,... | collective-permute-start | bytes 589832 | tf_op jit(solution)/shard_map/AR1b/ppermute | solution.py:217
  53.3 12.6 %collective-permute-start.24 = (bf16[48,2048]{1,0:T(8,128)(2,1)S(1)}, bf16[48,2048]{1,0:T(8,128)(2,1)S(1)}, u32[]{:S(2)}, u32[]{:S(2)}) collective-permute-start(bf16[48,2048]{1,0:T(8,128)(2,1)S(1)} %get-tuple-element.155), channel_id=1, source_target_pairs={{0,2},{1,3},{2,0},{3,1},{4,6},{5,7},{6,4},{7,5},{8,10},{9,11},{10,... | collective-permute-start | bytes 589832 | tf_op jit(solution)/shard_map/BRx/ppermute | solution.py:217
  55.6 10.3 %collective-permute-start.25 = (bf16[48,2048]{1,0:T(8,128)(2,1)S(1)}, bf16[48,2048]{1,0:T(8,128)(2,1)S(1)}, u32[]{:S(2)}, u32[]{:S(2)}) collective-permute-start(bf16[48,2048]{1,0:T(8,128)(2,1)S(1)} %get-tuple-element.156), channel_id=1, source_target_pairs={{0,4},{1,5},{2,6},{3,7},{4,0},{5,1},{6,2},{7,3},{8,12},{9,13},{10,... | collective-permute-start | bytes 589832 | tf_op jit(solution)/shard_map/BRy/ppermute | solution.py:217
  58.4 9.2 %collective-permute-start.26 = (bf16[48,2048]{1,0:T(8,128)(2,1)S(1)}, bf16[48,2048]{1,0:T(8,128)(2,1)S(1)}, u32[]{:S(2)}, u32[]{:S(2)}) collective-permute-start(bf16[48,2048]{1,0:T(8,128)(2,1)S(1)} %get-tuple-element.157), channel_id=1, source_target_pairs={{0,6},{1,7},{2,4},{3,5},{4,2},{5,3},{6,0},{7,1},{8,14},{9,15},{10,... | collective-permute-start | bytes 589832 | tf_op jit(solution)/shard_map/BRd/ppermute | solution.py:217
  58.5 13.2 %collective-permute-start.19 = (bf16[96,2048]{1,0:T(8,128)(2,1)S(1)}, bf16[96,2048]{1,0:T(8,128)(2,1)S(1)}, u32[]{:S(2)}, u32[]{:S(2)}) collective-permute-start(bf16[96,2048]{1,0:T(8,128)(2,1)S(1)} %pad_maximum_fusion.1), channel_id=1, source_target_pairs={{0,4},{1,5},{2,6},{3,7},{4,0},{5,1},{6,2},{7,3},{8,12},{9,13},{10,... | collective-permute-start | bytes 1179656 | tf_op jit(solution)/shard_map/AR2y/ppermute | solution.py:217
  60.1 11.6 %collective-permute-start.18 = (bf16[96,2048]{1,0:T(8,128)(2,1)S(1)}, bf16[96,2048]{1,0:T(8,128)(2,1)S(1)}, u32[]{:S(2)}, u32[]{:S(2)}) collective-permute-start(bf16[96,2048]{1,0:T(8,128)(2,1)S(1)} %pad_maximum_fusion), channel_id=1, source_target_pairs={{0,2},{1,3},{2,0},{3,1},{4,6},{5,7},{6,4},{7,5},{8,10},{9,11},{10,... | collective-permute-start | bytes 1179656 | tf_op jit(solution)/shard_map/AR2x/ppermute | solution.py:217
  67.7 13.6 %collective-permute-start.27 = (bf16[48,2048]{1,0:T(8,128)(2,1)S(1)}, bf16[48,2048]{1,0:T(8,128)(2,1)S(1)}, u32[]{:S(2)}, u32[]{:S(2)}) collective-permute-start(bf16[48,2048]{1,0:T(8,128)(2,1)S(1)} %add_convert_fusion.1), channel_id=1, source_target_pairs={{0,16},{1,17},{2,18},{3,19},{4,20},{5,21},{6,22},{7,23},{8,24},{9,... | collective-permute-start | bytes 589832 | tf_op jit(solution)/shard_map/c2/ppermute | solution.py:220
  71.7 6.5 %collective-permute-start.20 = (bf16[48,2048]{1,0:T(8,128)(2,1)S(1)}, bf16[48,2048]{1,0:T(8,128)(2,1)S(1)}, u32[]{:S(2)}, u32[]{:S(2)}) collective-permute-start(bf16[48,2048]{1,0:T(8,128)(2,1)S(1)} %get-tuple-element.167), channel_id=1, source_target_pairs={{0,2},{1,3},{2,0},{3,1},{4,6},{5,7},{6,4},{7,5},{8,10},{9,11},{10,... | collective-permute-start | bytes 589832 | tf_op jit(solution)/shard_map/ORx/ppermute | solution.py:217
  73.0 8.1 %collective-permute-start.21 = (bf16[48,2048]{1,0:T(8,128)(2,1)S(1)}, bf16[48,2048]{1,0:T(8,128)(2,1)S(1)}, u32[]{:S(2)}, u32[]{:S(2)}) collective-permute-start(bf16[48,2048]{1,0:T(8,128)(2,1)S(1)} %get-tuple-element.168), channel_id=1, source_target_pairs={{0,4},{1,5},{2,6},{3,7},{4,0},{5,1},{6,2},{7,3},{8,12},{9,13},{10,... | collective-permute-start | bytes 589832 | tf_op jit(solution)/shard_map/ORy/ppermute | solution.py:217
  74.2 7.0 %collective-permute-start.22 = (bf16[48,2048]{1,0:T(8,128)(2,1)S(1)}, bf16[48,2048]{1,0:T(8,128)(2,1)S(1)}, u32[]{:S(2)}, u32[]{:S(2)}) collective-permute-start(bf16[48,2048]{1,0:T(8,128)(2,1)S(1)} %get-tuple-element.169), channel_id=1, source_target_pairs={{0,6},{1,7},{2,4},{3,5},{4,2},{5,3},{6,0},{7,1},{8,14},{9,15},{10,... | collective-permute-start | bytes 589832 | tf_op jit(solution)/shard_map/ORd/ppermute | solution.py:217
  75.3 7.0 %collective-permute-start.23 = (bf16[48,2048]{1,0:T(8,128)(2,1)S(1)}, bf16[48,2048]{1,0:T(8,128)(2,1)S(1)}, u32[]{:S(2)}, u32[]{:S(2)}) collective-permute-start(bf16[48,2048]{1,0:T(8,128)(2,1)S(1)} %get-tuple-element.178), channel_id=1, source_target_pairs={{0,24},{1,25},{2,26},{3,27},{4,28},{5,29},{6,30},{7,31},{8,0},{9,1... | collective-permute-start | bytes 589832 | tf_op jit(solution)/shard_map/c1/ppermute | solution.py:220
  78.2 7.5 %collective-permute-start.28 = (bf16[48,2048]{1,0:T(8,128)(2,1)S(1)}, bf16[48,2048]{1,0:T(8,128)(2,1)S(1)}, u32[]{:S(2)}, u32[]{:S(2)}) collective-permute-start(bf16[48,2048]{1,0:T(8,128)(2,1)S(1)} %get-tuple-element.177), channel_id=1, source_target_pairs={{0,8},{1,9},{2,10},{3,11},{4,12},{5,13},{6,14},{7,15},{8,16},{9,17... | collective-permute-start | bytes 589832 | tf_op jit(solution)/shard_map/c3/ppermute | solution.py:220
